TPU v7x, 128 devices: a whole 4x4x4 slice. The times are simulated.
128 devices in a mesh: space: 16 (over y_lo, z, core), filt: 8 (over y_hi, x).
Axes of the slice: x: 4, y: 4 (y_hi: 2, y_lo: 2; y = y_hi * 2 + y_lo), z: 4, core: 2. Of those that a mesh axis runs over, the one named last changes fastest.
Arguments:
- inputs: bfloat16 [2, 64, 128, 128, 128], P(None, None, 'space', 'filt'), may hold values from -6 to 6
- kernel_one: bfloat16 [3, 3, 3, 64, 128], replicated, may hold values from -0.15625 to 0.15625
- kernel_two: bfloat16 [3, 3, 3, 128, 256], P(None, None, None, None, 'filt'), may hold values from -0.109375 to 0.109375
- cotangent: bfloat16 [2, 256, 32, 1024], P(None, 'filt', 'space'), may hold values from -0.023925781 to 0.023925781
Outputs:
- activation: bfloat16 [2, 256, 32, 1024], P(None, 'filt', 'space')
- grad_one: float32 [3, 3, 3, 64, 128], replicated
- grad_two: float32 [3, 3, 3, 128, 256], P(None, None, None, None, 'filt')
All inputs are finite; a program needn't handle non-finite values.
Results may differ from a plain program's by a relative error of at most 0.03.
The roundings to bfloat16 on the way count: a program that leaves them out, or rounds other values in their place, can miss the bound.
Values may be sent and summed in bfloat16 or wider, within the bound.
No kernel may reach another device: no remote copies, remote signals or barrier semaphores. Data moves between devices by JAX's collectives and lax.ppermute only.
A program may use at most 192 MiB of HBM per device.

v0:
```python
import jax
import jax.numpy as jnp
from jax import lax
from jax.sharding import PartitionSpec as P


def shifted(value, axis, by):
    devices = lax.axis_size(axis)
    pairs = [(i, i + by) for i in range(devices) if 0 <= i + by < devices]
    return lax.ppermute(value, axis, pairs)


def leaky(value):
    return jnp.where(value > 0, value, 0.3 * value)


def slope_of(value):
    return jnp.where(value > 0, 1.0, 0.3).astype(jnp.float32)


def forward_conv(field, kernel, pads):
    return lax.conv_general_dilated(
        field,
        kernel,
        (2, 2, 2),
        pads,
        dimension_numbers=("NCDHW", "DHWIO", "NCDHW"),
        preferred_element_type=jnp.float32,
    )


def kernel_grad(field, delta, pads):
    return lax.conv_general_dilated(
        field,
        delta,
        (1, 1, 1),
        pads,
        rhs_dilation=(2, 2, 2),
        dimension_numbers=("CNDHW", "IODHW", "DHWNC"),
        preferred_element_type=jnp.float32,
    )


def input_grad(delta, kernel, pads):
    flipped = kernel[::-1, ::-1, ::-1]
    return lax.conv_general_dilated(
        delta,
        flipped,
        (1, 1, 1),
        pads,
        lhs_dilation=(2, 2, 2),
        dimension_numbers=("NCDHW", "DHWOI", "NCDHW"),
        preferred_element_type=jnp.float32,
    )


def depth_extend(block):
    rim = shifted(block[:, :, -1:], "space", 1)
    return jnp.concatenate([rim, block], 2)


def depth_return(grad_ext):
    back = shifted(grad_ext[:, :, :1].astype(jnp.bfloat16), "space", -1).astype(jnp.float32)
    inner = grad_ext[:, :, 1:]
    return inner + jnp.concatenate([jnp.zeros_like(inner[:, :, 1:]), back], 2)


def body(inputs, kernel_one, kernel_two, cotangent):
    samples = inputs.shape[0]
    lower = shifted(inputs[:, :, -1:], "space", 1)
    deeper = jnp.concatenate([lower, inputs], 2)
    below = shifted(deeper[:, :, :, -1:], "filt", 1)
    extended = jnp.concatenate([below, deeper], 3)
    pre_one = forward_conv(extended, kernel_one, ((0, 0), (0, 0), (1, 1)))
    hidden = leaky(pre_one).astype(jnp.bfloat16)
    hidden_ext = depth_extend(hidden)
    out_width = hidden.shape[4] // 2
    out_height = cotangent.shape[3] // out_width
    grad_in = cotangent.reshape(
        samples, cotangent.shape[1], cotangent.shape[2], out_height, out_width
    )
    gathered = lax.all_gather(hidden_ext, "filt", axis=3, tiled=True)
    pre_two = forward_conv(gathered, kernel_two, ((0, 0), (1, 1), (1, 1)))
    activation = leaky(pre_two).astype(jnp.bfloat16).reshape(cotangent.shape)
    delta_two = (grad_in.astype(jnp.float32) * slope_of(pre_two)).astype(jnp.bfloat16)
    grad_two = lax.psum(
        kernel_grad(gathered, delta_two, ((0, 0), (1, 0), (1, 0))).astype(jnp.bfloat16), "space"
    ).astype(jnp.float32)
    partial_grad = input_grad(delta_two, kernel_two, ((2, 2), (1, 2), (1, 2)))
    depth_grad = lax.psum_scatter(
        partial_grad.astype(jnp.bfloat16), "filt", scatter_dimension=3, tiled=True
    ).astype(jnp.float32)
    back_one = depth_return(depth_grad)
    delta_one = (back_one * slope_of(pre_one)).astype(jnp.bfloat16)
    grad_one = lax.psum(
        kernel_grad(extended, delta_one, ((0, 0), (0, 0), (1, 0))), ("space", "filt")
    )
    return (activation, grad_one, grad_two)


def solution(mesh):
    in_specs = (
        P(None, None, "space", "filt", None),
        P(),
        P(None, None, None, None, "filt"),
        P(None, "filt", "space", None),
    )
    out_specs = (P(None, "filt", "space", None), P(), P(None, None, None, None, "filt"))
    return jax.shard_map(body, mesh=mesh, in_specs=in_specs, out_specs=out_specs, check_vma=False)
```

profile of v0, /device:TPU:1, one launch (start us, length us, event | category | flops | bytes accessed | tf_op | source)
XLA Modules:
  0.0 800.9 jit_solution(5909699806649103440)
XLA Ops:
  7.2 0.0 all-gather.2.cloned.1.call-start
  7.2 1.1 slice.19
  8.4 4.9 collective-permute-start
  13.3 14.4 %copy.79 = bf16[2,64,8,16,128]{1,0,4,3,2:T(2,128)(2,1)} copy(bf16[2,64,8,16,128]{4,3,2,1,0:T(8,128)(2,1)} %param.4) | data formatting | bytes 8388608 | tf_op args[0]
  27.7 0.7 copy.78
  28.5 2.0 pad_maximum_fusion.1
  30.4 0.7 copy.80
  31.1 3.1 collective-permute-start.1
  34.3 5.6 collective-permute-done.1
  39.9 0.7 copy.81
  40.6 30.9 %fusion.34 = bf16[64,9,17,2,128]{0,3,4,2,1:T(2,128)(2,1)S(1)} fusion(bf16[2,64,8,16,128]{1,0,4,3,2:T(2,128)(2,1)} %copy.79, bf16[2,64,1,16,128]{1,0,4,3,2:T(2,128)(2,1)S(1)} %copy.78, bf16[2,64,9,1,128]{1,0,4,3,2:T(2,128)(2,1)S(1)} %copy.81), kind=kLoop, calls=%fused_computation.45 | loop fusion | flops 5013504 | bytes 10027008 | tf_op jit(solution)/shard_map/concatenate | solution.py:73
  71.6 15.2 %pad.2 = bf16[64,9,17,2,144]{0,3,4,2,1:T(2,128)(2,1)S(1)} pad(bf16[64,9,17,2,128]{0,3,4,2,1:T(2,128)(2,1)S(1)} %fusion.34, bf16[]{:T(256)} %constant.1.clone.1), padding=0_0x0_0x0_0x0_0x1_15 | pad | bytes 10653698 | tf_op jit(solution)/shard_map/concatenate | solution.py:73
  86.8 4.1 copy.83
  91.0 0.3 slice.35
  91.3 6.5 compare_select_fusion.1
  97.8 0.1 copy.84
  97.9 0.3 copy.122
  98.2 3.2 collective-permute-start.2
  101.4 0.3 copy.86
  101.7 0.1 slice.38
  101.8 1.1 copy.121
  102.9 1.6 collective-permute-done.2
  104.4 2.7 pad_maximum_fusion
  107.2 0.0 reduce-scatter.4.cloned.1.call-start
  107.2 0.1 copy.92
  107.3 2.1 reshape.40
  109.4 130.6 %all-gather.2.cloned.1.call-done = bf16[2,128,5,64,64]{1,0,4,3,2:T(2,128)(2,1)} async-done(((bf16[2,128,5,8,64]{1,0,4,3,2:T(2,128)(2,1)}), bf16[2,128,5,64,64]{1,0,4,3,2:T(2,128)(2,1)}) %all-gather.2.cloned.1.call-update) | async-done | bytes 10485776 | tf_op jit(solution)/shard_map/all_gather | solution.py:82
  240.0 15.6 %pad.4 = bf16[128,5,64,2,80]{0,3,4,2,1:T(2,128)(2,1)S(1)} pad(bf16[128,5,64,2,64]{0,3,4,2,1:T(2,128)(2,1)} %bitcast.75, bf16[]{:T(256)} %constant.1.clone.1), padding=0_0x0_0x0_0x0_0x1_15 | pad | bytes 23592962 | tf_op jit(solution)/shard_map/all_gather | solution.py:82
  255.6 6.9 copy.89
  262.5 2.2 slice.39
  264.8 12.5 %compare_select_fusion = (f32[2,32,16,5,32]{4,2,3,1,0:T(8,128)}, bf16[2,32,16,5,32]{4,2,3,1,0:T(8,128)(2,1)}) fusion(pred[16,5]{0,1:T(8,128)(4,1)S(1)} %copy-done.10, bf16[3,3,3,128,32]{3,4,2,1,0:T(8,128)(2,1)S(1)} %copy-done.7, bf16[128,5,64,2,7,2]{0,4,3,5,2,1:T(8,128)(2,1)} %slice.39, bf16[128,5,64,2,8,10]{0,4,3,5,2,1:T(8,128)(2,1)S(1)} %copy.89), kind=kOutput, calls=%fused_computation.18 | convolution fusion | flops 1168834560 | bytes 16605264 | tf_op jit(solution)/shard_map/conv_general_dilated | solution.py:22
  277.3 2.5 copy.93
  279.8 1.5 slice.41
  281.4 4.1 copy.108
  285.4 2.7 fusion.17
  288.2 2.4 copy.111
  290.6 1.5 pad.6.clone
  292.1 1.6 fusion.18
  293.7 3.5 copy.96
  297.2 24.0 %select_convert_fusion = bf16[5,64,16,10,128]{4,2,3,1,0:T(8,128)(2,1)S(1)} fusion(pred[16,10]{0,1:T(8,128)(4,1)S(1)} %copy-done.8, bf16[3,3,3,128,32]{3,4,2,1,0:T(8,128)(2,1)S(1)} %copy-done.7, bf16[32,2,32,2,8,6]{0,4,3,5,2,1:T(8,128)(2,1)S(1)} %copy.96), kind=kOutput, calls=%fused_computation.2 | convolution fusion | flops 1133772800 | bytes 13721760 | tf_op jit(solution)/shard_map/conv_general_dilated | solution.py:46
  321.2 7.1 copy.97
  328.3 10.5 %slice_bitcast_fusion = bf16[2,128,5,64,64]{1,3,4,0,2:T(8,128)(2,1)} fusion(bf16[5,64,2,80,128]{4,1,3,2,0:T(8,128)(2,1)} %bitcast.72), kind=kLoop, calls=%fused_computation.12 | loop fusion | bytes 20971520 | tf_op jit(solution)/shard_map/convert_element_type | solution.py:91
  338.8 14.7 %copy.102 = bf16[2,128,5,64,64]{1,4,0,2,3:T(8,128)(2,1)} copy(bf16[2,128,5,64,64]{1,3,4,0,2:T(8,128)(2,1)} %slice_bitcast_fusion) | data formatting | bytes 20971520
  353.4 14.8 %copy.120 = bf16[8,8,640,128]{3,1,2,0:T(8,128)(2,1)} copy(bf16[8,8,640,128]{3,2,1,0:T(8,128)(2,1)} %bitcast.74) | data formatting | bytes 20971520
  368.3 0.0 all-reduce.6.cloned.1.call-start
  368.4 3.9 copy.98
  372.3 2.3 copy.100
  374.6 125.5 %reduce-scatter.4.cloned.1.call-done = bf16[8,81920]{1,0:T(8,128)(2,1)} async-done(((bf16[64,81920]{1,0:T(8,128)(2,1)}), bf16[8,81920]{1,0:T(8,128)(2,1)}) %reduce-scatter.4.cloned.1.call-update) | async-done | bytes 1310736
  500.1 1.5 copy.113
  501.6 0.2 copy.110
  501.8 3.1 collective-permute-start.3
  505.0 23.2 %convolution_convert_fusion = bf16[3,3,3,128,32]{3,4,2,1,0:T(8,128)(2,1)} fusion(bf16[2,128,5,64,64]{1,0,4,3,2:T(2,128)(2,1)} %all-gather.2.cloned.1.call-done, bf16[2,32,2,32,32]{1,0,4,3,2:T(2,128)(2,1)} %copy.100), kind=kOutput, calls=%fused_computation.32 | convolution fusion | flops 887304192 | bytes 10969088 | tf_op jit(solution)/shard_map/conv_general_dilated | solution.py:33
  528.2 0.0 all-reduce.4.cloned.1.call-start
  528.2 0.1 slice.44
  528.3 2.6 fusion.16
  530.9 28.8 %fusion.20 = f32[3,3,3,64,128]{4,3,2,1,0:T(8,128)} fusion(bf16[2,128,4,8,64]{1,3,4,0,2:T(8,128)(2,1)S(1)} %fusion.16, bf16[2,64,8,16,128]{1,0,4,3,2:T(2,128)(2,1)} %copy.79, bf16[2,64,1,16,128]{1,0,4,3,2:T(2,128)(2,1)S(1)} %copy.78, bf16[2,64,9,1,128]{1,0,4,3,2:T(2,128)(2,1)} %copy-done.4), kind=kOutput, calls=%fused_computation.35 | convolution fusion | flops 1817542656 | bytes 6946816 | tf_op jit(solution)/shard_map/conv_general_dilated | solution.py:33
  559.8 0.3 copy.90
  560.1 0.1 slice_bitcast_fusion.2
  560.2 2.2 copy.104
  562.4 1.7 reshape.55
  564.1 74.5 %all-reduce.6.cloned.1.call-done = bf16[3,3,3,128,32]{3,4,2,1,0:T(8,128)(2,1)} async-done(((bf16[3,3,3,128,32]{3,4,2,1,0:T(8,128)(2,1)}), bf16[3,3,3,128,32]{3,4,2,1,0:T(8,128)(2,1)}) %all-reduce.6.cloned.1.call-update) | async-done | bytes 221200 | tf_op jit(solution)/shard_map/psum | solution.py:86
  638.7 1.7 convert_element_type.38
  640.4 151.4 %all-reduce.4.cloned.1.call-done = f32[3,3,3,64,128]{4,3,2,1,0:T(8,128)} async-done(((f32[3,3,3,64,128]{4,3,2,1,0:T(8,128)}), f32[3,3,3,64,128]{4,3,2,1,0:T(8,128)}) %all-reduce.4.cloned.1.call-update) | async-done | bytes 884752 | tf_op jit(solution)/shard_map/psum | solution.py:95
  791.8 2.2 copy.125
  (32 shorter events, 0.2 us)
Async XLA Ops:
  7.2 84.1 %copy-start = (bf16[3,3,3,64,128]{4,3,2,1,0:T(8,128)(2,1)S(1)}, bf16[3,3,3,64,128]{4,3,2,1,0:T(8,128)(2,1)}, u32[]{:S(2)}) copy-start(bf16[3,3,3,64,128]{4,3,2,1,0:T(8,128)(2,1)} %param.5) | copy-start | bytes 1327108
  7.2 232.8 %all-gather.2.cloned.1.call-start = ((), (), s32[]{:S(2)}) async-start(), calls=%async_computation.1 | async-start | bytes 11796480 | tf_op jit(solution)/shard_map/all_gather | solution.py:82
  8.4 19.3 %collective-permute-start = (bf16[2,64,1,16,128]{4,3,2,1,0:T(8,128)(2,1)S(1)}, bf16[2,64,1,16,128]{4,3,2,1,0:T(8,128)(2,1)S(1)}, u32[]{:S(2)}, u32[]{:S(2)}) collective-permute-start(bf16[2,64,1,16,128]{4,3,2,1,0:T(8,128)(2,1)S(1)} %slice.19), channel_id=1, source_target_pairs={{0,8},{8,16},{16,24},{24,32},{32,40},{40,48},{48,56},{56,64},{64,7... | collective-permute-start | bytes 1572872 | tf_op jit(solution)/shard_map/ppermute | solution.py:10
  31.1 8.7 %collective-permute-start.1 = (bf16[2,64,9,1,128]{4,1,3,2,0:T(8,128)(2,1)S(1)}, bf16[2,64,9,1,128]{4,1,3,2,0:T(8,128)(2,1)S(1)}, u32[]{:S(2)}, u32[]{:S(2)}) collective-permute-start(bf16[2,64,9,1,128]{4,1,3,2,0:T(8,128)(2,1)S(1)} %copy.80), channel_id=1, source_target_pairs={{0,1},{1,2},{2,3},{3,4},{4,5},{5,6},{6,7},{8,9},{9,10},{10,11},{11... | collective-permute-start | bytes 884744 | tf_op jit(solution)/shard_map/ppermute | solution.py:10
  40.6 31.0 %copy-start.4 = (bf16[2,64,9,1,128]{1,0,4,3,2:T(2,128)(2,1)}, bf16[2,64,9,1,128]{1,0,4,3,2:T(2,128)(2,1)S(1)}, u32[]{:S(2)}) copy-start(bf16[2,64,9,1,128]{1,0,4,3,2:T(2,128)(2,1)S(1)} %copy.81) | copy-start | bytes 884740
  86.8 4.5 copy-start.9
  97.8 9.4 %copy-start.6 = (bf16[2,32,2,1024]{3,2,1,0:T(2,128)(2,1)S(1)}, bf16[2,32,2,1024]{3,2,1,0:T(2,128)(2,1)}, u32[]{:S(2)}) copy-start(bf16[2,32,2,1024]{3,2,1,0:T(2,128)(2,1)} %param.7) | copy-start | bytes 786436
  98.2 6.2 collective-permute-start.2
  107.2 392.9 %reduce-scatter.4.cloned.1.call-start = ((), (), s32[]{:S(2)}) async-start(), calls=%async_computation.4 | async-start | bytes 11796480
  255.6 9.2 %copy-start.7 = (bf16[3,3,3,128,32]{3,4,2,1,0:T(8,128)(2,1)S(1)}, bf16[3,3,3,128,32]{3,4,2,1,0:T(8,128)(2,1)}, u32[]{:S(2)}) copy-start(bf16[3,3,3,128,32]{3,4,2,1,0:T(8,128)(2,1)} %param.6) | copy-start | bytes 663556
  255.6 9.2 %copy-start.10 = (pred[16,5]{0,1:T(8,128)(4,1)S(1)}, pred[16,5]{0,1:T(8,128)(4,1)}, u32[]{:S(2)}) copy-start(pred[16,5]{0,1:T(8,128)(4,1)} %constant.28) | copy-start | bytes 244
  288.1 3.9 copy-start.2
  288.1 9.0 %copy-start.8 = (pred[16,10]{0,1:T(8,128)(4,1)S(1)}, pred[16,10]{0,1:T(8,128)(4,1)}, u32[]{:S(2)}) copy-start(pred[16,10]{0,1:T(8,128)(4,1)} %constant.30) | copy-start | bytes 484
  368.3 4.0 copy-start.3
  368.3 270.4 %all-reduce.6.cloned.1.call-start = ((), (), s32[]{:S(2)}) async-start(), calls=%async_computation.3 | async-start | bytes 442368 | tf_op jit(solution)/shard_map/psum | solution.py:86
  501.8 26.5 %collective-permute-start.3 = (bf16[2,128,1,8,64]{1,3,4,0,2:T(8,128)(2,1)S(1)}, bf16[2,128,1,8,64]{1,3,4,0,2:T(8,128)(2,1)S(1)}, u32[]{:S(2)}, u32[]{:S(2)}) collective-permute-start(bf16[2,128,1,8,64]{1,3,4,0,2:T(8,128)(2,1)S(1)} %copy.110), channel_id=1, source_target_pairs={{8,0},{16,8},{24,16},{32,24},{40,32},{48,40},{56,48},{64,56},{72,6... | collective-permute-start | bytes 786440 | tf_op jit(solution)/shard_map/ppermute | solution.py:10
  528.2 263.6 %all-reduce.4.cloned.1.call-start = ((), (), s32[]{:S(2)}) async-start(), calls=%async_computation.2 | async-start | bytes 1769472 | tf_op jit(solution)/shard_map/psum | solution.py:95
  530.9 28.9 %copy-start.5 = (bf16[2,32,16,5,32]{4,2,3,1,0:T(8,128)(2,1)S(1)}, bf16[2,32,16,5,32]{4,2,3,1,0:T(8,128)(2,1)}, u32[]{:S(2)}) copy-start(bf16[2,32,16,5,32]{4,2,3,1,0:T(8,128)(2,1)} %get-tuple-element.13) | copy-start | bytes 983044
  530.9 263.0 %copy-start.1 = (bf16[3,3,3,64,128]{4,3,2,1,0:T(8,128)(2,1)S(1)}, bf16[3,3,3,64,128]{4,3,2,1,0:T(8,128)(2,1)}, u32[]{:S(2)}) copy-start(bf16[3,3,3,64,128]{4,3,2,1,0:T(8,128)(2,1)} %param.5) | copy-start | bytes 1327108
Sparse Core Ops, SparseCore 0:
  107.3 132.6 all-gather.1
  368.4 131.6 reduce-scatter.3
  528.3 110.3 all-reduce.5
  643.9 147.8 all-reduce.3
where the time goes:
time: 810 us; the launch traced here: 801 us
  waiting for transfers between devices  489 us (60%)
  local copies, waits for them, and re-layouts  143 us (18%)
  matrix products  95 us (12%)
  other arithmetic  44.3 us (5%)
  between operations  14.6 us (2%)
  starting transfers between devices  14.5 us (2%)
    psum x1, waiting for transfers between devices, body(): lax.psum(kernel_grad(extended, delta_one, ((0, 0), (0, 0), (1, 0))), ('sp...  151 us
    all_gather x1, waiting for transfers between devices, body(): gathered = lax.all_gather(hidden_ext, 'filt', axis=3, tiled=True)  131 us
    unnamed x5, waiting for transfers between devices  126 us
    psum x1, waiting for transfers between devices, body(): lax.psum(kernel_grad(gathered, delta_two, ((0, 0), (1, 0), (1, 0))).astyp...  74.5 us
    unnamed x34, local copies, waits for them, and re-layouts  59.5 us
    conv_general_dilated x2, matrix products, kernel_grad(): lax.conv_general_dilated(field, delta, (1, 1, 1), pads, rhs_dilation=(2,...  52 us
    concatenate x1, other arithmetic, body(): extended = jnp.concatenate([below, deeper], 3)  30.9 us
    conv_general_dilated x1, matrix products, input_grad(): lax.conv_general_dilated(delta, flipped, (1, 1, 1), pads, lhs_dilation=(2...  24 us
  transfers between devices with their start and end apart: 8, of which 6 were waited for; matrix products, arithmetic and copies ran while one was open for 11% of the time, Pallas kernels for 0%

commit v1 on v0

v1 whole, which is shorter than its diff:
```python
import jax
import jax.numpy as jnp
import numpy as np
from jax import lax
from jax.experimental import pallas as pl
from jax.experimental.pallas import tpu as pltpu
from jax.sharding import PartitionSpec as P

BF = jnp.bfloat16
F32 = jnp.float32
MIB = 1 << 20
LANES = (((1,), (1,)), ((), ()))
PLAIN = (((1,), (0,)), ((), ()))


def params(mib):
    return pltpu.CompilerParams(vmem_limit_bytes=mib * MIB)


def vmem(count):
    return [pl.BlockSpec(memory_space=pltpu.VMEM)] * count


def dot(a, b, dims=PLAIN):
    return lax.dot_general(a, b, dims, preferred_element_type=F32)


def selection():
    rows = np.arange(192)
    column = 2 * (rows % 32) + (rows % 64) // 32
    wanted = 2 * column + rows // 64 - 1
    return (wanted[:, None] == np.arange(128)[None, :]).astype(np.float32)


def spread(sel, rows):
    return dot(sel, rows, LANES).astype(BF)


def split_kernel(x_ref, sel_ref, q_ref, wide):
    wide[...] = x_ref[...].reshape(2048, 128).astype(F32)
    sel = sel_ref[...]
    for k in range(8):
        pair = [wide[pl.ds(2 * k + p, 128, stride=16), :].astype(BF) for p in range(2)]
        both = spread(sel, jnp.concatenate(pair, 0))
        for p in range(2):
            q_ref[0, p, k] = both[:, 128 * p : 128 * p + 128].reshape(3, 64, 128)


def split(inputs, sel):
    return pl.pallas_call(
        split_kernel,
        grid=(8,),
        in_specs=[
            pl.BlockSpec((2, 64, 1, 16, 128), lambda d: (0, 0, d, 0, 0)),
            pl.BlockSpec((192, 128), lambda d: (0, 0)),
        ],
        out_specs=pl.BlockSpec((1, 2, 8, 3, 64, 128), lambda d: (d, 0, 0, 0, 0, 0)),
        out_shape=jax.ShapeDtypeStruct((8, 2, 8, 3, 64, 128), BF),
        scratch_shapes=[pltpu.VMEM((2048, 128), F32)],
        compiler_params=params(32),
        cost_estimate=pl.CostEstimate(flops=1 << 30, bytes_accessed=11 << 20, transcendentals=0),
        name="split_width",
    )(inputs, sel)


def field_rows(q_ref, qd_ref, qr_ref, a, t, u, v):
    d = 2 * a + t - 1
    if d < 0:
        piece = {0: qd_ref[0:8, v], 1: qd_ref[9:17, v], 2: qd_ref[1:9, v]}[u]
    elif u == 0:
        piece = jnp.concatenate([qr_ref[d, v][None], q_ref[d, 1, 0:7, v]], 0)
    else:
        piece = q_ref[d, u - 1, :, v]
    return piece.reshape(512, 128)


def first_kernel(q_ref, xd_ref, xr_ref, sel_ref, k_ref, h_ref, qd_ref, qr_ref, w_ref):
    sel = sel_ref[...]
    for k in range(17):
        qd_ref[k] = spread(sel, xd_ref[k]).reshape(3, 64, 128)
    for k in range(8):
        qr_ref[k] = spread(sel, xr_ref[k]).reshape(3, 64, 128)
    w_ref[...] = jnp.zeros_like(w_ref)
    for k in range(27):
        w_ref[k * 128 : k * 128 + 64, 0:128] = k_ref[k]
        w_ref[k * 128 + 64 : k * 128 + 128, 128:256] = k_ref[k]
    for a in range(4):
        taps = [field_rows(q_ref, qd_ref, qr_ref, a, t, u, v) for t in range(3) for u in range(3) for v in range(3)]
        pre = dot(jnp.concatenate(taps, 1), w_ref[...])
        h_ref[a] = jnp.where(pre > 0, pre, 0.3 * pre).astype(BF).reshape(8, 64, 256)


def first(q, xd, xr, sel, kernel):
    return pl.pallas_call(
        first_kernel,
        in_specs=vmem(5),
        out_specs=vmem(3),
        out_shape=(
            jax.ShapeDtypeStruct((4, 8, 64, 256), BF),
            jax.ShapeDtypeStruct((17, 3, 64, 128), BF),
            jax.ShapeDtypeStruct((8, 3, 64, 128), BF),
        ),
        scratch_shapes=[pltpu.VMEM((27 * 128, 256), BF)],
        compiler_params=params(40),
        name="first_layer",
    )(q, xd, xr, sel, kernel)


def hidden_part(h_ref, hd_ref, hr_ref, hc_ref, a, b):
    if a < 0 and b < 0:
        return hc_ref
    if a < 0:
        return hd_ref.at[b]
    if b < 0:
        return hr_ref.at[a]
    return h_ref.at[a, b]


def shift_rows(value, by):
    wide = pltpu.roll(value.astype(F32), by % 32, 0)
    row = lax.broadcasted_iota(jnp.int32, wide.shape, 0)
    keep = row >= by if by > 0 else row < 32 + by
    return jnp.where(keep, wide, 0.0).astype(BF)


def hidden_shifts(parts, hs_ref):
    for a in range(-1, 4):
        for b in range(-1, 8):
            hs_ref[a + 1, b + 1] = shift_rows(hidden_part(*parts, a, b)[32:64, :], 1)


def hidden_rows(parts, hs_ref, t, u, v):
    pieces = []
    for n in range(2):
        for a in range(2):
            for b in range(4):
                i, j = 2 * a + t - 1, 2 * b + u - 1
                cut = slice(128 * n, 128 * n + 128)
                if v == 0:
                    pieces.append(hs_ref[i + 1, j + 1, :, cut])
                else:
                    pieces.append(hidden_part(*parts, i, j)[32 * (v - 1) : 32 * v, cut])
    return jnp.concatenate(pieces, 0)


def tap_weight(w_ref, k):
    return w_ref[:, 32 * k : 32 * k + 32, :].reshape(256, 128)


def eye(size):
    rows = lax.broadcasted_iota(jnp.int32, (size, size), 0)
    return (rows == lax.broadcasted_iota(jnp.int32, (size, size), 1)).astype(F32).astype(BF)


def second_kernel(h_ref, hd_ref, hr_ref, hc_ref, w_ref, g_ref, act_ref, delta_ref, turned_ref, hs_ref):
    parts = (h_ref, hd_ref, hr_ref, hc_ref)
    hidden_shifts(parts, hs_ref)
    keys = [(t, u, v) for t in range(3) for u in range(3) for v in range(3)]
    left = jnp.concatenate([hidden_rows(parts, hs_ref, *key) for key in keys], 1)
    right = jnp.concatenate([tap_weight(w_ref, k) for k in range(27)], 1)
    pre = dot(left, right, LANES)
    act = jnp.where(pre > 0, pre, 0.3 * pre).astype(BF)
    slope = jnp.where(pre > 0, 1.0, 0.3).astype(F32)
    small, large = eye(128), eye(256)
    for n in range(2):
        for a in range(2):
            at = 256 * n + 128 * a
            rows = slice(at, at + 128)
            act_ref[:, a, n] = dot(large, act[rows], LANES).astype(BF).reshape(8, 32, 128)
            came = dot(small, g_ref[:, a, n].reshape(256, 128), LANES)
            delta = (came * slope[rows]).astype(BF)
            delta_ref[n, a] = delta.reshape(4, 32, 256)
            turned_ref[:, rows] = dot(large, delta, LANES).astype(BF)


def second(h, hd, hr, hc, w, g):
    return pl.pallas_call(
        second_kernel,
        in_specs=vmem(6),
        out_specs=vmem(3),
        out_shape=(
            jax.ShapeDtypeStruct((8, 2, 2, 32, 128), BF),
            jax.ShapeDtypeStruct((2, 2, 4, 32, 256), BF),
            jax.ShapeDtypeStruct((256, 512), BF),
        ),
        scratch_shapes=[pltpu.VMEM((5, 9, 32, 256), BF)],
        compiler_params=params(40),
        name="second_layer",
    )(h, hd, hr, hc, w, g)


def second_grad_kernel(h_ref, hd_ref, hr_ref, hc_ref, turned_ref, out_ref, hs_ref):
    parts = (h_ref, hd_ref, hr_ref, hc_ref)
    hidden_shifts(parts, hs_ref)
    turned = turned_ref[...]
    keys = [(t, u, v) for t in range(3) for u in range(3) for v in range(3)]
    for k in range(0, 27, 2):
        some = keys[k : k + 2]
        right = jnp.concatenate([hidden_rows(parts, hs_ref, *key) for key in some], 1)
        both = dot(turned, right).astype(BF)
        for p in range(len(some)):
            rows = slice(32 * (k + p), 32 * (k + p) + 32)
            out_ref[:, rows, :] = both[:, 128 * p : 128 * p + 128].reshape(8, 32, 128)


def second_grad(h, hd, hr, hc, turned):
    return pl.pallas_call(
        second_grad_kernel,
        in_specs=vmem(5),
        out_specs=vmem(1)[0],
        out_shape=jax.ShapeDtypeStruct((8, 864, 128), BF),
        scratch_shapes=[pltpu.VMEM((5, 9, 32, 256), BF)],
        compiler_params=params(40),
        name="second_kernel_grad",
    )(h, hd, hr, hc, turned)


def delta_part(d_ref, dd_ref, dr_ref, dc_ref, n, a, b):
    if a > 1 and b > 3:
        return dc_ref.at[n]
    if a > 1:
        return dd_ref.at[n, b]
    if b > 3:
        return dr_ref.at[n, a]
    return d_ref.at[n, a, b]


def back_kernel(d_ref, dd_ref, dr_ref, dc_ref, w_ref, h_ref, out_ref, ds_ref):
    parts = (d_ref, dd_ref, dr_ref, dc_ref)
    for n in range(2):
        for a in range(3):
            for b in range(5):
                ds_ref[n, a, b] = shift_rows(delta_part(*parts, n, a, b)[...], -1)
    nothing = jnp.zeros((256, 128), BF)
    choice = (((1, 0),), ((2, 0), (0, 1)))
    for pa in range(2):
        for pb in range(2):
            left, right = [], []
            for t, i in choice[pa]:
                for u, j in choice[pb]:
                    spots = [(n, a + i, b + j) for n in range(2) for a in range(2) for b in range(4)]
                    left.append(jnp.concatenate([delta_part(*parts, *spot)[...] for spot in spots], 0))
                    left.append(jnp.concatenate([ds_ref[spot] for spot in spots], 0))
                    k = 9 * t + 3 * u
                    right.append(jnp.concatenate([tap_weight(w_ref, k + 1), tap_weight(w_ref, k + 2)], 1))
                    right.append(jnp.concatenate([nothing, tap_weight(w_ref, k)], 1))
            back = dot(jnp.concatenate(left, 1), jnp.concatenate(right, 0))
            for n in range(2):
                for a in range(2):
                    for b in range(4):
                        at = 256 * n + 128 * a + 32 * b
                        for pc in range(2):
                            rows, cut = slice(32 * pc, 32 * pc + 32), slice(128 * n, 128 * n + 128)
                            spot = (2 * a + pa, 2 * b + pb, rows, cut)
                            slope = jnp.where(h_ref[spot].astype(F32) > 0, 1.0, 0.3)
                            value = back[at : at + 32, 128 * pc : 128 * pc + 128]
                            out_ref[spot] = (value * slope).astype(BF)


def back(d, dd, dr, dc, w, h):
    return pl.pallas_call(
        back_kernel,
        in_specs=vmem(6),
        out_specs=vmem(1)[0],
        out_shape=jax.ShapeDtypeStruct((4, 8, 64, 256), BF),
        scratch_shapes=[pltpu.VMEM((2, 3, 5, 32, 256), BF)],
        compiler_params=params(40),
        name="back_one",
    )(d, dd, dr, dc, w, h)


def first_grad_kernel(d_ref, q_ref, qd_ref, qr_ref, out_ref, turned_ref):
    large = eye(256)
    for a in range(4):
        turned_ref[:, 512 * a : 512 * a + 512] = dot(large, d_ref[a].reshape(512, 256), LANES).astype(BF)
    keys = [(t, u, v) for t in range(3) for u in range(3) for v in range(3)]
    lane = lax.broadcasted_iota(jnp.int32, (128, 128), 1)
    for k in range(0, 27, 2):
        some = keys[k : k + 2]
        right = [
            jnp.concatenate([field_rows(q_ref, qd_ref, qr_ref, a, *key) for a in range(4)], 0) for key in some
        ]
        both = dot(turned_ref[...], jnp.concatenate(right, 1))
        one = both[0:128, 0:128] + pltpu.roll(both[128:256, 0:128], 64, 1)
        if len(some) == 2:
            two = both[128:256, 128:256] + pltpu.roll(both[0:128, 128:256], 64, 1)
        else:
            two = jnp.zeros_like(one)
        out_ref[64 * k : 64 * k + 128, :] = jnp.where(lane < 64, one, two).T.astype(BF)
    out_ref[1792:2048, :] = jnp.zeros((256, 128), BF)


def first_grad(d, q, qd, qr):
    return pl.pallas_call(
        first_grad_kernel,
        in_specs=vmem(4),
        out_specs=vmem(1)[0],
        out_shape=jax.ShapeDtypeStruct((2048, 128), BF),
        scratch_shapes=[pltpu.VMEM((256, 2048), BF)],
        compiler_params=params(40),
        name="first_kernel_grad",
    )(d, q, qd, qr)


def exchange(value, axes):
    return lax.all_to_all(value, axes, 0, 0, tiled=True)


def everywhere(value, axis):
    devices = lax.axis_size(axis)
    return exchange(jnp.broadcast_to(value[None], (devices,) + value.shape), axis)


def shifted(value, depth, height):
    deep, high = lax.axis_size("space"), lax.axis_size("filt")
    pairs = [
        (i * high + j, (i + depth) * high + j + height)
        for i in range(deep)
        for j in range(high)
        if 0 <= i + depth < deep and 0 <= j + height < high
    ]
    return lax.ppermute(value, ("space", "filt"), pairs)


def body(inputs, kernel_one, kernel_two, cotangent):
    sel = jnp.asarray(selection(), BF)
    last = jnp.transpose(inputs[:, :, 7], (2, 0, 1, 3)).reshape(16, 128, 128)
    side = jnp.transpose(inputs[:, :, :, 15], (2, 0, 1, 3)).reshape(8, 128, 128)
    order = list(range(1, 16, 2)) + list(range(0, 16, 2))
    rim_depth = shifted(jnp.concatenate([last[k : k + 1] for k in order], 0), 1, 0)
    rim_corner = shifted(last[15:16], 1, 1)
    rim_side = shifted(side, 0, 1)
    own = jnp.transpose(kernel_two, (0, 1, 2, 4, 3)).reshape(864, 128)
    parts = jnp.transpose(cotangent.reshape(2, 32, 2, 8, 128), (3, 2, 0, 1, 4)).reshape(8, 128, 128)
    mixed = exchange(jnp.concatenate([jnp.broadcast_to(own[None], (8, 864, 128)), parts], 1), "filt")
    weight, grad_in = mixed[:, :864], mixed[:, 864:].reshape(8, 2, 2, 32, 128)

    q = split(inputs, sel)
    h, qd, qr = first(
        q, jnp.concatenate([rim_corner, rim_depth], 0), rim_side, sel, kernel_one.reshape(27, 64, 128)
    )
    hd, hr, hc = shifted(h[3], 1, 0), shifted(h[:, 7], 0, 1), shifted(h[3, 7], 1, 1)
    act, delta, turned = second(h, hd, hr, hc, weight, grad_in)
    dd, dr, dc = shifted(delta[:, 0], -1, 0), shifted(delta[:, :, 0], 0, -1), shifted(delta[:, 0, 0], -1, -1)
    grad_two = second_grad(h, hd, hr, hc, turned)
    delta_one = back(delta, dd, dr, dc, weight, h)
    grad_one = first_grad(delta_one, q, qd, qr)

    two = jnp.transpose(grad_two.reshape(8, 16, 54, 128), (1, 0, 2, 3)).reshape(128, 54, 128)
    one = grad_one.reshape(128, 16, 128)
    came = exchange(jnp.concatenate([two, one], 1), ("space", "filt"))
    total = jnp.sum(came.astype(F32), 0).astype(BF)
    one = everywhere(total[54:], "filt").reshape(128, 128)
    full = everywhere(jnp.concatenate([total[:54], one], 0), "space")
    grad_two = jnp.transpose(full[:, :54].reshape(3, 3, 3, 32, 128), (0, 1, 2, 4, 3)).astype(F32)
    grad_one = full[:, 54:].reshape(2048, 128)[:1728].reshape(3, 3, 3, 64, 128).astype(F32)

    act = exchange(act, "filt").reshape(8, 2, 2, 32, 128)
    activation = jnp.transpose(act, (2, 3, 1, 0, 4)).reshape(cotangent.shape)
    return (activation, grad_one, grad_two)


def solution(mesh):
    in_specs = (
        P(None, None, "space", "filt", None),
        P(),
        P(None, None, None, None, "filt"),
        P(None, "filt", "space", None),
    )
    out_specs = (P(None, "filt", "space", None), P(), P(None, None, None, None, "filt"))
    return jax.shard_map(body, mesh=mesh, in_specs=in_specs, out_specs=out_specs, check_vma=False)
```

time: 810 us -> 175 us (0.22)
  waiting for transfers between devices: 489 us -> 33.5 us
  local copies, waits for them, and re-layouts: 143 us -> 11.7 us
  matrix products: 95 us -> 0 us
  blocking collectives: 0 us -> 59.4 us
  other arithmetic: 44.3 us -> 3.19 us
  starting transfers between devices: 14.5 us -> 44.8 us
  Pallas kernels: 0 us -> 20.2 us
  between operations: 14.6 us -> 1.14 us
    psum x2 -> x0, waiting for transfers between devices: 226 us -> none  [the longest x1 151 us: body(): lax.psum(kernel_grad(extended, delta_one, ((0, 0), (0, 0), (1, 0))), ('sp...]
    all_gather x1 -> x0, waiting for transfers between devices: 131 us -> none  [body(): gathered = lax.all_gather(hidden_ext, 'filt', axis=3, tiled=True)]
    unnamed x5 -> x0, waiting for transfers between devices: 126 us -> none
    conv_general_dilated x5 -> x0, matrix products: 95 us -> none  [the longest x2 52 us: kernel_grad(): lax.conv_general_dilated(field, delta, (1, 1, 1), pads, rhs_dilation=(2,...]
    all_to_all x0 -> x2, blocking collectives: none -> 59.4 us  [exchange(): return lax.all_to_all(value, axes, 0, 0, tiled=True)]
    unnamed x34 -> x30, local copies, waits for them, and re-layouts: 59.5 us -> 1.26 us
    concatenate x3 -> x4, other arithmetic: 35.6 us -> 1.76 us  [the longest x1 1.49 us: body(): jnp.concatenate([jnp.broadcast_to(own[None], (8, 864, 128)), parts], 1)]
    convert_element_type x13 -> x1, local copies, waits for them, and re-layouts: 24.4 us -> 0.79 us  [body(): jnp.transpose(full[:, :54].reshape(3, 3, 3, 32, 128), (0, 1, 2, 4, 3))]
  transfers between devices with their start and end apart: 8 -> 12, of which waited for: 6 -> 4; matrix products, arithmetic and copies ran while one was open for 11% -> 3% of each run, Pallas kernels for 0% -> 6%
where the time goes in v1:
time: 175 us; the launch traced here: 174 us
  blocking collectives  59.4 us (34%)
  starting transfers between devices  44.8 us (26%)
  waiting for transfers between devices  33.5 us (19%)
  Pallas kernels  20.2 us (12%)
  local copies, waits for them, and re-layouts  11.7 us (7%)
  other arithmetic  3.19 us (2%)
    all_to_all x2, blocking collectives, exchange(): return lax.all_to_all(value, axes, 0, 0, tiled=True)  59.4 us
    ppermute x9, starting transfers between devices, shifted(): return lax.ppermute(value, ('space', 'filt'), pairs)  28 us
    all_to_all x3, waiting for transfers between devices, exchange(): return lax.all_to_all(value, axes, 0, 0, tiled=True)  19.4 us
    all_to_all x3, starting transfers between devices, exchange(): return lax.all_to_all(value, axes, 0, 0, tiled=True)  16.8 us
    ppermute x9, waiting for transfers between devices, shifted(): return lax.ppermute(value, ('space', 'filt'), pairs)  14.1 us
    pallas_call x1, Pallas kernels, split(): pl.pallas_call(split_kernel, grid=(8,), in_specs=[pl.BlockSpec((2, 64, 1,...  5.38 us
    pallas_call x1, Pallas kernels, first(): pl.pallas_call(first_kernel, in_specs=vmem(5), out_specs=vmem(3), out_sha...  4.59 us
    pallas_call x1, Pallas kernels, first_grad(): pl.pallas_call(first_grad_kernel, in_specs=vmem(4), out_specs=vmem(1)[0],...  4.42 us
  transfers between devices with their start and end apart: 12, of which 4 were waited for; matrix products, arithmetic and copies ran while one was open for 3% of the time, Pallas kernels for 6%

profile of v1, /device:TPU:1, one launch (start us, length us, event | category | flops | bytes accessed | tf_op | source)
XLA Modules:
  0.0 173.9 jit_solution(7714422946914579077)
XLA Ops:
  0.6 1.1 reshape.67
  1.8 0.1 copy.31
  1.8 1.2 broadcast_in_dim.9
  3.0 1.5 pad_maximum_fusion.1
  4.5 7.6 %all-to-all-start = ((bf16[8,992,128]{2,1,0:T(8,128)(2,1)}), bf16[8,992,128]{2,1,0:T(8,128)(2,1)}, u32[]{:S(2)}, u32[]{:S(2)}) async-start(bf16[8,992,128]{2,1,0:T(8,128)(2,1)} %pad_maximum_fusion.1), calls=%async_computation | async-start | bytes 4063232 | tf_op jit(solution)/shard_map/all_to_all | solution.py:306
  12.1 0.0 slice-done.2
  12.1 0.1 copy.57
  12.3 0.0 copy-start.3
  12.6 4.6 %collective-permute-start.1 = (bf16[16,128,128]{2,1,0:T(8,128)(2,1)S(1)}, bf16[16,128,128]{2,1,0:T(8,128)(2,1)S(1)}, u32[]{:S(2)}, u32[]{:S(2)}) collective-permute-start(bf16[16,128,128]{2,1,0:T(8,128)(2,1)S(1)} %constant_dynamic-update-slice_fusion), channel_id=1, source_target_pairs={{0,8},{1,9},{2,10},{3,11},{4,12},{5,13},{6,14},{7,15},{8,16},{9,17... | collective-permute-start | bytes 1572872 | tf_op jit(solution)/shard_map/ppermute | solution.py:322
  17.2 0.0 copy-done.1
  17.2 0.6 slice.175
  17.8 0.1 copy.45
  17.9 0.0 copy-start.2
  17.9 3.8 %collective-permute-start.2 = (bf16[8,128,128]{2,1,0:T(8,128)(2,1)S(1)}, bf16[8,128,128]{2,1,0:T(8,128)(2,1)S(1)}, u32[]{:S(2)}, u32[]{:S(2)}) collective-permute-start(bf16[8,128,128]{2,1,0:T(8,128)(2,1)S(1)} %bitcast.75), channel_id=1, source_target_pairs={{0,1},{1,2},{2,3},{3,4},{4,5},{5,6},{6,7},{8,9},{9,10},{10,11},{11... | collective-permute-start | bytes 786440 | tf_op jit(solution)/shard_map/ppermute | solution.py:322
  21.7 3.1 %collective-permute-start = (bf16[1,128,128]{2,1,0:T(8,128)(2,1)S(1)}, bf16[1,128,128]{2,1,0:T(8,128)(2,1)S(1)}, u32[]{:S(2)}, u32[]{:S(2)}) collective-permute-start(bf16[1,128,128]{2,1,0:T(8,128)(2,1)S(1)} %bitcast.78), channel_id=1, source_target_pairs={{0,9},{1,10},{2,11},{3,12},{4,13},{5,14},{6,15},{8,17},{9,18},{10,... | collective-permute-start | bytes 98312 | tf_op jit(solution)/shard_map/ppermute | solution.py:322
  24.8 0.0 copy-done.3
  24.8 5.4 %split_width.1.q_ref = bf16[8,2,8,3,64,128]{5,4,3,2,1,0:T(8,128)(2,1)S(1)} custom-call(bf16[2,64,8,16,128]{4,3,2,1,0:T(8,128)(2,1)S(1)} %copy-done.1, bf16[192,128]{1,0:T(8,128)(2,1)S(1)} %copy-done.3), custom_call_target="tpu_custom_call" | custom-call | flops 1073741824 | bytes 11534336 | tf_op jit(solution)/shard_map/split_width/pallas_call | solution.py:50
  30.2 0.0 copy-start
  30.2 10.7 %collective-permute-done = bf16[1,128,128]{2,1,0:T(8,128)(2,1)S(1)} collective-permute-done((bf16[1,128,128]{2,1,0:T(8,128)(2,1)S(1)}, bf16[1,128,128]{2,1,0:T(8,128)(2,1)S(1)}, u32[]{:S(2)}, u32[]{:S(2)}) %collective-permute-start) | collective-permute-done | bytes 32800 | tf_op jit(solution)/shard_map/ppermute | solution.py:322
  40.9 0.0 collective-permute-done.1
  40.9 0.1 pad_maximum_fusion.2.xd_ref
  40.9 0.0 collective-permute-done.2.xr_ref
  40.9 0.0 copy-done.2
  41.0 4.6 %first_layer.1 = (bf16[4,8,64,256]{3,2,1,0:T(8,128)(2,1)S(1)}, bf16[17,3,64,128]{3,2,1,0:T(8,128)(2,1)S(1)}, bf16[8,3,64,128]{3,2,1,0:T(8,128)(2,1)S(1)}) custom-call(bf16[8,2,8,3,64,128]{5,4,3,2,1,0:T(8,128)(2,1)S(1)} %split_width.1.q_ref, bf16[17,128,128]{2,1,0:T(8,128)(2,1)S(1)} %pad_maximum_fusion.2.xd_ref, ...), custom_call_target="tpu_custom_call" | custom-call | tf_op jit(solution)/shard_map/first_layer/pallas_call | solution.py:94
  45.6 0.0 copy-done
  45.6 5.0 %collective-permute-start.3 = (bf16[8,64,256]{2,1,0:T(8,128)(2,1)S(1)}, bf16[8,64,256]{2,1,0:T(8,128)(2,1)S(1)}, u32[]{:S(2)}, u32[]{:S(2)}) collective-permute-start(bf16[8,64,256]{2,1,0:T(8,128)(2,1)S(1)} %slice_bitcast_fusion), channel_id=1, source_target_pairs={{0,8},{1,9},{2,10},{3,11},{4,12},{5,13},{6,14},{7,15},{8,16},{9,17... | collective-permute-start | bytes 786440 | tf_op jit(solution)/shard_map/ppermute | solution.py:322
  50.6 3.7 %collective-permute-start.4 = (bf16[4,64,256]{2,1,0:T(8,128)(2,1)S(1)}, bf16[4,64,256]{2,1,0:T(8,128)(2,1)S(1)}, u32[]{:S(2)}, u32[]{:S(2)}) collective-permute-start(bf16[4,64,256]{2,1,0:T(8,128)(2,1)S(1)} %slice_bitcast_fusion.2), channel_id=1, source_target_pairs={{0,1},{1,2},{2,3},{3,4},{4,5},{5,6},{6,7},{8,9},{9,10},{10,11},{11... | collective-permute-start | bytes 393224 | tf_op jit(solution)/shard_map/ppermute | solution.py:322
  54.3 2.8 %collective-permute-start.5 = (bf16[64,256]{1,0:T(8,128)(2,1)S(1)}, bf16[64,256]{1,0:T(8,128)(2,1)S(1)}, u32[]{:S(2)}, u32[]{:S(2)}) collective-permute-start(bf16[64,256]{1,0:T(8,128)(2,1)S(1)} %slice_bitcast_fusion.5), channel_id=1, source_target_pairs={{0,9},{1,10},{2,11},{3,12},{4,13},{5,14},{6,15},{8,17},{9,18},{10,... | collective-permute-start | bytes 98312 | tf_op jit(solution)/shard_map/ppermute | solution.py:322
  57.1 0.0 all-to-all-done
  57.1 1.0 slice.207
  58.1 1.6 slice.206.w_ref
  59.7 0.0 collective-permute-done.5.hc_ref
  59.7 0.0 collective-permute-done.4.hr_ref
  59.7 0.0 collective-permute-done.3.hd_ref
  59.7 3.2 %second_layer.1 = (bf16[8,2,2,32,128]{4,3,2,1,0:T(8,128)(2,1)}, bf16[2,2,4,32,256]{4,3,2,1,0:T(8,128)(2,1)S(1)}, bf16[256,512]{1,0:T(8,128)(2,1)S(1)}) custom-call(bf16[4,8,64,256]{3,2,1,0:T(8,128)(2,1)S(1)} %get-tuple-element.9.h_ref, bf16[8,64,256]{2,1,0:T(8,128)(2,1)S(1)} %collective-permute-done.3.hd_ref, ...), custom_call_target="tpu_custom_call" | custom-call | tf_op jit(solution)/shard_map/second_layer/pallas_call | solution.py:177
  63.0 1.3 collective-permute-start.7
  64.3 2.2 %collective-permute-start.6 = (bf16[2,4,32,256]{3,2,1,0:T(8,128)(2,1)S(1)}, bf16[2,4,32,256]{3,2,1,0:T(8,128)(2,1)S(1)}, u32[]{:S(2)}, u32[]{:S(2)}) collective-permute-start(bf16[2,4,32,256]{3,2,1,0:T(8,128)(2,1)S(1)} %slice_bitcast_fusion.1), channel_id=1, source_target_pairs={{8,0},{9,1},{10,2},{11,3},{12,4},{13,5},{14,6},{15,7},{16,8},{17,9... | collective-permute-start | bytes 393224 | tf_op jit(solution)/shard_map/ppermute | solution.py:322
  66.5 1.5 collective-permute-start.8
  68.0 1.2 second_kernel_grad.1
  69.2 0.0 slice-start
  69.2 0.7 copy.33
  69.9 0.0 slice-start.1
  69.9 0.5 copy.56
  70.4 3.4 %collective-permute-done.8.dc_ref = bf16[2,32,256]{2,1,0:T(8,128)(2,1)S(1)} collective-permute-done((bf16[2,32,256]{2,1,0:T(8,128)(2,1)S(1)}, bf16[2,32,256]{2,1,0:T(8,128)(2,1)S(1)}, u32[]{:S(2)}, u32[]{:S(2)}) %collective-permute-start.8) | collective-permute-done | bytes 32800 | tf_op jit(solution)/shard_map/ppermute | solution.py:322
  73.8 0.0 collective-permute-done.7.dr_ref
  73.8 0.0 collective-permute-done.6.dd_ref
  73.8 1.4 back_one.1.d_ref
  75.2 4.4 %first_kernel_grad.1 = bf16[2048,128]{1,0:T(8,128)(2,1)S(1)} custom-call(bf16[4,8,64,256]{3,2,1,0:T(8,128)(2,1)S(1)} %back_one.1.d_ref, bf16[8,2,8,3,64,128]{5,4,3,2,1,0:T(8,128)(2,1)S(1)} %bitcast.63, bf16[17,3,64,128]{3,2,1,0:T(8,128)(2,1)S(1)} %get-tuple-element.13.qd_ref, bf16[8,3,64,128]{3,2,1,0:T(8,128)(2,1)S(1)} %get-tuple-element.14.qr_ref), custom_call_target="tpu_custom_call" | custom-call | tf_op jit(solution)/shard_map/first_kernel_grad/pallas_call | solution.py:294
  79.7 0.1 copy.38
  79.8 0.2 pad_maximum_fusion
  80.0 1.5 copy.39
  81.5 48.0 %all_to_all.25 = bf16[128,70,128]{2,1,0:T(8,128)(2,1)S(1)} all-to-all(bf16[128,70,128]{2,1,0:T(8,128)(2,1)S(1)} %copy.39), channel_id=1, replica_groups=mesh['space'=16,'filt'=8] {'space','filt'}, dimensions={0} | all-to-all | bytes 4587520 | tf_op jit(solution)/shard_map/all_to_all | solution.py:306
  129.5 0.4 reduce_sum.12
  129.9 11.5 %all_to_all.26 = bf16[8,16,128]{2,1,0:T(8,128)(2,1)S(1)} all-to-all(bf16[8,16,128]{2,1,0:T(8,128)(2,1)S(1)} %broadcast_in_dim.10), channel_id=1, replica_groups=mesh['space'=16,'filt'=8] {'filt'}, dimensions={0} | all-to-all | bytes 65536 | tf_op jit(solution)/shard_map/all_to_all | solution.py:306
  141.3 3.4 %all-to-all-start.1 = ((bf16[8,2,2,32,128]{4,3,2,1,0:T(8,128)(2,1)}), bf16[8,2,2,32,128]{4,3,2,1,0:T(8,128)(2,1)S(1)}, u32[]{:S(2)}, u32[]{:S(2)}) async-start(bf16[8,2,2,32,128]{4,3,2,1,0:T(8,128)(2,1)} %get-tuple-element.10), calls=%async_computation.1 | async-start | bytes 524288 | tf_op jit(solution)/shard_map/all_to_all | solution.py:306
  144.8 7.7 %all-to-all-done.1 = bf16[8,2,2,32,128]{4,3,2,1,0:T(8,128)(2,1)S(1)} async-done(((bf16[8,2,2,32,128]{4,3,2,1,0:T(8,128)(2,1)}), bf16[8,2,2,32,128]{4,3,2,1,0:T(8,128)(2,1)S(1)}, u32[]{:S(2)}, u32[]{:S(2)}) %all-to-all-start.1) | async-done | bytes 262176 | tf_op jit(solution)/shard_map/all_to_all | solution.py:306
  152.5 1.0 broadcast_in_dim.22
  153.5 5.8 %all-to-all-start.4 = ((bf16[16,182,128]{2,1,0:T(8,128)(2,1)}), bf16[16,182,128]{2,1,0:T(8,128)(2,1)S(1)}, u32[]{:S(2)}, u32[]{:S(2)}) async-start(bf16[16,182,128]{2,1,0:T(8,128)(2,1)} %broadcast_in_dim.22), calls=%async_computation.4 | async-start | bytes 1507328 | tf_op jit(solution)/shard_map/all_to_all | solution.py:306
  159.2 0.2 copy.41
  159.4 0.8 reshape.78
  160.2 11.7 %all-to-all-done.4 = bf16[16,182,128]{2,1,0:T(8,128)(2,1)S(1)} async-done(((bf16[16,182,128]{2,1,0:T(8,128)(2,1)}), bf16[16,182,128]{2,1,0:T(8,128)(2,1)S(1)}, u32[]{:S(2)}, u32[]{:S(2)}) %all-to-all-start.4) | async-done | bytes 745504 | tf_op jit(solution)/shard_map/all_to_all | solution.py:306
  171.9 0.8 reshape.77
  172.7 0.2 slice.213
  172.9 1.0 convert.4
  (34 shorter events, 0.4 us)
Async XLA Ops:
  4.5 7.6 %slice-start.2 = ((bf16[2,64,8,16,128]{4,3,2,1,0:T(8,128)(2,1)}), bf16[2,64,1,16,128]{4,3,2,1,0:T(8,128)(2,1)S(1)}, s32[]{:S(2)}) async-start(bf16[2,64,8,16,128]{4,3,2,1,0:T(8,128)(2,1)} %x_ref.1), calls=%async_computation.7 | async-start | bytes 1048576 | tf_op jit(solution)/shard_map/slice | solution.py:327
  4.5 52.6 %all-to-all-start = ((bf16[8,992,128]{2,1,0:T(8,128)(2,1)}), bf16[8,992,128]{2,1,0:T(8,128)(2,1)}, u32[]{:S(2)}, u32[]{:S(2)}) async-start(bf16[8,992,128]{2,1,0:T(8,128)(2,1)} %pad_maximum_fusion.1), calls=%async_computation | async-start | bytes 4063232 | tf_op jit(solution)/shard_map/all_to_all | solution.py:306
  12.1 5.1 %copy-start.1 = (bf16[2,64,8,16,128]{4,3,2,1,0:T(8,128)(2,1)S(1)}, bf16[2,64,8,16,128]{4,3,2,1,0:T(8,128)(2,1)}, u32[]{:S(2)}) copy-start(bf16[2,64,8,16,128]{4,3,2,1,0:T(8,128)(2,1)} %x_ref.1) | copy-start | bytes 12582916
  12.3 12.5 %copy-start.3 = (bf16[192,128]{1,0:T(8,128)(2,1)S(1)}, bf16[192,128]{1,0:T(8,128)(2,1)}, u32[]{:S(2)}) copy-start(bf16[192,128]{1,0:T(8,128)(2,1)} %constant.5.clone.sel_ref) | copy-start | bytes 147460
  12.6 28.3 %collective-permute-start.1 = (bf16[16,128,128]{2,1,0:T(8,128)(2,1)S(1)}, bf16[16,128,128]{2,1,0:T(8,128)(2,1)S(1)}, u32[]{:S(2)}, u32[]{:S(2)}) collective-permute-start(bf16[16,128,128]{2,1,0:T(8,128)(2,1)S(1)} %constant_dynamic-update-slice_fusion), channel_id=1, source_target_pairs={{0,8},{1,9},{2,10},{3,11},{4,12},{5,13},{6,14},{7,15},{8,16},{9,17... | collective-permute-start | bytes 1572872 | tf_op jit(solution)/shard_map/ppermute | solution.py:322
  17.9 23.0 %copy-start.2 = (bf16[3,3,3,64,128]{4,3,2,1,0:T(8,128)(2,1)S(1)}, bf16[3,3,3,64,128]{4,3,2,1,0:T(8,128)(2,1)}, u32[]{:S(2)}) copy-start(bf16[3,3,3,64,128]{4,3,2,1,0:T(8,128)(2,1)} %param.6) | copy-start | bytes 1327108
  17.9 23.0 %collective-permute-start.2 = (bf16[8,128,128]{2,1,0:T(8,128)(2,1)S(1)}, bf16[8,128,128]{2,1,0:T(8,128)(2,1)S(1)}, u32[]{:S(2)}, u32[]{:S(2)}) collective-permute-start(bf16[8,128,128]{2,1,0:T(8,128)(2,1)S(1)} %bitcast.75), channel_id=1, source_target_pairs={{0,1},{1,2},{2,3},{3,4},{4,5},{5,6},{6,7},{8,9},{9,10},{10,11},{11... | collective-permute-start | bytes 786440 | tf_op jit(solution)/shard_map/ppermute | solution.py:322
  21.7 19.2 %collective-permute-start = (bf16[1,128,128]{2,1,0:T(8,128)(2,1)S(1)}, bf16[1,128,128]{2,1,0:T(8,128)(2,1)S(1)}, u32[]{:S(2)}, u32[]{:S(2)}) collective-permute-start(bf16[1,128,128]{2,1,0:T(8,128)(2,1)S(1)} %bitcast.78), channel_id=1, source_target_pairs={{0,9},{1,10},{2,11},{3,12},{4,13},{5,14},{6,15},{8,17},{9,18},{10,... | collective-permute-start | bytes 98312 | tf_op jit(solution)/shard_map/ppermute | solution.py:322
  30.2 15.3 %copy-start = (bf16[8,2,8,3,64,128]{5,4,3,2,1,0:T(8,128)(2,1)}, bf16[8,2,8,3,64,128]{5,4,3,2,1,0:T(8,128)(2,1)S(1)}, u32[]{:S(2)}) copy-start(bf16[8,2,8,3,64,128]{5,4,3,2,1,0:T(8,128)(2,1)S(1)} %split_width.1.q_ref) | copy-start | bytes 18874372
  45.6 14.1 %collective-permute-start.3 = (bf16[8,64,256]{2,1,0:T(8,128)(2,1)S(1)}, bf16[8,64,256]{2,1,0:T(8,128)(2,1)S(1)}, u32[]{:S(2)}, u32[]{:S(2)}) collective-permute-start(bf16[8,64,256]{2,1,0:T(8,128)(2,1)S(1)} %slice_bitcast_fusion), channel_id=1, source_target_pairs={{0,8},{1,9},{2,10},{3,11},{4,12},{5,13},{6,14},{7,15},{8,16},{9,17... | collective-permute-start | bytes 786440 | tf_op jit(solution)/shard_map/ppermute | solution.py:322
  50.6 9.1 %collective-permute-start.4 = (bf16[4,64,256]{2,1,0:T(8,128)(2,1)S(1)}, bf16[4,64,256]{2,1,0:T(8,128)(2,1)S(1)}, u32[]{:S(2)}, u32[]{:S(2)}) collective-permute-start(bf16[4,64,256]{2,1,0:T(8,128)(2,1)S(1)} %slice_bitcast_fusion.2), channel_id=1, source_target_pairs={{0,1},{1,2},{2,3},{3,4},{4,5},{5,6},{6,7},{8,9},{9,10},{10,11},{11... | collective-permute-start | bytes 393224 | tf_op jit(solution)/shard_map/ppermute | solution.py:322
  54.3 5.4 %collective-permute-start.5 = (bf16[64,256]{1,0:T(8,128)(2,1)S(1)}, bf16[64,256]{1,0:T(8,128)(2,1)S(1)}, u32[]{:S(2)}, u32[]{:S(2)}) collective-permute-start(bf16[64,256]{1,0:T(8,128)(2,1)S(1)} %slice_bitcast_fusion.5), channel_id=1, source_target_pairs={{0,9},{1,10},{2,11},{3,12},{4,13},{5,14},{6,15},{8,17},{9,18},{10,... | collective-permute-start | bytes 98312 | tf_op jit(solution)/shard_map/ppermute | solution.py:322
  63.0 10.8 %collective-permute-start.7 = (bf16[2,2,32,256]{3,2,1,0:T(8,128)(2,1)S(1)}, bf16[2,2,32,256]{3,2,1,0:T(8,128)(2,1)S(1)}, u32[]{:S(2)}, u32[]{:S(2)}) collective-permute-start(bf16[2,2,32,256]{3,2,1,0:T(8,128)(2,1)S(1)} %slice_bitcast_fusion.3), channel_id=1, source_target_pairs={{1,0},{2,1},{3,2},{4,3},{5,4},{6,5},{7,6},{9,8},{10,9},{11,10},{12... | collective-permute-start | bytes 196616 | tf_op jit(solution)/shard_map/ppermute | solution.py:322
  64.3 9.5 %collective-permute-start.6 = (bf16[2,4,32,256]{3,2,1,0:T(8,128)(2,1)S(1)}, bf16[2,4,32,256]{3,2,1,0:T(8,128)(2,1)S(1)}, u32[]{:S(2)}, u32[]{:S(2)}) collective-permute-start(bf16[2,4,32,256]{3,2,1,0:T(8,128)(2,1)S(1)} %slice_bitcast_fusion.1), channel_id=1, source_target_pairs={{8,0},{9,1},{10,2},{11,3},{12,4},{13,5},{14,6},{15,7},{16,8},{17,9... | collective-permute-start | bytes 393224 | tf_op jit(solution)/shard_map/ppermute | solution.py:322
  66.5 7.3 %collective-permute-start.8 = (bf16[2,32,256]{2,1,0:T(8,128)(2,1)S(1)}, bf16[2,32,256]{2,1,0:T(8,128)(2,1)S(1)}, u32[]{:S(2)}, u32[]{:S(2)}) collective-permute-start(bf16[2,32,256]{2,1,0:T(8,128)(2,1)S(1)} %slice_bitcast_fusion.4), channel_id=1, source_target_pairs={{9,0},{10,1},{11,2},{12,3},{13,4},{14,5},{15,6},{17,8},{18,9},{19,... | collective-permute-start | bytes 98312 | tf_op jit(solution)/shard_map/ppermute | solution.py:322
  69.2 6.1 %slice-start = ((s8[6291456]{0:T(1024)(128)(4,1)}), s8[4194304]{0:T(1024)(128)(4,1)S(1)}, s32[]{:S(2)}) async-start(s8[6291456]{0:T(1024)(128)(4,1)} %bitcast.62), calls=%async_computation.5 | async-start | bytes 8388608
  69.9 5.4 %slice-start.1 = ((s8[6291456]{0:T(1024)(128)(4,1)}), s8[2097152]{0:T(1024)(128)(4,1)S(1)}, s32[]{:S(2)}) async-start(s8[6291456]{0:T(1024)(128)(4,1)} %bitcast.62), calls=%async_computation.6 | async-start | bytes 4194304
  141.3 11.1 %all-to-all-start.1 = ((bf16[8,2,2,32,128]{4,3,2,1,0:T(8,128)(2,1)}), bf16[8,2,2,32,128]{4,3,2,1,0:T(8,128)(2,1)S(1)}, u32[]{:S(2)}, u32[]{:S(2)}) async-start(bf16[8,2,2,32,128]{4,3,2,1,0:T(8,128)(2,1)} %get-tuple-element.10), calls=%async_computation.1 | async-start | bytes 524288 | tf_op jit(solution)/shard_map/all_to_all | solution.py:306
  153.5 18.4 %all-to-all-start.4 = ((bf16[16,182,128]{2,1,0:T(8,128)(2,1)}), bf16[16,182,128]{2,1,0:T(8,128)(2,1)S(1)}, u32[]{:S(2)}, u32[]{:S(2)}) async-start(bf16[16,182,128]{2,1,0:T(8,128)(2,1)} %broadcast_in_dim.22), calls=%async_computation.4 | async-start | bytes 1507328 | tf_op jit(solution)/shard_map/all_to_all | solution.py:306

commit v2 on v1

--- a/solution.py
+++ b/solution.py
@@ -17,8 +17,15 @@
     return pltpu.CompilerParams(vmem_limit_bytes=mib * MIB)
 
 
+def cost(gigaflops, mib):
+    return pl.CostEstimate(flops=gigaflops << 30, bytes_accessed=mib * MIB, transcendentals=0)
+
+
 def vmem(count):
     return [pl.BlockSpec(memory_space=pltpu.VMEM)] * count
+
+
+SCALAR = pl.BlockSpec(memory_space=pltpu.SMEM)
 
 
 def dot(a, b, dims=PLAIN):
@@ -58,7 +65,7 @@
         out_shape=jax.ShapeDtypeStruct((8, 2, 8, 3, 64, 128), BF),
         scratch_shapes=[pltpu.VMEM((2048, 128), F32)],
         compiler_params=params(32),
-        cost_estimate=pl.CostEstimate(flops=1 << 30, bytes_accessed=11 << 20, transcendentals=0),
+        cost_estimate=cost(2, 11),
         name="split_width",
     )(inputs, sel)
 
@@ -102,6 +109,7 @@
         ),
         scratch_shapes=[pltpu.VMEM((27 * 128, 256), BF)],
         compiler_params=params(40),
+        cost_estimate=cost(4, 10),
         name="first_layer",
     )(q, xd, xr, sel, kernel)
 
@@ -152,7 +160,7 @@
     return (rows == lax.broadcasted_iota(jnp.int32, (size, size), 1)).astype(F32).astype(BF)
 
 
-def second_kernel(h_ref, hd_ref, hr_ref, hc_ref, w_ref, g_ref, act_ref, delta_ref, turned_ref, hs_ref):
+def second_kernel(h_ref, hd_ref, hr_ref, hc_ref, w_ref, act_ref, delta_ref, turned_ref, hs_ref):
     parts = (h_ref, hd_ref, hr_ref, hc_ref)
     hidden_shifts(parts, hs_ref)
     keys = [(t, u, v) for t in range(3) for u in range(3) for v in range(3)]
@@ -166,53 +174,64 @@
         for a in range(2):
             at = 256 * n + 128 * a
             rows = slice(at, at + 128)
-            act_ref[:, a, n] = dot(large, act[rows], LANES).astype(BF).reshape(8, 32, 128)
-            came = dot(small, g_ref[:, a, n].reshape(256, 128), LANES)
+            some = slice(64 * a + 32 * n, 32 + 64 * a + 32 * n)
+            act_ref[:, some, :] = dot(large, act[rows], LANES).astype(BF).reshape(8, 32, 128)
+            some = slice(864 + 64 * a + 32 * n, 896 + 64 * a + 32 * n)
+            came = dot(small, w_ref[:, some, :].reshape(256, 128), LANES)
             delta = (came * slope[rows]).astype(BF)
             delta_ref[n, a] = delta.reshape(4, 32, 256)
             turned_ref[:, rows] = dot(large, delta, LANES).astype(BF)
 
 
-def second(h, hd, hr, hc, w, g):
+def second(h, hd, hr, hc, w):
     return pl.pallas_call(
         second_kernel,
-        in_specs=vmem(6),
+        in_specs=vmem(5),
         out_specs=vmem(3),
         out_shape=(
-            jax.ShapeDtypeStruct((8, 2, 2, 32, 128), BF),
+            jax.ShapeDtypeStruct((8, 128, 128), BF),
             jax.ShapeDtypeStruct((2, 2, 4, 32, 256), BF),
             jax.ShapeDtypeStruct((256, 512), BF),
         ),
         scratch_shapes=[pltpu.VMEM((5, 9, 32, 256), BF)],
         compiler_params=params(40),
+        cost_estimate=cost(1, 4),
         name="second_layer",
-    )(h, hd, hr, hc, w, g)
-
-
-def second_grad_kernel(h_ref, hd_ref, hr_ref, hc_ref, turned_ref, out_ref, hs_ref):
+    )(h, hd, hr, hc, w)
+
+
+def second_grad_kernel(core_ref, h_ref, hd_ref, hr_ref, hc_ref, turned_ref, keep_ref, send_ref, hs_ref):
     parts = (h_ref, hd_ref, hr_ref, hc_ref)
     hidden_shifts(parts, hs_ref)
     turned = turned_ref[...]
+    even = core_ref[0] == 0
     keys = [(t, u, v) for t in range(3) for u in range(3) for v in range(3)]
     for k in range(0, 27, 2):
         some = keys[k : k + 2]
         right = jnp.concatenate([hidden_rows(parts, hs_ref, *key) for key in some], 1)
-        both = dot(turned, right).astype(BF)
+        both = dot(turned, right)
         for p in range(len(some)):
-            rows = slice(32 * (k + p), 32 * (k + p) + 32)
-            out_ref[:, rows, :] = both[:, 128 * p : 128 * p + 128].reshape(8, 32, 128)
-
-
-def second_grad(h, hd, hr, hc, turned):
+            one = both[:, 128 * p : 128 * p + 128].reshape(8, 2, 16, 128)
+            low, high = one[:, 0], one[:, 1]
+            spot = ((k + p) // 4, slice(None), slice(16 * ((k + p) % 4), 16 * ((k + p) % 4) + 16))
+            keep_ref[spot] = jnp.where(even, low, high).astype(BF)
+            send_ref[spot] = jnp.where(even, high, low).astype(BF)
+    for ref in (keep_ref, send_ref):
+        ref[6, :, 48:64] = jnp.zeros((8, 16, 128), BF)
+        ref[7] = jnp.zeros((8, 64, 128), BF)
+
+
+def second_grad(core, h, hd, hr, hc, turned):
     return pl.pallas_call(
         second_grad_kernel,
-        in_specs=vmem(5),
-        out_specs=vmem(1)[0],
-        out_shape=jax.ShapeDtypeStruct((8, 864, 128), BF),
+        in_specs=[SCALAR] + vmem(5),
+        out_specs=vmem(2),
+        out_shape=(jax.ShapeDtypeStruct((8, 8, 64, 128), BF),) * 2,
         scratch_shapes=[pltpu.VMEM((5, 9, 32, 256), BF)],
         compiler_params=params(40),
+        cost_estimate=cost(1, 4),
         name="second_kernel_grad",
-    )(h, hd, hr, hc, turned)
+    )(core, h, hd, hr, hc, turned)
 
 
 def delta_part(d_ref, dd_ref, dr_ref, dc_ref, n, a, b):
@@ -265,14 +284,16 @@
         out_shape=jax.ShapeDtypeStruct((4, 8, 64, 256), BF),
         scratch_shapes=[pltpu.VMEM((2, 3, 5, 32, 256), BF)],
         compiler_params=params(40),
+        cost_estimate=cost(1, 5),
         name="back_one",
     )(d, dd, dr, dc, w, h)
 
 
-def first_grad_kernel(d_ref, q_ref, qd_ref, qr_ref, out_ref, turned_ref):
+def first_grad_kernel(core_ref, d_ref, q_ref, qd_ref, qr_ref, keep_ref, send_ref, turned_ref):
     large = eye(256)
     for a in range(4):
         turned_ref[:, 512 * a : 512 * a + 512] = dot(large, d_ref[a].reshape(512, 256), LANES).astype(BF)
+    even = core_ref[0] == 0
     keys = [(t, u, v) for t in range(3) for u in range(3) for v in range(3)]
     lane = lax.broadcasted_iota(jnp.int32, (128, 128), 1)
     for k in range(0, 27, 2):
@@ -286,43 +307,65 @@
             two = both[128:256, 128:256] + pltpu.roll(both[0:128, 128:256], 64, 1)
         else:
             two = jnp.zeros_like(one)
-        out_ref[64 * k : 64 * k + 128, :] = jnp.where(lane < 64, one, two).T.astype(BF)
-    out_ref[1792:2048, :] = jnp.zeros((256, 128), BF)
-
-
-def first_grad(d, q, qd, qr):
+        rows = jnp.where(lane < 64, one, two).T
+        for j in range(4):
+            low, high = rows[32 * j : 32 * j + 16], rows[32 * j + 16 : 32 * j + 32]
+            spot = (k // 4, 2 * (k % 4) + j)
+            keep_ref[spot] = jnp.where(even, low, high).astype(BF)
+            send_ref[spot] = jnp.where(even, high, low).astype(BF)
+    for ref in (keep_ref, send_ref):
+        ref[7] = jnp.zeros((8, 16, 128), BF)
+
+
+def first_grad(core, d, q, qd, qr):
     return pl.pallas_call(
         first_grad_kernel,
-        in_specs=vmem(4),
-        out_specs=vmem(1)[0],
-        out_shape=jax.ShapeDtypeStruct((2048, 128), BF),
+        in_specs=[SCALAR] + vmem(4),
+        out_specs=vmem(2),
+        out_shape=(jax.ShapeDtypeStruct((8, 8, 16, 128), BF),) * 2,
         scratch_shapes=[pltpu.VMEM((256, 2048), BF)],
         compiler_params=params(40),
+        cost_estimate=cost(4, 9),
         name="first_kernel_grad",
-    )(d, q, qd, qr)
+    )(core, d, q, qd, qr)
+
+
+SPACE = ("y_lo", "z", "core")
+FILT = ("y_hi", "x")
+CHIPS = ("y_lo", "z", "y_hi", "x")
 
 
 def exchange(value, axes):
     return lax.all_to_all(value, axes, 0, 0, tiled=True)
 
 
-def everywhere(value, axis):
-    devices = lax.axis_size(axis)
-    return exchange(jnp.broadcast_to(value[None], (devices,) + value.shape), axis)
+def everywhere(value, axes):
+    devices = lax.axis_size(axes)
+    return exchange(jnp.broadcast_to(value[None], (devices,) + value.shape), axes)
+
+
+def total(pieces):
+    return jnp.sum(pieces.astype(F32), 0).astype(BF)
+
+
+def paired(keep, send):
+    came = lax.ppermute(send, "core", [(0, 1), (1, 0)])
+    return (keep.astype(F32) + came.astype(F32)).astype(BF)
 
 
 def shifted(value, depth, height):
-    deep, high = lax.axis_size("space"), lax.axis_size("filt")
+    deep, high = lax.axis_size(SPACE), lax.axis_size(FILT)
     pairs = [
         (i * high + j, (i + depth) * high + j + height)
         for i in range(deep)
         for j in range(high)
         if 0 <= i + depth < deep and 0 <= j + height < high
     ]
-    return lax.ppermute(value, ("space", "filt"), pairs)
+    return lax.ppermute(value, SPACE + FILT, pairs)
 
 
 def body(inputs, kernel_one, kernel_two, cotangent):
+    core = lax.axis_index("core").reshape(1)
     sel = jnp.asarray(selection(), BF)
     last = jnp.transpose(inputs[:, :, 7], (2, 0, 1, 3)).reshape(16, 128, 128)
     side = jnp.transpose(inputs[:, :, :, 15], (2, 0, 1, 3)).reshape(8, 128, 128)
@@ -330,42 +373,49 @@
     rim_depth = shifted(jnp.concatenate([last[k : k + 1] for k in order], 0), 1, 0)
     rim_corner = shifted(last[15:16], 1, 1)
     rim_side = shifted(side, 0, 1)
+    q = split(inputs, sel)
     own = jnp.transpose(kernel_two, (0, 1, 2, 4, 3)).reshape(864, 128)
     parts = jnp.transpose(cotangent.reshape(2, 32, 2, 8, 128), (3, 2, 0, 1, 4)).reshape(8, 128, 128)
-    mixed = exchange(jnp.concatenate([jnp.broadcast_to(own[None], (8, 864, 128)), parts], 1), "filt")
-    weight, grad_in = mixed[:, :864], mixed[:, 864:].reshape(8, 2, 2, 32, 128)
-
-    q = split(inputs, sel)
+    mixed = jnp.concatenate([jnp.broadcast_to(own[None], (8, 864, 128)), parts], 1)
+    mixed, rim_depth, rim_side, rim_corner = lax.optimization_barrier((mixed, rim_depth, rim_side, rim_corner))
+    mixed = exchange(mixed, FILT)
+
     h, qd, qr = first(
         q, jnp.concatenate([rim_corner, rim_depth], 0), rim_side, sel, kernel_one.reshape(27, 64, 128)
     )
     hd, hr, hc = shifted(h[3], 1, 0), shifted(h[:, 7], 0, 1), shifted(h[3, 7], 1, 1)
-    act, delta, turned = second(h, hd, hr, hc, weight, grad_in)
+    act, delta, turned = second(h, hd, hr, hc, mixed)
     dd, dr, dc = shifted(delta[:, 0], -1, 0), shifted(delta[:, :, 0], 0, -1), shifted(delta[:, 0, 0], -1, -1)
-    grad_two = second_grad(h, hd, hr, hc, turned)
-    delta_one = back(delta, dd, dr, dc, weight, h)
-    grad_one = first_grad(delta_one, q, qd, qr)
-
-    two = jnp.transpose(grad_two.reshape(8, 16, 54, 128), (1, 0, 2, 3)).reshape(128, 54, 128)
-    one = grad_one.reshape(128, 16, 128)
-    came = exchange(jnp.concatenate([two, one], 1), ("space", "filt"))
-    total = jnp.sum(came.astype(F32), 0).astype(BF)
-    one = everywhere(total[54:], "filt").reshape(128, 128)
-    full = everywhere(jnp.concatenate([total[:54], one], 0), "space")
-    grad_two = jnp.transpose(full[:, :54].reshape(3, 3, 3, 32, 128), (0, 1, 2, 4, 3)).astype(F32)
-    grad_one = full[:, 54:].reshape(2048, 128)[:1728].reshape(3, 3, 3, 64, 128).astype(F32)
-
-    act = exchange(act, "filt").reshape(8, 2, 2, 32, 128)
+    two = second_grad(core, h, hd, hr, hc, turned)
+    two, dd, dr, dc = lax.optimization_barrier((two, dd, dr, dc))
+    two = paired(*two)
+    delta_one = back(delta, dd, dr, dc, mixed, h)
+    one = paired(*first_grad(core, delta_one, q, qd, qr))
+
+    both = jnp.concatenate([two, one], 2).reshape(64, 80, 128)
+    both = total(exchange(both, CHIPS))
+    one = jnp.broadcast_to(both[None, 64:], (8, 16, 128))
+    came = exchange(jnp.concatenate([act, one], 1), FILT)
+    full = everywhere(jnp.concatenate([both[:64], came[:, 128:].reshape(128, 128)], 0), SPACE)
+    two = full[:, :64].reshape(8, 2, 4, 16, 128)
+    two = jnp.transpose(two, (0, 2, 1, 3, 4)).reshape(1024, 128)[:864].reshape(3, 3, 3, 32, 128)
+    grad_two = jnp.transpose(two, (0, 1, 2, 4, 3)).astype(F32)
+    one = full[:, 64:].reshape(8, 2, 8, 16, 128)
+    one = jnp.transpose(one, (0, 2, 1, 3, 4)).reshape(2048, 128)[:1728]
+    grad_one = one.reshape(3, 3, 3, 64, 128).astype(F32)
+
+    act = came[:, :128].reshape(8, 2, 2, 32, 128)
     activation = jnp.transpose(act, (2, 3, 1, 0, 4)).reshape(cotangent.shape)
     return (activation, grad_one, grad_two)
 
 
 def solution(mesh):
+    fine = jax.sharding.Mesh(mesh.devices.reshape(2, 4, 2, 2, 4), ("y_lo", "z", "core", "y_hi", "x"))
     in_specs = (
-        P(None, None, "space", "filt", None),
+        P(None, None, SPACE, FILT, None),
         P(),
-        P(None, None, None, None, "filt"),
-        P(None, "filt", "space", None),
+        P(None, None, None, None, FILT),
+        P(None, FILT, SPACE, None),
     )
-    out_specs = (P(None, "filt", "space", None), P(), P(None, None, None, None, "filt"))
-    return jax.shard_map(body, mesh=mesh, in_specs=in_specs, out_specs=out_specs, check_vma=False)
+    out_specs = (P(None, FILT, SPACE, None), P(), P(None, None, None, None, FILT))
+    return jax.shard_map(body, mesh=fine, in_specs=in_specs, out_specs=out_specs, check_vma=False)

time: 175 us -> 148 us (0.85)
  blocking collectives: 59.4 us -> 35.4 us
  waiting for transfers between devices: 33.5 us -> 26.2 us
  local copies, waits for them, and re-layouts: 11.7 us -> 13.5 us
    all_to_all x2 -> x1, blocking collectives: 59.4 us -> 35.4 us  [exchange(): return lax.all_to_all(value, axes, 0, 0, tiled=True)]
    ppermute x9 -> x11, waiting for transfers between devices: 14.1 us -> 5.27 us  [the longest x9 4.11 us: shifted(): return lax.ppermute(value, SPACE + FILT, pairs)]
    unnamed x30 -> x46, local copies, waits for them, and re-layouts: 1.26 us -> 6 us
    slice x6 -> x8, local copies, waits for them, and re-layouts: 2.77 us -> 0.13 us  [the longest x1 0.03 us: body(): one = full[:, 64:].reshape(8, 2, 8, 16, 128)]
    ppermute x9 -> x11, starting transfers between devices: 28 us -> 27.9 us  [the longest x9 27.1 us: shifted(): return lax.ppermute(value, SPACE + FILT, pairs)]
  transfers between devices with their start and end apart: 12 -> 14, of which waited for: 4 -> 8; matrix products, arithmetic and copies ran while one was open for 3% -> 5% of each run, Pallas kernels for 6% -> 12%
where the time goes in v2:
time: 148 us; the launch traced here: 147 us
  starting transfers between devices  46.1 us (31%)
  blocking collectives  35.4 us (24%)
  waiting for transfers between devices  26.2 us (18%)
  Pallas kernels  19.6 us (13%)
  local copies, waits for them, and re-layouts  13.5 us (9%)
  other arithmetic  4.9 us (3%)
    all_to_all x1, blocking collectives, exchange(): return lax.all_to_all(value, axes, 0, 0, tiled=True)  35.4 us
    ppermute x9, starting transfers between devices, shifted(): return lax.ppermute(value, SPACE + FILT, pairs)  27.1 us
    all_to_all x3, waiting for transfers between devices, exchange(): return lax.all_to_all(value, axes, 0, 0, tiled=True)  20.9 us
    all_to_all x3, starting transfers between devices, exchange(): return lax.all_to_all(value, axes, 0, 0, tiled=True)  18.2 us
    unnamed x46, local copies, waits for them, and re-layouts  6 us
    pallas_call x1, Pallas kernels, split(): pl.pallas_call(split_kernel, grid=(8,), in_specs=[pl.BlockSpec((2, 64, 1,...  5.37 us
    pallas_call x1, Pallas kernels, first(): pl.pallas_call(first_kernel, in_specs=vmem(5), out_specs=vmem(3), out_sha...  4.58 us
    pallas_call x1, Pallas kernels, first_grad(): pl.pallas_call(first_grad_kernel, in_specs=[SCALAR] + vmem(4), out_specs=...  4.42 us
  transfers between devices with their start and end apart: 14, of which 8 were waited for; matrix products, arithmetic and copies ran while one was open for 5% of the time, Pallas kernels for 12%

profile of v2, /device:TPU:1, one launch (start us, length us, event | category | flops | bytes accessed | tf_op | source)
XLA Modules:
  0.0 146.9 jit_solution(13334502035304731113)
XLA Ops:
  0.6 1.1 slice.145
  1.7 0.1 copy.47
  1.9 0.0 copy-start.11
  1.9 0.0 copy-start.12
  2.2 4.9 %collective-permute-start = (bf16[16,128,128]{2,1,0:T(8,128)(2,1)S(1)}, bf16[16,128,128]{2,1,0:T(8,128)(2,1)S(1)}, u32[]{:S(2)}, u32[]{:S(2)}) collective-permute-start(bf16[16,128,128]{2,1,0:T(8,128)(2,1)S(1)} %constant_dynamic-update-slice_fusion), channel_id=1, source_target_pairs={{0,8},{1,9},{2,10},{3,11},{4,12},{5,13},{6,14},{7,15},{8,16},{9,17... | collective-permute-start | bytes 1572872 | tf_op jit(solution)/shard_map/ppermute | solution.py:364
  7.1 2.1 %slice.178 = bf16[2,64,8,1,128]{4,3,2,1,0:T(2,128)(2,1)S(1)} slice(bf16[2,64,8,16,128]{4,3,2,1,0:T(8,128)(2,1)} %x_ref.1), slice={[0:2], [0:64], [0:8], [15:16], [0:128]} | slice | bytes 524288 | tf_op jit(solution)/shard_map/slice | solution.py:371
  9.3 0.1 copy.37
  9.4 3.1 %collective-permute-start.1 = (bf16[8,128,128]{2,1,0:T(8,128)(2,1)S(1)}, bf16[8,128,128]{2,1,0:T(8,128)(2,1)S(1)}, u32[]{:S(2)}, u32[]{:S(2)}) collective-permute-start(bf16[8,128,128]{2,1,0:T(8,128)(2,1)S(1)} %bitcast.81), channel_id=1, source_target_pairs={{0,1},{1,2},{2,3},{3,4},{4,5},{5,6},{6,7},{8,9},{9,10},{10,11},{11... | collective-permute-start | bytes 786440 | tf_op jit(solution)/shard_map/ppermute | solution.py:364
  12.5 3.1 %collective-permute-start.2 = (bf16[1,128,128]{2,1,0:T(8,128)(2,1)S(1)}, bf16[1,128,128]{2,1,0:T(8,128)(2,1)S(1)}, u32[]{:S(2)}, u32[]{:S(2)}) collective-permute-start(bf16[1,128,128]{2,1,0:T(8,128)(2,1)S(1)} %bitcast.84), channel_id=1, source_target_pairs={{0,9},{1,10},{2,11},{3,12},{4,13},{5,14},{6,15},{8,17},{9,18},{10,... | collective-permute-start | bytes 98312 | tf_op jit(solution)/shard_map/ppermute | solution.py:364
  15.7 0.2 reshape.71
  15.8 0.1 copy.24
  15.9 0.2 broadcast_in_dim.9
  16.2 1.5 %pad_maximum_fusion = bf16[8,992,128]{2,1,0:T(8,128)(2,1)} fusion(bf16[8,128,128]{2,1,0:T(8,128)(2,1)S(1)} %bitcast.76, bf16[8,864,128]{2,1,0:T(8,128)(2,1)S(1)} %broadcast_in_dim.9), kind=kLoop, calls=%fused_computation.1 | loop fusion | flops 4063232 | bytes 4063232 | tf_op jit(solution)/shard_map/concatenate | solution.py:379
  17.7 0.5 collective-permute-done.2
  18.1 0.0 collective-permute-done.1.xr_ref
  18.1 0.0 collective-permute-done
  18.1 8.1 %all-to-all-start = ((bf16[8,992,128]{2,1,0:T(8,128)(2,1)}), bf16[8,992,128]{2,1,0:T(8,128)(2,1)S(1)}, u32[]{:S(2)}, u32[]{:S(2)}) async-start(bf16[8,992,128]{2,1,0:T(8,128)(2,1)} %pad_maximum_fusion), calls=%async_computation | async-start | bytes 4063232 | tf_op jit(solution)/shard_map/all_to_all | solution.py:339
  26.3 0.0 copy-start
  26.3 2.2 %copy-done = bf16[2,64,8,16,128]{4,3,2,1,0:T(8,128)(2,1)S(1)} copy-done((bf16[2,64,8,16,128]{4,3,2,1,0:T(8,128)(2,1)S(1)}, bf16[2,64,8,16,128]{4,3,2,1,0:T(8,128)(2,1)}, u32[]{:S(2)}) %copy-start) | copy-done | bytes 4194328
  28.5 5.4 %split_width.1.q_ref = bf16[8,2,8,3,64,128]{5,4,3,2,1,0:T(8,128)(2,1)S(1)} custom-call(bf16[2,64,8,16,128]{4,3,2,1,0:T(8,128)(2,1)S(1)} %copy-done, bf16[192,128]{1,0:T(8,128)(2,1)S(1)} %copy-done.2), custom_call_target="tpu_custom_call" | custom-call | flops 2147483648 | bytes 11534336 | tf_op jit(solution)/shard_map/split_width/pallas_call | solution.py:57
  33.9 0.1 pad_maximum_fusion.2.xd_ref
  33.9 4.6 %first_layer.1 = (bf16[4,8,64,256]{3,2,1,0:T(8,128)(2,1)S(1)}, bf16[17,3,64,128]{3,2,1,0:T(8,128)(2,1)S(1)}, bf16[8,3,64,128]{3,2,1,0:T(8,128)(2,1)S(1)}) custom-call(bf16[8,2,8,3,64,128]{5,4,3,2,1,0:T(8,128)(2,1)S(1)} %split_width.1.q_ref, bf16[17,128,128]{2,1,0:T(8,128)(2,1)S(1)} %pad_maximum_fusion.2.xd_ref, ...), custom_call_target="tpu_custom_call" | custom-call | flops 4294967296 | bytes 10485760 | tf_op jit(solution)/shard_map/first_layer/pallas_call | solution.py:101
  38.5 0.0 copy-start.7
  38.6 0.9 copy-done.7
  39.4 0.7 slice_bitcast_fusion
  40.2 4.3 %collective-permute-start.3 = (bf16[8,64,256]{2,1,0:T(8,128)(2,1)}, bf16[8,64,256]{2,1,0:T(8,128)(2,1)S(1)}, u32[]{:S(2)}, u32[]{:S(2)}) collective-permute-start(bf16[8,64,256]{2,1,0:T(8,128)(2,1)} %slice_bitcast_fusion), channel_id=1, source_target_pairs={{0,8},{1,9},{2,10},{3,11},{4,12},{5,13},{6,14},{7,15},{8,16},{9,17... | collective-permute-start | bytes 786440 | tf_op jit(solution)/shard_map/ppermute | solution.py:364
  44.5 0.7 slice_bitcast_fusion.2
  45.2 3.6 %collective-permute-start.4 = (bf16[4,64,256]{2,1,0:T(8,128)(2,1)}, bf16[4,64,256]{2,1,0:T(8,128)(2,1)S(1)}, u32[]{:S(2)}, u32[]{:S(2)}) collective-permute-start(bf16[4,64,256]{2,1,0:T(8,128)(2,1)} %slice_bitcast_fusion.2), channel_id=1, source_target_pairs={{0,1},{1,2},{2,3},{3,4},{4,5},{5,6},{6,7},{8,9},{9,10},{10,11},{11... | collective-permute-start | bytes 393224 | tf_op jit(solution)/shard_map/ppermute | solution.py:364
  48.8 3.1 %collective-permute-start.5 = (bf16[64,256]{1,0:T(8,128)(2,1)S(1)}, bf16[64,256]{1,0:T(8,128)(2,1)S(1)}, u32[]{:S(2)}, u32[]{:S(2)}) collective-permute-start(bf16[64,256]{1,0:T(8,128)(2,1)S(1)} %slice_bitcast_fusion.5), channel_id=1, source_target_pairs={{0,9},{1,10},{2,11},{3,12},{4,13},{5,14},{6,15},{8,17},{9,18},{10,... | collective-permute-start | bytes 98312 | tf_op jit(solution)/shard_map/ppermute | solution.py:364
  51.9 1.0 collective-permute-done.5.hc_ref
  52.9 0.0 collective-permute-done.4.hr_ref
  52.9 0.7 copy-done.4
  53.6 0.6 all-to-all-done.w_ref
  54.3 0.9 copy-done.5
  55.2 2.7 %second_layer.1 = (bf16[8,128,128]{2,1,0:T(8,128)(2,1)S(1)}, bf16[2,2,4,32,256]{4,3,2,1,0:T(8,128)(2,1)S(1)}, bf16[256,512]{1,0:T(8,128)(2,1)S(1)}) custom-call(bf16[4,8,64,256]{3,2,1,0:T(8,128)(2,1)S(1)} %get-tuple-element.25.h_ref, bf16[8,64,256]{2,1,0:T(8,128)(2,1)S(1)} %copy-done.5, bf16[4,64,256]{2,1,0:T(8,128)(2,1)S(1)} %collective-permute-done.4.hr_ref, ...), custom_call_target="tpu_custom_call" | custom-call | flops 1073741824 | bytes 4194304 | tf_op jit(solution)/shard_map/second_layer/pallas_call | solution.py:187
  57.9 2.3 %collective-permute-start.6 = (bf16[2,4,32,256]{3,2,1,0:T(8,128)(2,1)S(1)}, bf16[2,4,32,256]{3,2,1,0:T(8,128)(2,1)S(1)}, u32[]{:S(2)}, u32[]{:S(2)}) collective-permute-start(bf16[2,4,32,256]{3,2,1,0:T(8,128)(2,1)S(1)} %slice_bitcast_fusion.1), channel_id=1, source_target_pairs={{8,0},{9,1},{10,2},{11,3},{12,4},{13,5},{14,6},{15,7},{16,8},{17,9... | collective-permute-start | bytes 393224 | tf_op jit(solution)/shard_map/ppermute | solution.py:364
  60.2 1.3 collective-permute-start.8
  61.5 1.3 collective-permute-start.7
  62.9 0.0 copy-start.6
  62.9 0.9 copy-done.6
  63.8 1.2 second_kernel_grad.1
  65.0 2.0 %collective-permute-done.8.dc_ref = bf16[2,32,256]{2,1,0:T(8,128)(2,1)S(1)} collective-permute-done((bf16[2,32,256]{2,1,0:T(8,128)(2,1)S(1)}, bf16[2,32,256]{2,1,0:T(8,128)(2,1)S(1)}, u32[]{:S(2)}, u32[]{:S(2)}) %collective-permute-start.8) | collective-permute-done | bytes 32800 | tf_op jit(solution)/shard_map/ppermute | solution.py:364
  67.0 0.6 collective-permute-done.7.dr_ref
  67.6 0.0 collective-permute-done.6.dd_ref
  67.6 0.3 collective-permute-start.9
  67.9 1.4 back_one.1.d_ref
  69.4 4.4 %first_kernel_grad.1 = (bf16[8,8,16,128]{3,2,1,0:T(8,128)(2,1)S(1)}, bf16[8,8,16,128]{3,2,1,0:T(8,128)(2,1)S(1)}) custom-call(s32[1]{0:T(128)} %bitcast.30.core_ref, bf16[4,8,64,256]{3,2,1,0:T(8,128)(2,1)S(1)} %back_one.1.d_ref, bf16[8,2,8,3,64,128]{5,4,3,2,1,0:T(8,128)(2,1)S(1)} %bitcast.69, bf16[17,3,64,128]{3,2,1,0:T(8,128)(2,1)S(1)} %copy-done.8, ...), custom_call_target="tpu_custom_call" | custom-call | flops 4294967296 | bytes 9437184 | tf_op jit(solution)/shard_map/first_kernel_grad/pallas_call | solution.py:321
  73.8 0.6 collective-permute-start.10
  74.4 1.2 collective-permute-done.10
  75.5 0.1 add_convert_fusion.1
  75.6 0.4 add_convert_fusion
  76.0 0.1 pad_maximum_fusion.1
  76.2 35.4 %all_to_all.20 = bf16[64,80,128]{2,1,0:T(8,128)(2,1)S(1)} all-to-all(bf16[64,80,128]{2,1,0:T(8,128)(2,1)S(1)} %bitcast.71), channel_id=1, replica_groups=mesh['y_lo'=2,'z'=4,'core'=2,'y_hi'=2,'x'=4] {'y_lo','z','y_hi','x'}, dimensions={0} | all-to-all | bytes 2621440 | tf_op jit(solution)/shard_map/all_to_all | solution.py:339
  111.5 0.2 reduce_sum.12
  111.7 0.7 pad_maximum_fusion.3
  112.5 4.4 %all-to-all-start.2 = ((bf16[8,144,128]{2,1,0:T(8,128)(2,1)}), bf16[8,144,128]{2,1,0:T(8,128)(2,1)S(1)}, u32[]{:S(2)}, u32[]{:S(2)}) async-start(bf16[8,144,128]{2,1,0:T(8,128)(2,1)} %pad_maximum_fusion.3), calls=%async_computation.2 | async-start | bytes 589824 | tf_op jit(solution)/shard_map/all_to_all | solution.py:339
  116.8 8.2 %all-to-all-done.2 = bf16[8,144,128]{2,1,0:T(8,128)(2,1)S(1)} async-done(((bf16[8,144,128]{2,1,0:T(8,128)(2,1)}), bf16[8,144,128]{2,1,0:T(8,128)(2,1)S(1)}, u32[]{:S(2)}, u32[]{:S(2)}) %all-to-all-start.2) | async-done | bytes 294944 | tf_op jit(solution)/shard_map/all_to_all | solution.py:339
  125.0 1.0 broadcast_in_dim.22
  126.1 5.7 %all-to-all-start.3 = ((bf16[16,192,128]{2,1,0:T(8,128)(2,1)}), bf16[16,192,128]{2,1,0:T(8,128)(2,1)S(1)}, u32[]{:S(2)}, u32[]{:S(2)}) async-start(bf16[16,192,128]{2,1,0:T(8,128)(2,1)} %broadcast_in_dim.22), calls=%async_computation.3 | async-start | bytes 1572864 | tf_op jit(solution)/shard_map/all_to_all | solution.py:339
  131.8 0.2 copy.32
  132.0 0.8 reshape.78
  132.8 12.1 %all-to-all-done.3 = bf16[16,192,128]{2,1,0:T(8,128)(2,1)S(1)} async-done(((bf16[16,192,128]{2,1,0:T(8,128)(2,1)}), bf16[16,192,128]{2,1,0:T(8,128)(2,1)S(1)}, u32[]{:S(2)}, u32[]{:S(2)}) %all-to-all-start.3) | async-done | bytes 786464 | tf_op jit(solution)/shard_map/all_to_all | solution.py:339
  145.1 0.8 convert_bitcast_fusion
  145.9 1.0 convert.4
  (56 shorter events, 0.5 us)
Async XLA Ops:
  1.9 13.8 %copy-start.11 = (bf16[2,32,2,1024]{3,2,1,0:T(2,128)(2,1)S(1)}, bf16[2,32,2,1024]{3,2,1,0:T(2,128)(2,1)}, u32[]{:S(2)}) copy-start(bf16[2,32,2,1024]{3,2,1,0:T(2,128)(2,1)} %param.8) | copy-start | bytes 786436
  1.9 14.0 %copy-start.12 = (bf16[3,3,3,128,32]{3,4,2,1,0:T(8,128)(2,1)S(1)}, bf16[3,3,3,128,32]{3,4,2,1,0:T(8,128)(2,1)}, u32[]{:S(2)}) copy-start(bf16[3,3,3,128,32]{3,4,2,1,0:T(8,128)(2,1)} %param.7) | copy-start | bytes 663556
  2.2 15.9 %collective-permute-start = (bf16[16,128,128]{2,1,0:T(8,128)(2,1)S(1)}, bf16[16,128,128]{2,1,0:T(8,128)(2,1)S(1)}, u32[]{:S(2)}, u32[]{:S(2)}) collective-permute-start(bf16[16,128,128]{2,1,0:T(8,128)(2,1)S(1)} %constant_dynamic-update-slice_fusion), channel_id=1, source_target_pairs={{0,8},{1,9},{2,10},{3,11},{4,12},{5,13},{6,14},{7,15},{8,16},{9,17... | collective-permute-start | bytes 1572872 | tf_op jit(solution)/shard_map/ppermute | solution.py:364
  9.4 8.7 %collective-permute-start.1 = (bf16[8,128,128]{2,1,0:T(8,128)(2,1)S(1)}, bf16[8,128,128]{2,1,0:T(8,128)(2,1)S(1)}, u32[]{:S(2)}, u32[]{:S(2)}) collective-permute-start(bf16[8,128,128]{2,1,0:T(8,128)(2,1)S(1)} %bitcast.81), channel_id=1, source_target_pairs={{0,1},{1,2},{2,3},{3,4},{4,5},{5,6},{6,7},{8,9},{9,10},{10,11},{11... | collective-permute-start | bytes 786440 | tf_op jit(solution)/shard_map/ppermute | solution.py:364
  12.5 5.6 %collective-permute-start.2 = (bf16[1,128,128]{2,1,0:T(8,128)(2,1)S(1)}, bf16[1,128,128]{2,1,0:T(8,128)(2,1)S(1)}, u32[]{:S(2)}, u32[]{:S(2)}) collective-permute-start(bf16[1,128,128]{2,1,0:T(8,128)(2,1)S(1)} %bitcast.84), channel_id=1, source_target_pairs={{0,9},{1,10},{2,11},{3,12},{4,13},{5,14},{6,15},{8,17},{9,18},{10,... | collective-permute-start | bytes 98312 | tf_op jit(solution)/shard_map/ppermute | solution.py:364
  17.7 8.6 %copy-start.2 = (bf16[192,128]{1,0:T(8,128)(2,1)S(1)}, bf16[192,128]{1,0:T(8,128)(2,1)}, u32[]{:S(2)}) copy-start(bf16[192,128]{1,0:T(8,128)(2,1)} %constant.11.clone.sel_ref) | copy-start | bytes 147460
  18.1 36.1 %all-to-all-start = ((bf16[8,992,128]{2,1,0:T(8,128)(2,1)}), bf16[8,992,128]{2,1,0:T(8,128)(2,1)S(1)}, u32[]{:S(2)}, u32[]{:S(2)}) async-start(bf16[8,992,128]{2,1,0:T(8,128)(2,1)} %pad_maximum_fusion), calls=%async_computation | async-start | bytes 4063232 | tf_op jit(solution)/shard_map/all_to_all | solution.py:339
  26.3 2.2 %copy-start = (bf16[2,64,8,16,128]{4,3,2,1,0:T(8,128)(2,1)S(1)}, bf16[2,64,8,16,128]{4,3,2,1,0:T(8,128)(2,1)}, u32[]{:S(2)}) copy-start(bf16[2,64,8,16,128]{4,3,2,1,0:T(8,128)(2,1)} %x_ref.1) | copy-start | bytes 12582916
  28.5 5.5 %copy-start.3 = (bf16[3,3,3,64,128]{4,3,2,1,0:T(8,128)(2,1)S(1)}, bf16[3,3,3,64,128]{4,3,2,1,0:T(8,128)(2,1)}, u32[]{:S(2)}) copy-start(bf16[3,3,3,64,128]{4,3,2,1,0:T(8,128)(2,1)} %param.6) | copy-start | bytes 1327108
  33.9 4.7 %copy-start.1 = (bf16[8,2,8,3,64,128]{5,4,3,2,1,0:T(8,128)(2,1)}, bf16[8,2,8,3,64,128]{5,4,3,2,1,0:T(8,128)(2,1)S(1)}, u32[]{:S(2)}) copy-start(bf16[8,2,8,3,64,128]{5,4,3,2,1,0:T(8,128)(2,1)S(1)} %split_width.1.q_ref) | copy-start | bytes 18874372
  38.5 0.9 copy-start.7
  39.4 9.4 %copy-start.9 = (bf16[8,3,64,128]{3,2,1,0:T(8,128)(2,1)}, bf16[8,3,64,128]{3,2,1,0:T(8,128)(2,1)S(1)}, u32[]{:S(2)}) copy-start(bf16[8,3,64,128]{3,2,1,0:T(8,128)(2,1)S(1)} %get-tuple-element.38.qr_ref) | copy-start | bytes 1179652
  40.2 12.7 %collective-permute-start.3 = (bf16[8,64,256]{2,1,0:T(8,128)(2,1)}, bf16[8,64,256]{2,1,0:T(8,128)(2,1)S(1)}, u32[]{:S(2)}, u32[]{:S(2)}) collective-permute-start(bf16[8,64,256]{2,1,0:T(8,128)(2,1)} %slice_bitcast_fusion), channel_id=1, source_target_pairs={{0,8},{1,9},{2,10},{3,11},{4,12},{5,13},{6,14},{7,15},{8,16},{9,17... | collective-permute-start | bytes 786440 | tf_op jit(solution)/shard_map/ppermute | solution.py:364
  45.2 7.8 %collective-permute-start.4 = (bf16[4,64,256]{2,1,0:T(8,128)(2,1)}, bf16[4,64,256]{2,1,0:T(8,128)(2,1)S(1)}, u32[]{:S(2)}, u32[]{:S(2)}) collective-permute-start(bf16[4,64,256]{2,1,0:T(8,128)(2,1)} %slice_bitcast_fusion.2), channel_id=1, source_target_pairs={{0,1},{1,2},{2,3},{3,4},{4,5},{5,6},{6,7},{8,9},{9,10},{10,11},{11... | collective-permute-start | bytes 393224 | tf_op jit(solution)/shard_map/ppermute | solution.py:364
  48.8 4.1 %collective-permute-start.5 = (bf16[64,256]{1,0:T(8,128)(2,1)S(1)}, bf16[64,256]{1,0:T(8,128)(2,1)S(1)}, u32[]{:S(2)}, u32[]{:S(2)}) collective-permute-start(bf16[64,256]{1,0:T(8,128)(2,1)S(1)} %slice_bitcast_fusion.5), channel_id=1, source_target_pairs={{0,9},{1,10},{2,11},{3,12},{4,13},{5,14},{6,15},{8,17},{9,18},{10,... | collective-permute-start | bytes 98312 | tf_op jit(solution)/shard_map/ppermute | solution.py:364
  52.9 0.7 copy-start.4
  54.3 1.0 copy-start.5
  55.2 14.1 %slice-start = ((s8[6291456]{0:T(1024)(128)(4,1)}), s8[4194304]{0:T(1024)(128)(4,1)S(1)}, s32[]{:S(2)}) async-start(s8[6291456]{0:T(1024)(128)(4,1)} %bitcast.68), calls=%async_computation.4 | async-start | bytes 8388608
  57.9 9.7 %collective-permute-start.6 = (bf16[2,4,32,256]{3,2,1,0:T(8,128)(2,1)S(1)}, bf16[2,4,32,256]{3,2,1,0:T(8,128)(2,1)S(1)}, u32[]{:S(2)}, u32[]{:S(2)}) collective-permute-start(bf16[2,4,32,256]{3,2,1,0:T(8,128)(2,1)S(1)} %slice_bitcast_fusion.1), channel_id=1, source_target_pairs={{8,0},{9,1},{10,2},{11,3},{12,4},{13,5},{14,6},{15,7},{16,8},{17,9... | collective-permute-start | bytes 393224 | tf_op jit(solution)/shard_map/ppermute | solution.py:364
  60.2 6.8 %collective-permute-start.8 = (bf16[2,32,256]{2,1,0:T(8,128)(2,1)S(1)}, bf16[2,32,256]{2,1,0:T(8,128)(2,1)S(1)}, u32[]{:S(2)}, u32[]{:S(2)}) collective-permute-start(bf16[2,32,256]{2,1,0:T(8,128)(2,1)S(1)} %slice_bitcast_fusion.4), channel_id=1, source_target_pairs={{9,0},{10,1},{11,2},{12,3},{13,4},{14,5},{15,6},{17,8},{18,9},{19,... | collective-permute-start | bytes 98312 | tf_op jit(solution)/shard_map/ppermute | solution.py:364
  61.5 6.1 %collective-permute-start.7 = (bf16[2,2,32,256]{3,2,1,0:T(8,128)(2,1)S(1)}, bf16[2,2,32,256]{3,2,1,0:T(8,128)(2,1)S(1)}, u32[]{:S(2)}, u32[]{:S(2)}) collective-permute-start(bf16[2,2,32,256]{3,2,1,0:T(8,128)(2,1)S(1)} %slice_bitcast_fusion.3), channel_id=1, source_target_pairs={{1,0},{2,1},{3,2},{4,3},{5,4},{6,5},{7,6},{9,8},{10,9},{11,10},{12... | collective-permute-start | bytes 196616 | tf_op jit(solution)/shard_map/ppermute | solution.py:364
  62.9 1.0 copy-start.6
  63.8 5.5 %slice-start.1 = ((s8[6291456]{0:T(1024)(128)(4,1)}), s8[2097152]{0:T(1024)(128)(4,1)S(1)}, s32[]{:S(2)}) async-start(s8[6291456]{0:T(1024)(128)(4,1)} %bitcast.68), calls=%async_computation.5 | async-start | bytes 4194304
  67.6 1.7 %copy-start.8 = (bf16[17,3,64,128]{3,2,1,0:T(8,128)(2,1)S(1)}, bf16[17,3,64,128]{3,2,1,0:T(8,128)(2,1)}, u32[]{:S(2)}) copy-start(bf16[17,3,64,128]{3,2,1,0:T(8,128)(2,1)} %copy-done.7) | copy-start | bytes 2506756
  67.6 1.7 %copy-start.10 = (bf16[8,3,64,128]{3,2,1,0:T(8,128)(2,1)S(1)}, bf16[8,3,64,128]{3,2,1,0:T(8,128)(2,1)}, u32[]{:S(2)}) copy-start(bf16[8,3,64,128]{3,2,1,0:T(8,128)(2,1)} %copy-done.9) | copy-start | bytes 1179652
  67.6 8.0 %collective-permute-start.9 = (bf16[8,8,64,128]{3,2,1,0:T(8,128)(2,1)S(1)}, bf16[8,8,64,128]{3,2,1,0:T(8,128)(2,1)S(1)}, u32[]{:S(2)}, u32[]{:S(2)}) collective-permute-start(bf16[8,8,64,128]{3,2,1,0:T(8,128)(2,1)S(1)} %get-tuple-element.33), channel_id=1, source_target_pairs={{0,8},{8,0},{1,9},{9,1},{2,10},{10,2},{3,11},{11,3},{4,12},{12,4},... | collective-permute-start | bytes 3145736 | tf_op jit(solution)/shard_map/ppermute | solution.py:352
  73.8 1.7 %collective-permute-start.10 = (bf16[8,8,16,128]{3,2,1,0:T(8,128)(2,1)S(1)}, bf16[8,8,16,128]{3,2,1,0:T(8,128)(2,1)S(1)}, u32[]{:S(2)}, u32[]{:S(2)}) collective-permute-start(bf16[8,8,16,128]{3,2,1,0:T(8,128)(2,1)S(1)} %get-tuple-element.40), channel_id=1, source_target_pairs={{0,8},{8,0},{1,9},{9,1},{2,10},{10,2},{3,11},{11,3},{4,12},{12,4},... | collective-permute-start | bytes 786440 | tf_op jit(solution)/shard_map/ppermute | solution.py:352
  112.5 12.6 %all-to-all-start.2 = ((bf16[8,144,128]{2,1,0:T(8,128)(2,1)}), bf16[8,144,128]{2,1,0:T(8,128)(2,1)S(1)}, u32[]{:S(2)}, u32[]{:S(2)}) async-start(bf16[8,144,128]{2,1,0:T(8,128)(2,1)} %pad_maximum_fusion.3), calls=%async_computation.2 | async-start | bytes 589824 | tf_op jit(solution)/shard_map/all_to_all | solution.py:339
  126.1 18.8 %all-to-all-start.3 = ((bf16[16,192,128]{2,1,0:T(8,128)(2,1)}), bf16[16,192,128]{2,1,0:T(8,128)(2,1)S(1)}, u32[]{:S(2)}, u32[]{:S(2)}) async-start(bf16[16,192,128]{2,1,0:T(8,128)(2,1)} %broadcast_in_dim.22), calls=%async_computation.3 | async-start | bytes 1572864 | tf_op jit(solution)/shard_map/all_to_all | solution.py:339

commit v3 on v2

v3 whole, which is shorter than its diff:
```python
import jax
import jax.numpy as jnp
import numpy as np
from jax import lax
from jax.experimental import pallas as pl
from jax.experimental.pallas import tpu as pltpu
from jax.sharding import PartitionSpec as P

BF = jnp.bfloat16
F32 = jnp.float32
MIB = 1 << 20
LANES = (((1,), (1,)), ((), ()))
PLAIN = (((1,), (0,)), ((), ()))


def params(mib):
    return pltpu.CompilerParams(vmem_limit_bytes=mib * MIB)


def cost(gigaflops, mib):
    return pl.CostEstimate(flops=gigaflops << 30, bytes_accessed=mib * MIB, transcendentals=0)


def vmem(count):
    return [pl.BlockSpec(memory_space=pltpu.VMEM)] * count


SCALAR = pl.BlockSpec(memory_space=pltpu.SMEM)


def dot(a, b, dims=PLAIN):
    return lax.dot_general(a, b, dims, preferred_element_type=F32)


def selection():
    column = 2 * (np.arange(64) % 32) + np.arange(64) // 32
    wanted = np.concatenate([2 * column[:32] - 1, 2 * column, 2 * column + 1])
    return (wanted[:, None] == np.arange(128)[None, :]).astype(np.float32)


def spread(sel, rows):
    return dot(sel, rows, LANES).astype(BF)


PITCH = 24


def slab_rows(x_ref, d, wide):
    wide[:, 0:16, :] = x_ref[:, :, d].reshape(128, 16, 128).astype(F32)


def row(wide, h):
    return wide.reshape(128 * PITCH, 128)[pl.ds(h, 128, stride=PITCH), :].astype(BF)


def rims_kernel(x_ref, side_ref, last_ref, wide):
    for d in range(8):
        slab_rows(x_ref, d, wide)
        side_ref[d] = row(wide, 15)
    for k in range(8):
        last_ref[k] = row(wide, 2 * k + 1)
        last_ref[8 + k] = row(wide, 2 * k)


def rims_of(inputs):
    return pl.pallas_call(
        rims_kernel,
        in_specs=vmem(1),
        out_specs=vmem(2),
        out_shape=(jax.ShapeDtypeStruct((8, 128, 128), BF), jax.ShapeDtypeStruct((16, 128, 128), BF)),
        scratch_shapes=[pltpu.VMEM((128, PITCH, 128), F32)],
        compiler_params=params(16),
        cost_estimate=cost(0, 6),
        name="input_rims",
    )(inputs)


def mix_kernel(core_ref, own_ref, parts_ref, out_ref):
    even = core_ref[0] == 0
    for k in range(27):
        low, high = own_ref[32 * k : 32 * k + 16], own_ref[32 * k + 16 : 32 * k + 32]
        half = jnp.where(even, low.astype(F32), high.astype(F32)).astype(BF)
        for g in range(8):
            out_ref[g, 16 * k : 16 * k + 16] = half
    for g in range(8):
        out_ref[g, 432:560] = parts_ref[g]


def mix(core, own, parts):
    return pl.pallas_call(
        mix_kernel,
        in_specs=[SCALAR] + vmem(2),
        out_specs=vmem(1)[0],
        out_shape=jax.ShapeDtypeStruct((8, 560, 128), BF),
        compiler_params=params(16),
        cost_estimate=cost(0, 3),
        name="weights_and_cotangent",
    )(core, own, parts)


def field_tile(q_ref, qd_ref, qr_ref, a, b, t, u, v):
    d = 2 * a + t - 1
    if d < 0:
        ref = qd_ref.at[(b, 9 + b, b + 1)[u]]
    elif u == 0:
        ref = q_ref.at[d, 1, b - 1] if b else qr_ref.at[d]
    else:
        ref = q_ref.at[d, u - 1, b]
    if v == 0:
        return jnp.concatenate([ref[0:32, :], ref[96:128, :]], 0)
    return ref[64 * v - 32 : 64 * v + 32, :]


def field_rows(q_ref, qd_ref, qr_ref, a, t, u, v):
    return jnp.concatenate([field_tile(q_ref, qd_ref, qr_ref, a, b, t, u, v) for b in range(8)], 0)


def first_kernel(
    x_ref, xd_ref, xr_ref, xc_ref, sel_ref, k_ref,
    h_ref, q_out, qd_ref, qr_ref, last_ref, side_ref, end_ref,
    x_slabs, q_ref, w_ref, wide, came, went,
):
    def load(d):
        return pltpu.make_async_copy(x_ref.at[:, :, d], x_slabs.at[d], came.at[d])

    def store(d):
        return pltpu.make_async_copy(q_ref.at[d], q_out.at[d], went.at[d])

    for d in range(8):
        load(d).start()
    sel = sel_ref[...]
    qd_ref[0] = spread(sel, xc_ref[...])
    for k in range(16):
        qd_ref[k + 1] = spread(sel, xd_ref[k])
    for k in range(8):
        qr_ref[k] = spread(sel, xr_ref[k])
    w_ref[...] = jnp.zeros_like(w_ref)
    for k in range(27):
        w_ref[k * 128 : k * 128 + 64, 0:128] = k_ref[k]
        w_ref[k * 128 + 64 : k * 128 + 128, 128:256] = k_ref[k]

    @pl.loop(0, 8)
    def slab(d):
        load(d).wait()
        wide[:, 0:16, :] = x_slabs[d].reshape(128, 16, 128).astype(F32)
        for k in range(8):
            both = spread(sel, jnp.concatenate([row(wide, 2 * k), row(wide, 2 * k + 1)], 0))
            for p in range(2):
                q_ref[d, p, k] = both[:, 128 * p : 128 * p + 128]
        store(d).start()

    for a in range(4):
        taps = [field_rows(q_ref, qd_ref, qr_ref, a, t, u, v) for t in range(3) for u in range(3) for v in range(3)]
        pre = dot(jnp.concatenate(taps, 1), w_ref[...])
        out = jnp.where(pre > 0, pre, 0.3 * pre).astype(BF).reshape(8, 64, 256)
        h_ref[a] = out
        side_ref[a] = out[7]
        if a == 3:
            last_ref[...] = out
            end_ref[...] = out[7]
    for d in range(8):
        store(d).wait()


def first(x, xd, xr, xc, sel, kernel):
    anywhere = pl.BlockSpec(memory_space=pl.ANY)
    return pl.pallas_call(
        first_kernel,
        in_specs=[anywhere] + vmem(5),
        out_specs=vmem(1) + [anywhere] + vmem(5),
        out_shape=(
            jax.ShapeDtypeStruct((4, 8, 64, 256), BF),
            jax.ShapeDtypeStruct((8, 2, 8, 160, 128), BF),
            jax.ShapeDtypeStruct((17, 160, 128), BF),
            jax.ShapeDtypeStruct((8, 160, 128), BF),
            jax.ShapeDtypeStruct((8, 64, 256), BF),
            jax.ShapeDtypeStruct((4, 64, 256), BF),
            jax.ShapeDtypeStruct((64, 256), BF),
        ),
        scratch_shapes=[
            pltpu.VMEM((8, 2, 64, 16, 128), BF),
            pltpu.VMEM((8, 2, 8, 160, 128), BF),
            pltpu.VMEM((27 * 128, 256), BF),
            pltpu.VMEM((128, PITCH, 128), F32),
            pltpu.SemaphoreType.DMA((8,)),
            pltpu.SemaphoreType.DMA((8,)),
        ],
        compiler_params=params(56),
        cost_estimate=cost(6, 20),
        name="first_layer",
    )(x, xd, xr, xc, sel, kernel)


def hidden_part(h_ref, hd_ref, hr_ref, hc_ref, a, b):
    if a < 0 and b < 0:
        return hc_ref
    if a < 0:
        return hd_ref.at[b]
    if b < 0:
        return hr_ref.at[a]
    return h_ref.at[a, b]


def shift_rows(value, by):
    wide = pltpu.roll(value.astype(F32), by % 32, 0)
    row = lax.broadcasted_iota(jnp.int32, wide.shape, 0)
    keep = row >= by if by > 0 else row < 32 + by
    return jnp.where(keep, wide, 0.0).astype(BF)


def hidden_shifts(parts, hs_ref):
    for a in range(-1, 4):
        for b in range(-1, 8):
            hs_ref[a + 1, b + 1] = shift_rows(hidden_part(*parts, a, b)[32:64, :], 1)


def hidden_rows(parts, hs_ref, t, u, v):
    pieces = []
    for n in range(2):
        for a in range(2):
            for b in range(4):
                i, j = 2 * a + t - 1, 2 * b + u - 1
                cut = slice(128 * n, 128 * n + 128)
                if v == 0:
                    pieces.append(hs_ref[i + 1, j + 1, :, cut])
                else:
                    pieces.append(hidden_part(*parts, i, j)[32 * (v - 1) : 32 * v, cut])
    return jnp.concatenate(pieces, 0)


WEIGHT = pltpu.VMEM((8, 864, 128), BF)


def whole_weight(core_ref, mine_ref, other_ref, w_ref):
    even = core_ref[0] == 0
    for k in range(27):
        mine, other = (ref[:, 16 * k : 16 * k + 16, :].astype(F32) for ref in (mine_ref, other_ref))
        w_ref[:, 32 * k : 32 * k + 16, :] = jnp.where(even, mine, other).astype(BF)
        w_ref[:, 32 * k + 16 : 32 * k + 32, :] = jnp.where(even, other, mine).astype(BF)


def tap_weight(w_ref, k):
    return w_ref[:, 32 * k : 32 * k + 32, :].reshape(256, 128)


def eye(size):
    rows = lax.broadcasted_iota(jnp.int32, (size, size), 0)
    return (rows == lax.broadcasted_iota(jnp.int32, (size, size), 1)).astype(F32).astype(BF)


def second_kernel(
    core_ref, h_ref, hd_ref, hr_ref, hc_ref, m_ref, o_ref, act_ref, delta_ref, turned_ref, last_ref, side_ref, w_ref, hs_ref
):
    parts = (h_ref, hd_ref, hr_ref, hc_ref)
    hidden_shifts(parts, hs_ref)
    whole_weight(core_ref, m_ref, o_ref, w_ref)
    keys = [(t, u, v) for t in range(3) for u in range(3) for v in range(3)]
    left = jnp.concatenate([hidden_rows(parts, hs_ref, *key) for key in keys], 1)
    right = jnp.concatenate([tap_weight(w_ref, k) for k in range(27)], 1)
    pre = dot(left, right, LANES)
    act = jnp.where(pre > 0, pre, 0.3 * pre).astype(BF)
    slope = jnp.where(pre > 0, 1.0, 0.3).astype(F32)
    small, large = eye(128), eye(256)
    for n in range(2):
        for a in range(2):
            at = 256 * n + 128 * a
            rows = slice(at, at + 128)
            some = slice(64 * a + 32 * n, 32 + 64 * a + 32 * n)
            act_ref[:, some, :] = dot(large, act[rows], LANES).astype(BF).reshape(8, 32, 128)
            some = slice(432 + 64 * a + 32 * n, 464 + 64 * a + 32 * n)
            came = dot(small, m_ref[:, some, :].reshape(256, 128), LANES)
            delta = (came * slope[rows]).astype(BF)
            delta_ref[n, a] = delta.reshape(4, 32, 256)
            side_ref[n, a] = delta[0:32]
            if a == 0:
                last_ref[n] = delta.reshape(4, 32, 256)
            turned_ref[:, rows] = dot(large, delta, LANES).astype(BF)


def second(core, h, hd, hr, hc, mine, other):
    return pl.pallas_call(
        second_kernel,
        in_specs=[SCALAR] + vmem(6),
        out_specs=vmem(5),
        out_shape=(
            jax.ShapeDtypeStruct((8, 128, 128), BF),
            jax.ShapeDtypeStruct((2, 2, 4, 32, 256), BF),
            jax.ShapeDtypeStruct((256, 512), BF),
            jax.ShapeDtypeStruct((2, 4, 32, 256), BF),
            jax.ShapeDtypeStruct((2, 2, 32, 256), BF),
        ),
        scratch_shapes=[WEIGHT, pltpu.VMEM((5, 9, 32, 256), BF)],
        compiler_params=params(40),
        cost_estimate=cost(1, 4),
        name="second_layer",
    )(core, h, hd, hr, hc, mine, other)


def second_grad_kernel(core_ref, h_ref, hd_ref, hr_ref, hc_ref, turned_ref, keep_ref, send_ref, hs_ref):
    parts = (h_ref, hd_ref, hr_ref, hc_ref)
    hidden_shifts(parts, hs_ref)
    turned = turned_ref[...]
    even = core_ref[0] == 0
    keys = [(t, u, v) for t in range(3) for u in range(3) for v in range(3)]
    for k in range(0, 27, 2):
        some = keys[k : k + 2]
        right = jnp.concatenate([hidden_rows(parts, hs_ref, *key) for key in some], 1)
        both = dot(turned, right)
        for p in range(len(some)):
            one = both[:, 128 * p : 128 * p + 128].reshape(8, 2, 16, 128)
            low, high = one[:, 0], one[:, 1]
            spot = ((k + p) // 4, slice(None), slice(16 * ((k + p) % 4), 16 * ((k + p) % 4) + 16))
            keep_ref[spot] = jnp.where(even, low, high).astype(BF)
            send_ref[spot] = jnp.where(even, high, low).astype(BF)
    for ref in (keep_ref, send_ref):
        ref[6, :, 48:64] = jnp.zeros((8, 16, 128), BF)
        ref[7] = jnp.zeros((8, 64, 128), BF)


def second_grad(core, h, hd, hr, hc, turned):
    return pl.pallas_call(
        second_grad_kernel,
        in_specs=[SCALAR] + vmem(5),
        out_specs=vmem(2),
        out_shape=(jax.ShapeDtypeStruct((8, 8, 64, 128), BF),) * 2,
        scratch_shapes=[pltpu.VMEM((5, 9, 32, 256), BF)],
        compiler_params=params(40),
        cost_estimate=cost(1, 4),
        name="second_kernel_grad",
    )(core, h, hd, hr, hc, turned)


def delta_part(d_ref, dd_ref, dr_ref, n, a, b):
    if a > 1:
        return dd_ref.at[n, b]
    if b > 3:
        return dr_ref.at[n, a]
    return d_ref.at[n, a, b]


INNER = [(a, b) for a in range(3) for b in range(7) if (a, b) != (2, 6)]
OUTER = [(3, b) for b in range(8)] + [(0, 7), (1, 7), (2, 7), (2, 6)]


def back_rows(parts, ds_ref, w_ref, h_ref, d_ref, places):
    nothing = jnp.zeros((256, 128), BF)
    choice = (((1, 0),), ((2, 0), (0, 1)))
    for pa in range(2):
        for pb in range(2):
            some = [(a // 2, b // 2) for a, b in places if (a % 2, b % 2) == (pa, pb)]
            left, right = [], []
            for t, i in choice[pa]:
                for u, j in choice[pb]:
                    spots = [(n, a + i, b + j) for n in range(2) for a, b in some]
                    left.append(jnp.concatenate([delta_part(*parts, *spot)[...] for spot in spots], 0))
                    left.append(jnp.concatenate([ds_ref[spot] for spot in spots], 0))
                    k = 9 * t + 3 * u
                    right.append(jnp.concatenate([tap_weight(w_ref, k + 1), tap_weight(w_ref, k + 2)], 1))
                    right.append(jnp.concatenate([nothing, tap_weight(w_ref, k)], 1))
            back = dot(jnp.concatenate(left, 1), jnp.concatenate(right, 0))
            for n in range(2):
                for x, (a, b) in enumerate(some):
                    at = 32 * (n * len(some) + x)
                    place = 2 * a + pa, 2 * b + pb
                    for pc in range(2):
                        rows, cut = slice(32 * pc, 32 * pc + 32), slice(128 * n, 128 * n + 128)
                        slope = jnp.where(h_ref[(*place, rows, cut)].astype(F32) > 0, 1.0, 0.3)
                        value = back[at : at + 32, 128 * pc : 128 * pc + 128]
                        d_ref[places.index(place), rows, cut] = (value * slope).astype(BF)


def grad_rows(d_ref, fields, places):
    turned = dot(eye(256), d_ref[...].reshape(64 * len(places), 256), LANES).astype(BF)
    keys = [(t, u, v) for t in range(3) for u in range(3) for v in range(3)]
    lane = lax.broadcasted_iota(jnp.int32, (128, 128), 1)
    for k in range(0, 27, 2):
        some = keys[k : k + 2]
        right = [jnp.concatenate([field_tile(*fields, *place, *key) for place in places], 0) for key in some]
        both = dot(turned, jnp.concatenate(right, 1))
        one = both[0:128, 0:128] + pltpu.roll(both[128:256, 0:128], 64, 1)
        if len(some) == 2:
            two = both[128:256, 128:256] + pltpu.roll(both[0:128, 128:256], 64, 1)
        else:
            two = jnp.zeros_like(one)
        yield k, jnp.where(lane < 64, one, two).T


def inner_kernel(core_ref, d_ref, m_ref, o_ref, h_ref, q_ref, qd_ref, qr_ref, out_ref, w_ref, ds_ref, one_ref):
    whole_weight(core_ref, m_ref, o_ref, w_ref)
    for n in range(2):
        for a in range(2):
            for b in range(4):
                ds_ref[n, a, b] = shift_rows(d_ref[n, a, b], -1)
    parts = (d_ref, None, None)
    back_rows(parts, ds_ref, w_ref, h_ref, one_ref, INNER)
    for k, rows in grad_rows(one_ref, (q_ref, qd_ref, qr_ref), INNER):
        out_ref[k // 2] = rows


def inner(core, d, mine, other, h, q, qd, qr):
    return pl.pallas_call(
        inner_kernel,
        in_specs=[SCALAR] + vmem(7),
        out_specs=vmem(1)[0],
        out_shape=jax.ShapeDtypeStruct((14, 128, 128), F32),
        scratch_shapes=[WEIGHT, pltpu.VMEM((2, 2, 4, 32, 256), BF), pltpu.VMEM((len(INNER), 64, 256), BF)],
        compiler_params=params(40),
        cost_estimate=cost(4, 9),
        name="first_kernel_grad_inner",
    )(core, d, mine, other, h, q, qd, qr)


def outer_kernel(
    core_ref, d_ref, dd_ref, dr_ref, m_ref, o_ref, h_ref, q_ref, qd_ref, qr_ref, sum_ref,
    keep_ref, send_ref, w_ref, ds_ref, one_ref,
):
    whole_weight(core_ref, m_ref, o_ref, w_ref)
    parts = (d_ref, dd_ref, dr_ref)
    for n in range(2):
        for a in range(3):
            for b in range(5):
                ds_ref[n, a, b] = shift_rows(delta_part(*parts, n, a, b)[...], -1)
    back_rows(parts, ds_ref, w_ref, h_ref, one_ref, OUTER)
    even = core_ref[0] == 0
    for k, rows in grad_rows(one_ref, (q_ref, qd_ref, qr_ref), OUTER):
        rows = rows + sum_ref[k // 2]
        for j in range(4):
            low, high = rows[32 * j : 32 * j + 16], rows[32 * j + 16 : 32 * j + 32]
            spot = (k // 4, 2 * (k % 4) + j)
            keep_ref[spot] = jnp.where(even, low, high).astype(BF)
            send_ref[spot] = jnp.where(even, high, low).astype(BF)
    for ref in (keep_ref, send_ref):
        ref[7] = jnp.zeros((8, 16, 128), BF)


def outer(core, d, dd, dr, mine, other, h, q, qd, qr, partial):
    return pl.pallas_call(
        outer_kernel,
        in_specs=[SCALAR] + vmem(10),
        out_specs=vmem(2),
        out_shape=(jax.ShapeDtypeStruct((8, 8, 16, 128), BF),) * 2,
        scratch_shapes=[WEIGHT, pltpu.VMEM((2, 3, 5, 32, 256), BF), pltpu.VMEM((len(OUTER), 64, 256), BF)],
        compiler_params=params(40),
        cost_estimate=cost(2, 9),
        name="first_kernel_grad",
    )(core, d, dd, dr, mine, other, h, q, qd, qr, partial)


SPACE = ("y_lo", "z", "core")
FILT = ("y_hi", "x")
SLABS = ("y_lo", "z")
CHIPS = ("y_lo", "z", "y_hi", "x")


def exchange(value, axes):
    return lax.all_to_all(value, axes, 0, 0, tiled=True)


def everywhere(value, axes):
    devices = lax.axis_size(axes)
    return exchange(jnp.broadcast_to(value[None], (devices,) + value.shape), axes)


def total(pieces):
    return jnp.sum(pieces.astype(F32), 0).astype(BF)


def paired(keep, send):
    came = lax.ppermute(send, "core", [(0, 1), (1, 0)])
    return (keep.astype(F32) + came.astype(F32)).astype(BF)


def shifted(value, depth, height):
    deep, high = lax.axis_size(SPACE), lax.axis_size(FILT)
    pairs = [
        (i * high + j, (i + depth) * high + j + height)
        for i in range(deep)
        for j in range(high)
        if 0 <= i + depth < deep and 0 <= j + height < high
    ]
    return lax.ppermute(value, SPACE + FILT, pairs)


def body(inputs, kernel_one, kernel_two, cotangent):
    core = lax.axis_index("core").reshape(1)
    sel = jnp.asarray(selection(), BF)
    own = jnp.transpose(kernel_two, (0, 1, 2, 4, 3)).reshape(864, 128)
    parts = jnp.transpose(cotangent.reshape(2, 32, 2, 8, 128), (3, 2, 0, 1, 4)).reshape(8, 128, 128)
    mixed = mix(core, own, parts)

    side, last = rims_of(inputs)
    xr = shifted(side, 0, 1)
    xd = shifted(last, 1, 0)
    xc = shifted(last[7], 1, 1)
    mixed, xr, xd, xc = lax.optimization_barrier((mixed, xr, xd, xc))
    mixed = exchange(mixed, FILT)
    h, q, qd, qr, last, side, end = first(inputs, xd, xr, xc, sel, kernel_one.reshape(27, 64, 128))
    mixed, end = lax.optimization_barrier((mixed, end))
    other = lax.ppermute(mixed, "core", [(0, 1), (1, 0)])
    hr = shifted(side, 0, 1)
    hd = shifted(last, 1, 0)
    hc = shifted(end, 1, 1)
    act, delta, turned, last, side = second(core, h, hd, hr, hc, mixed, other)
    dr = shifted(side, 0, -1)
    partial = inner(core, delta, mixed, other, h, q, qd, qr)
    dr, partial = lax.optimization_barrier((dr, partial))
    dd = shifted(jnp.concatenate([last, dr[:, :1]], 1), -1, 0)
    two = second_grad(core, h, hd, hr, hc, turned)
    two, dd = lax.optimization_barrier((two, dd))
    two = paired(*two)
    one = paired(*outer(core, delta, dd, dr, mixed, other, h, q, qd, qr, partial))

    both = jnp.concatenate([two, one], 2).reshape(64, 80, 128)
    both = total(exchange(both, CHIPS))
    one = jnp.broadcast_to(both[None, 64:], (8, 16, 128))
    came = exchange(jnp.concatenate([act, one], 1), FILT)
    mine = everywhere(jnp.concatenate([both[:64], came[:, 128:].reshape(128, 128)], 0), SLABS)
    other = lax.ppermute(mine, "core", [(0, 1), (1, 0)])
    even = lax.axis_index("core") == 0
    full = jnp.stack([jnp.where(even, mine, other), jnp.where(even, other, mine)], 1)
    two = full[:, :, :64].reshape(8, 2, 4, 16, 128)
    two = jnp.transpose(two, (0, 2, 1, 3, 4)).reshape(1024, 128)[:864].reshape(3, 3, 3, 32, 128)
    grad_two = jnp.transpose(two, (0, 1, 2, 4, 3)).astype(F32)
    one = full[:, :, 64:].reshape(8, 2, 8, 16, 128)
    one = jnp.transpose(one, (0, 2, 1, 3, 4)).reshape(2048, 128)[:1728]
    grad_one = one.reshape(3, 3, 3, 64, 128).astype(F32)

    act = came[:, :128].reshape(8, 2, 2, 32, 128)
    activation = jnp.transpose(act, (2, 3, 1, 0, 4)).reshape(cotangent.shape)
    return (activation, grad_one, grad_two)


def solution(mesh):
    fine = jax.sharding.Mesh(mesh.devices.reshape(2, 4, 2, 2, 4), ("y_lo", "z", "core", "y_hi", "x"))
    in_specs = (
        P(None, None, SPACE, FILT, None),
        P(),
        P(None, None, None, None, FILT),
        P(None, FILT, SPACE, None),
    )
    out_specs = (P(None, FILT, SPACE, None), P(), P(None, None, None, None, FILT))
    return jax.shard_map(body, mesh=fine, in_specs=in_specs, out_specs=out_specs, check_vma=False)
```

time: 148 us -> 143 us (0.966)
  local copies, waits for them, and re-layouts: 13.5 us -> 7.3 us
  blocking collectives: 35.4 us -> 41.4 us
  Pallas kernels: 19.6 us -> 24.3 us
  starting transfers between devices: 46.1 us -> 42 us
  waiting for transfers between devices: 26.2 us -> 22.5 us
    all_to_all x1 -> x2, blocking collectives: 35.4 us -> 41.4 us  [exchange(): return lax.all_to_all(value, axes, 0, 0, tiled=True)]
    all_to_all x3 -> x2, starting transfers between devices: 18.2 us -> 12.5 us  [exchange(): return lax.all_to_all(value, axes, 0, 0, tiled=True)]
    all_to_all x3 -> x2, waiting for transfers between devices: 20.9 us -> 15.3 us  [exchange(): return lax.all_to_all(value, axes, 0, 0, tiled=True)]
    ppermute x0 -> x2, starting transfers between devices: none -> 5.02 us  [the longest x1 4.62 us: body(): other = lax.ppermute(mine, 'core', [(0, 1), (1, 0)])]
    pallas_call x5 -> x6, Pallas kernels: 18.4 us -> 23.1 us  [the longest x1 11.1 us: first(): pl.pallas_call(first_kernel, in_specs=[anywhere] + vmem(5), out_specs=vme...]
    slice x5 -> x1, local copies, waits for them, and re-layouts: 3.34 us -> 0.01 us  [body(): dd = shifted(jnp.concatenate([last, dr[:, :1]], 1), -1, 0)]
    ppermute x9 -> x8, starting transfers between devices: 27.1 us -> 23.8 us  [shifted(): return lax.ppermute(value, SPACE + FILT, pairs)]
    ppermute x9 -> x8, waiting for transfers between devices: 4.11 us -> 5.66 us  [shifted(): return lax.ppermute(value, SPACE + FILT, pairs)]
  transfers between devices with their start and end apart: 14 -> 14, of which waited for: 8 -> 8; matrix products, arithmetic and copies ran while one was open for 5% -> 1% of each run, Pallas kernels for 12% -> 15%
where the time goes in v3:
time: 143 us; the launch traced here: 142 us
  starting transfers between devices  42 us (29%)
  blocking collectives  41.4 us (29%)
  Pallas kernels  24.3 us (17%)
  waiting for transfers between devices  22.5 us (16%)
  local copies, waits for them, and re-layouts  7.3 us (5%)
  other arithmetic  3.52 us (2%)
    all_to_all x2, blocking collectives, exchange(): return lax.all_to_all(value, axes, 0, 0, tiled=True)  41.4 us
    ppermute x8, starting transfers between devices, shifted(): return lax.ppermute(value, SPACE + FILT, pairs)  23.8 us
    all_to_all x2, waiting for transfers between devices, exchange(): return lax.all_to_all(value, axes, 0, 0, tiled=True)  15.3 us
    all_to_all x2, starting transfers between devices, exchange(): return lax.all_to_all(value, axes, 0, 0, tiled=True)  12.5 us
    pallas_call x1, Pallas kernels, first(): pl.pallas_call(first_kernel, in_specs=[anywhere] + vmem(5), out_specs=vme...  11.1 us
    unnamed x22, local copies, waits for them, and re-layouts  5.92 us
    ppermute x8, waiting for transfers between devices, shifted(): return lax.ppermute(value, SPACE + FILT, pairs)  5.66 us
    ppermute x1, starting transfers between devices, body(): other = lax.ppermute(mine, 'core', [(0, 1), (1, 0)])  4.62 us
  transfers between devices with their start and end apart: 14, of which 8 were waited for; matrix products, arithmetic and copies ran while one was open for 1% of the time, Pallas kernels for 15%

profile of v3, /device:TPU:1, one launch (start us, length us, event | category | flops | bytes accessed | tf_op | source)
XLA Modules:
  0.0 142.0 jit_solution(5522501138381379407)
XLA Ops:
  0.6 0.0 copy-start.2
  0.6 2.2 %copy-done.2 = bf16[2,64,8,16,128]{4,3,2,1,0:T(8,128)(2,1)S(1)} copy-done((bf16[2,64,8,16,128]{4,3,2,1,0:T(8,128)(2,1)S(1)}, bf16[2,64,8,16,128]{4,3,2,1,0:T(8,128)(2,1)}, u32[]{:S(2)}) %copy-start.2) | copy-done | bytes 4194328
  2.8 0.9 input_rims.1
  3.7 4.9 %collective-permute-start.1 = (bf16[16,128,128]{2,1,0:T(8,128)(2,1)S(1)}, bf16[16,128,128]{2,1,0:T(8,128)(2,1)S(1)}, u32[]{:S(2)}, u32[]{:S(2)}) collective-permute-start(bf16[16,128,128]{2,1,0:T(8,128)(2,1)S(1)} %get-tuple-element.33), channel_id=1, source_target_pairs={{0,8},{1,9},{2,10},{3,11},{4,12},{5,13},{6,14},{7,15},{8,16},{9,17... | collective-permute-start | bytes 1572872 | tf_op jit(solution)/shard_map/ppermute | solution.py:481
  8.7 3.1 %collective-permute-start = (bf16[8,128,128]{2,1,0:T(8,128)(2,1)S(1)}, bf16[8,128,128]{2,1,0:T(8,128)(2,1)S(1)}, u32[]{:S(2)}, u32[]{:S(2)}) collective-permute-start(bf16[8,128,128]{2,1,0:T(8,128)(2,1)S(1)} %get-tuple-element.32), channel_id=1, source_target_pairs={{0,1},{1,2},{2,3},{3,4},{4,5},{5,6},{6,7},{8,9},{9,10},{10,11},{11... | collective-permute-start | bytes 786440 | tf_op jit(solution)/shard_map/ppermute | solution.py:481
  11.8 3.1 %collective-permute-start.2 = (bf16[128,128]{1,0:T(8,128)(2,1)S(1)}, bf16[128,128]{1,0:T(8,128)(2,1)S(1)}, u32[]{:S(2)}, u32[]{:S(2)}) collective-permute-start(bf16[128,128]{1,0:T(8,128)(2,1)S(1)} %slice_bitcast_fusion), channel_id=1, source_target_pairs={{0,9},{1,10},{2,11},{3,12},{4,13},{5,14},{6,15},{8,17},{9,18},{10,... | collective-permute-start | bytes 98312 | tf_op jit(solution)/shard_map/ppermute | solution.py:481
  14.9 0.0 copy-done.7
  14.9 0.2 reshape.55
  15.1 0.1 copy.13
  15.2 0.0 copy-done.6
  15.2 1.1 weights_and_cotangent.1
  16.3 1.1 collective-permute-done.2.xc_ref
  17.4 0.0 collective-permute-done.xr_ref
  17.4 0.0 collective-permute-done.1.xd_ref
  17.4 0.0 copy-start.8
  17.4 8.1 %all-to-all-start = ((bf16[8,560,128]{2,1,0:T(8,128)(2,1)}), bf16[8,560,128]{2,1,0:T(8,128)(2,1)S(1)}, u32[]{:S(2)}, u32[]{:S(2)}) async-start(bf16[8,560,128]{2,1,0:T(8,128)(2,1)} %weights_and_cotangent.1), calls=%async_computation | async-start | bytes 2293760 | tf_op jit(solution)/shard_map/all_to_all | solution.py:456
  25.6 0.0 copy-done.10
  25.6 0.0 copy-done.9
  25.6 0.0 copy-done.8
  25.6 11.1 %first_layer.1 = (bf16[4,8,64,256]{3,2,1,0:T(8,128)(2,1)}, bf16[8,2,8,160,128]{4,3,2,1,0:T(8,128)(2,1)}, bf16[17,160,128]{2,1,0:T(8,128)(2,1)}, bf16[8,160,128]{...) custom-call(bf16[2,64,8,16,128]{4,3,2,1,0:T(8,128)(2,1)} %x_ref.3, ...), custom_call_target="tpu_custom_call" | custom-call | flops 6442450944 | bytes 20971520 | tf_op jit(solution)/shard_map/first_layer/pallas_call | solution.py:167
  36.7 7.4 %all-to-all-done.m_ref = bf16[8,560,128]{2,1,0:T(8,128)(2,1)S(1)} async-done(((bf16[8,560,128]{2,1,0:T(8,128)(2,1)}), bf16[8,560,128]{2,1,0:T(8,128)(2,1)S(1)}, u32[]{:S(2)}, u32[]{:S(2)}) %all-to-all-start) | async-done | bytes 1146912 | tf_op jit(solution)/shard_map/all_to_all | solution.py:456
  44.1 0.4 collective-permute-start.6
  44.5 3.9 %collective-permute-start.3 = (bf16[8,64,256]{2,1,0:T(8,128)(2,1)}, bf16[8,64,256]{2,1,0:T(8,128)(2,1)S(1)}, u32[]{:S(2)}, u32[]{:S(2)}) collective-permute-start(bf16[8,64,256]{2,1,0:T(8,128)(2,1)} %get-tuple-element.38), channel_id=1, source_target_pairs={{0,8},{1,9},{2,10},{3,11},{4,12},{5,13},{6,14},{7,15},{8,16},{9,17... | collective-permute-start | bytes 786440 | tf_op jit(solution)/shard_map/ppermute | solution.py:481
  48.4 2.5 %collective-permute-start.4 = (bf16[4,64,256]{2,1,0:T(8,128)(2,1)}, bf16[4,64,256]{2,1,0:T(8,128)(2,1)S(1)}, u32[]{:S(2)}, u32[]{:S(2)}) collective-permute-start(bf16[4,64,256]{2,1,0:T(8,128)(2,1)} %get-tuple-element.39), channel_id=1, source_target_pairs={{0,1},{1,2},{2,3},{3,4},{4,5},{5,6},{6,7},{8,9},{9,10},{10,11},{11... | collective-permute-start | bytes 393224 | tf_op jit(solution)/shard_map/ppermute | solution.py:481
  50.9 2.1 %collective-permute-start.5 = (bf16[64,256]{1,0:T(8,128)(2,1)}, bf16[64,256]{1,0:T(8,128)(2,1)S(1)}, u32[]{:S(2)}, u32[]{:S(2)}) collective-permute-start(bf16[64,256]{1,0:T(8,128)(2,1)} %get-tuple-element.42), channel_id=1, source_target_pairs={{0,9},{1,10},{2,11},{3,12},{4,13},{5,14},{6,15},{8,17},{9,18},{10,... | collective-permute-start | bytes 98312 | tf_op jit(solution)/shard_map/ppermute | solution.py:481
  53.0 0.4 collective-permute-done.4.hr_ref
  53.4 0.0 collective-permute-done.3.hd_ref
  53.5 0.9 collective-permute-done.5.hc_ref
  54.3 0.0 collective-permute-done.6.o_ref
  54.4 1.2 copy-done.3
  55.6 2.9 %second_layer.1 = (bf16[8,128,128]{2,1,0:T(8,128)(2,1)S(1)}, bf16[2,2,4,32,256]{4,3,2,1,0:T(8,128)(2,1)S(1)}, bf16[256,512]{1,0:T(8,128)(2,1)S(1)}, bf16[2,4,32,...) custom-call(s32[1]{0:T(128)} %bitcast.core_ref, bf16[4,8,64,256]{3,2,1,0:T(8,128)(2,1)S(1)} %copy-done.3, ...), custom_call_target="tpu_custom_call" | custom-call | flops 1073741824 | bytes 4194304 | tf_op jit(solution)/shard_map/second_layer/pallas_call | solution.py:281
  58.4 1.3 collective-permute-start.7
  59.7 0.0 copy-done.4
  59.8 0.0 copy-done.5
  59.8 0.0 copy-start
  59.8 2.5 %copy-done = bf16[8,2,8,160,128]{4,3,2,1,0:T(8,128)(2,1)S(1)} copy-done((bf16[8,2,8,160,128]{4,3,2,1,0:T(8,128)(2,1)S(1)}, bf16[8,2,8,160,128]{4,3,2,1,0:T(8,128)(2,1)}, u32[]{:S(2)}) %copy-start) | copy-done | bytes 5242904
  62.3 4.0 %first_kernel_grad_inner.1.sum_ref = f32[14,128,128]{2,1,0:T(8,128)S(1)} custom-call(s32[1]{0:T(128)} %bitcast.core_ref, bf16[2,2,4,32,256]{4,3,2,1,0:T(8,128)(2,1)S(1)} %get-tuple-element.50.d_ref, bf16[8,560,128]{2,1,0:T(8,128)(2,1)S(1)} %all-to-all-done.m_ref, bf16[8,560,128]{2,1,0:T(8,128)(2,1)S(1)} %collective-permute-done.6.o_ref, ...), custom_call_target="tpu_custom_call" | custom-call | flops 4294967296 | bytes 9437184 | tf_op jit(solution)/shard_map/first_kernel_grad_inner/pallas_call | solution.py:401
  66.2 0.0 collective-permute-done.7.dr_ref
  66.3 2.8 %collective-permute-start.8 = (bf16[2,5,32,256]{3,2,1,0:T(8,128)(2,1)S(1)}, bf16[2,5,32,256]{3,2,1,0:T(8,128)(2,1)S(1)}, u32[]{:S(2)}, u32[]{:S(2)}) collective-permute-start(bf16[2,5,32,256]{3,2,1,0:T(8,128)(2,1)S(1)} %pad_maximum_fusion.3), channel_id=1, source_target_pairs={{8,0},{9,1},{10,2},{11,3},{12,4},{13,5},{14,6},{15,7},{16,8},{17,9... | collective-permute-start | bytes 491528 | tf_op jit(solution)/shard_map/ppermute | solution.py:481
  69.1 1.2 second_kernel_grad.1
  70.3 3.3 %collective-permute-done.8.dd_ref = bf16[2,5,32,256]{3,2,1,0:T(8,128)(2,1)S(1)} collective-permute-done((bf16[2,5,32,256]{3,2,1,0:T(8,128)(2,1)S(1)}, bf16[2,5,32,256]{3,2,1,0:T(8,128)(2,1)S(1)}, u32[]{:S(2)}, u32[]{:S(2)}) %collective-permute-start.8) | collective-permute-done | bytes 163872 | tf_op jit(solution)/shard_map/ppermute | solution.py:481
  73.6 0.0 collective-permute-start.9
  73.6 3.2 %first_kernel_grad.1 = (bf16[8,8,16,128]{3,2,1,0:T(8,128)(2,1)S(1)}, bf16[8,8,16,128]{3,2,1,0:T(8,128)(2,1)S(1)}) custom-call(s32[1]{0:T(128)} %bitcast.core_ref, bf16[2,2,4,32,256]{4,3,2,1,0:T(8,128)(2,1)S(1)} %get-tuple-element.50.d_ref, bf16[2,5,32,256]{3,2,1,0:T(8,128)(2,1)S(1)} %collective-permute-done.8.dd_ref, ...), custom_call_target="tpu_custom_call" | custom-call | flops 2147483648 | bytes 9437184 | tf_op jit(solution)/shard_map/first_kernel_grad/pallas_call | solution.py:437
  76.8 0.6 collective-permute-start.10
  77.4 1.2 collective-permute-done.10
  78.6 0.1 add_convert_fusion.1
  78.6 0.0 collective-permute-done.9
  78.6 0.4 add_convert_fusion
  79.1 0.1 pad_maximum_fusion
  79.2 32.1 %all_to_all.20 = bf16[64,80,128]{2,1,0:T(8,128)(2,1)S(1)} all-to-all(bf16[64,80,128]{2,1,0:T(8,128)(2,1)S(1)} %bitcast.39), channel_id=1, replica_groups=mesh['y_lo'=2,'z'=4,'core'=2,'y_hi'=2,'x'=4] {'y_lo','z','y_hi','x'}, dimensions={0} | all-to-all | bytes 2621440 | tf_op jit(solution)/shard_map/all_to_all | solution.py:456
  111.3 0.2 reduce_sum.12
  111.5 0.7 pad_maximum_fusion.1
  112.3 4.4 %all-to-all-start.2 = ((bf16[8,144,128]{2,1,0:T(8,128)(2,1)}), bf16[8,144,128]{2,1,0:T(8,128)(2,1)S(1)}, u32[]{:S(2)}, u32[]{:S(2)}) async-start(bf16[8,144,128]{2,1,0:T(8,128)(2,1)} %pad_maximum_fusion.1), calls=%async_computation.2 | async-start | bytes 589824 | tf_op jit(solution)/shard_map/all_to_all | solution.py:456
  116.6 8.0 %all-to-all-done.2 = bf16[8,144,128]{2,1,0:T(8,128)(2,1)S(1)} async-done(((bf16[8,144,128]{2,1,0:T(8,128)(2,1)}), bf16[8,144,128]{2,1,0:T(8,128)(2,1)S(1)}, u32[]{:S(2)}, u32[]{:S(2)}) %all-to-all-start.2) | async-done | bytes 294944 | tf_op jit(solution)/shard_map/all_to_all | solution.py:456
  124.6 0.1 broadcast_in_dim.5
  124.7 9.2 %all_to_all.21 = bf16[8,192,128]{2,1,0:T(8,128)(2,1)S(1)} all-to-all(bf16[8,192,128]{2,1,0:T(8,128)(2,1)S(1)} %broadcast_in_dim.5), channel_id=1, replica_groups=mesh['y_lo'=2,'z'=4,'core'=2,'y_hi'=2,'x'=4] {'y_lo','z'}, dimensions={0} | all-to-all | bytes 786432 | tf_op jit(solution)/shard_map/all_to_all | solution.py:456
  133.9 4.6 %collective-permute-start.11 = (bf16[8,192,128]{2,1,0:T(8,128)(2,1)S(1)}, bf16[8,192,128]{2,1,0:T(8,128)(2,1)S(1)}, u32[]{:S(2)}, u32[]{:S(2)}) collective-permute-start(bf16[8,192,128]{2,1,0:T(8,128)(2,1)S(1)} %all_to_all.21), channel_id=1, source_target_pairs={{0,8},{8,0},{1,9},{9,1},{2,10},{10,2},{3,11},{11,3},{4,12},{12,4},... | collective-permute-start | bytes 1179656 | tf_op jit(solution)/shard_map/ppermute | solution.py:518
  138.6 0.2 copy.14
  138.7 0.8 reshape.60
  139.5 0.4 collective-permute-done.11
  139.9 0.1 select_bitcast_fusion
  139.9 0.1 fusion
  140.1 1.0 convert.4
  141.2 0.8 convert_bitcast_fusion
  (23 shorter events, 0.2 us)
Async XLA Ops:
  0.6 2.2 %copy-start.2 = (bf16[2,64,8,16,128]{4,3,2,1,0:T(8,128)(2,1)S(1)}, bf16[2,64,8,16,128]{4,3,2,1,0:T(8,128)(2,1)}, u32[]{:S(2)}) copy-start(bf16[2,64,8,16,128]{4,3,2,1,0:T(8,128)(2,1)} %x_ref.3) | copy-start | bytes 12582916
  2.8 12.1 %copy-start.7 = (bf16[2,32,2,1024]{3,2,1,0:T(2,128)(2,1)S(1)}, bf16[2,32,2,1024]{3,2,1,0:T(2,128)(2,1)}, u32[]{:S(2)}) copy-start(bf16[2,32,2,1024]{3,2,1,0:T(2,128)(2,1)} %param.8) | copy-start | bytes 786436
  2.8 12.4 %copy-start.6 = (bf16[3,3,3,128,32]{3,4,2,1,0:T(8,128)(2,1)S(1)}, bf16[3,3,3,128,32]{3,4,2,1,0:T(8,128)(2,1)}, u32[]{:S(2)}) copy-start(bf16[3,3,3,128,32]{3,4,2,1,0:T(8,128)(2,1)} %param.7) | copy-start | bytes 663556
  3.7 13.7 %collective-permute-start.1 = (bf16[16,128,128]{2,1,0:T(8,128)(2,1)S(1)}, bf16[16,128,128]{2,1,0:T(8,128)(2,1)S(1)}, u32[]{:S(2)}, u32[]{:S(2)}) collective-permute-start(bf16[16,128,128]{2,1,0:T(8,128)(2,1)S(1)} %get-tuple-element.33), channel_id=1, source_target_pairs={{0,8},{1,9},{2,10},{3,11},{4,12},{5,13},{6,14},{7,15},{8,16},{9,17... | collective-permute-start | bytes 1572872 | tf_op jit(solution)/shard_map/ppermute | solution.py:481
  8.7 8.7 %collective-permute-start = (bf16[8,128,128]{2,1,0:T(8,128)(2,1)S(1)}, bf16[8,128,128]{2,1,0:T(8,128)(2,1)S(1)}, u32[]{:S(2)}, u32[]{:S(2)}) collective-permute-start(bf16[8,128,128]{2,1,0:T(8,128)(2,1)S(1)} %get-tuple-element.32), channel_id=1, source_target_pairs={{0,1},{1,2},{2,3},{3,4},{4,5},{5,6},{6,7},{8,9},{9,10},{10,11},{11... | collective-permute-start | bytes 786440 | tf_op jit(solution)/shard_map/ppermute | solution.py:481
  11.8 5.6 %collective-permute-start.2 = (bf16[128,128]{1,0:T(8,128)(2,1)S(1)}, bf16[128,128]{1,0:T(8,128)(2,1)S(1)}, u32[]{:S(2)}, u32[]{:S(2)}) collective-permute-start(bf16[128,128]{1,0:T(8,128)(2,1)S(1)} %slice_bitcast_fusion), channel_id=1, source_target_pairs={{0,9},{1,10},{2,11},{3,12},{4,13},{5,14},{6,15},{8,17},{9,18},{10,... | collective-permute-start | bytes 98312 | tf_op jit(solution)/shard_map/ppermute | solution.py:481
  17.4 8.2 %copy-start.10 = (bf16[128,128]{1,0:T(8,128)(2,1)}, bf16[128,128]{1,0:T(8,128)(2,1)S(1)}, u32[]{:S(2)}) copy-start(bf16[128,128]{1,0:T(8,128)(2,1)S(1)} %collective-permute-done.2.xc_ref) | copy-start | bytes 98308
  17.4 8.2 %copy-start.9 = (bf16[8,128,128]{2,1,0:T(8,128)(2,1)}, bf16[8,128,128]{2,1,0:T(8,128)(2,1)S(1)}, u32[]{:S(2)}) copy-start(bf16[8,128,128]{2,1,0:T(8,128)(2,1)S(1)} %collective-permute-done.xr_ref) | copy-start | bytes 786436
  17.4 8.2 %copy-start.8 = (bf16[16,128,128]{2,1,0:T(8,128)(2,1)}, bf16[16,128,128]{2,1,0:T(8,128)(2,1)S(1)}, u32[]{:S(2)}) copy-start(bf16[16,128,128]{2,1,0:T(8,128)(2,1)S(1)} %collective-permute-done.1.xd_ref) | copy-start | bytes 1572868
  17.4 26.7 %all-to-all-start = ((bf16[8,560,128]{2,1,0:T(8,128)(2,1)}), bf16[8,560,128]{2,1,0:T(8,128)(2,1)S(1)}, u32[]{:S(2)}, u32[]{:S(2)}) async-start(bf16[8,560,128]{2,1,0:T(8,128)(2,1)} %weights_and_cotangent.1), calls=%async_computation | async-start | bytes 2293760 | tf_op jit(solution)/shard_map/all_to_all | solution.py:456
  44.1 10.3 %collective-permute-start.6 = (bf16[8,560,128]{2,1,0:T(8,128)(2,1)S(1)}, bf16[8,560,128]{2,1,0:T(8,128)(2,1)S(1)}, u32[]{:S(2)}, u32[]{:S(2)}) collective-permute-start(bf16[8,560,128]{2,1,0:T(8,128)(2,1)S(1)} %all-to-all-done.m_ref), channel_id=1, source_target_pairs={{0,8},{8,0},{1,9},{9,1},{2,10},{10,2},{3,11},{11,3},{4,12},{12,4},... | collective-permute-start | bytes 3440648 | tf_op jit(solution)/shard_map/ppermute | solution.py:499
  44.5 9.0 %collective-permute-start.3 = (bf16[8,64,256]{2,1,0:T(8,128)(2,1)}, bf16[8,64,256]{2,1,0:T(8,128)(2,1)S(1)}, u32[]{:S(2)}, u32[]{:S(2)}) collective-permute-start(bf16[8,64,256]{2,1,0:T(8,128)(2,1)} %get-tuple-element.38), channel_id=1, source_target_pairs={{0,8},{1,9},{2,10},{3,11},{4,12},{5,13},{6,14},{7,15},{8,16},{9,17... | collective-permute-start | bytes 786440 | tf_op jit(solution)/shard_map/ppermute | solution.py:481
  48.4 5.1 %collective-permute-start.4 = (bf16[4,64,256]{2,1,0:T(8,128)(2,1)}, bf16[4,64,256]{2,1,0:T(8,128)(2,1)S(1)}, u32[]{:S(2)}, u32[]{:S(2)}) collective-permute-start(bf16[4,64,256]{2,1,0:T(8,128)(2,1)} %get-tuple-element.39), channel_id=1, source_target_pairs={{0,1},{1,2},{2,3},{3,4},{4,5},{5,6},{6,7},{8,9},{9,10},{10,11},{11... | collective-permute-start | bytes 393224 | tf_op jit(solution)/shard_map/ppermute | solution.py:481
  50.9 3.5 %collective-permute-start.5 = (bf16[64,256]{1,0:T(8,128)(2,1)}, bf16[64,256]{1,0:T(8,128)(2,1)S(1)}, u32[]{:S(2)}, u32[]{:S(2)}) collective-permute-start(bf16[64,256]{1,0:T(8,128)(2,1)} %get-tuple-element.42), channel_id=1, source_target_pairs={{0,9},{1,10},{2,11},{3,12},{4,13},{5,14},{6,15},{8,17},{9,18},{10,... | collective-permute-start | bytes 98312 | tf_op jit(solution)/shard_map/ppermute | solution.py:481
  54.4 1.2 copy-start.3
  55.6 4.2 %copy-start.4 = (bf16[17,160,128]{2,1,0:T(8,128)(2,1)S(1)}, bf16[17,160,128]{2,1,0:T(8,128)(2,1)}, u32[]{:S(2)}) copy-start(bf16[17,160,128]{2,1,0:T(8,128)(2,1)} %get-tuple-element.52.qd_ref) | copy-start | bytes 2088964
  55.6 4.2 %copy-start.5 = (bf16[8,160,128]{2,1,0:T(8,128)(2,1)S(1)}, bf16[8,160,128]{2,1,0:T(8,128)(2,1)}, u32[]{:S(2)}) copy-start(bf16[8,160,128]{2,1,0:T(8,128)(2,1)} %get-tuple-element.53.qr_ref) | copy-start | bytes 983044
  58.4 7.8 %collective-permute-start.7 = (bf16[2,2,32,256]{3,2,1,0:T(8,128)(2,1)S(1)}, bf16[2,2,32,256]{3,2,1,0:T(8,128)(2,1)S(1)}, u32[]{:S(2)}, u32[]{:S(2)}) collective-permute-start(bf16[2,2,32,256]{3,2,1,0:T(8,128)(2,1)S(1)} %get-tuple-element.49), channel_id=1, source_target_pairs={{1,0},{2,1},{3,2},{4,3},{5,4},{6,5},{7,6},{9,8},{10,9},{11,10},{12... | collective-permute-start | bytes 196616 | tf_op jit(solution)/shard_map/ppermute | solution.py:481
  59.8 2.5 %copy-start = (bf16[8,2,8,160,128]{4,3,2,1,0:T(8,128)(2,1)S(1)}, bf16[8,2,8,160,128]{4,3,2,1,0:T(8,128)(2,1)}, u32[]{:S(2)}) copy-start(bf16[8,2,8,160,128]{4,3,2,1,0:T(8,128)(2,1)} %get-tuple-element.51.q_ref) | copy-start | bytes 15728644
  62.3 11.4 %copy-start.1 = (bf16[8,2,8,160,128]{4,3,2,1,0:T(8,128)(2,1)S(1)}, bf16[8,2,8,160,128]{4,3,2,1,0:T(8,128)(2,1)}, u32[]{:S(2)}) copy-start(bf16[8,2,8,160,128]{4,3,2,1,0:T(8,128)(2,1)} %get-tuple-element.51.q_ref) | copy-start | bytes 15728644
  66.3 7.3 %collective-permute-start.8 = (bf16[2,5,32,256]{3,2,1,0:T(8,128)(2,1)S(1)}, bf16[2,5,32,256]{3,2,1,0:T(8,128)(2,1)S(1)}, u32[]{:S(2)}, u32[]{:S(2)}) collective-permute-start(bf16[2,5,32,256]{3,2,1,0:T(8,128)(2,1)S(1)} %pad_maximum_fusion.3), channel_id=1, source_target_pairs={{8,0},{9,1},{10,2},{11,3},{12,4},{13,5},{14,6},{15,7},{16,8},{17,9... | collective-permute-start | bytes 491528 | tf_op jit(solution)/shard_map/ppermute | solution.py:481
  73.6 5.0 %collective-permute-start.9 = (bf16[8,8,64,128]{3,2,1,0:T(8,128)(2,1)S(1)}, bf16[8,8,64,128]{3,2,1,0:T(8,128)(2,1)S(1)}, u32[]{:S(2)}, u32[]{:S(2)}) collective-permute-start(bf16[8,8,64,128]{3,2,1,0:T(8,128)(2,1)S(1)} %get-tuple-element.56), channel_id=1, source_target_pairs={{0,8},{8,0},{1,9},{9,1},{2,10},{10,2},{3,11},{11,3},{4,12},{12,4},... | collective-permute-start | bytes 3145736 | tf_op jit(solution)/shard_map/ppermute | solution.py:469
  76.8 1.7 %collective-permute-start.10 = (bf16[8,8,16,128]{3,2,1,0:T(8,128)(2,1)S(1)}, bf16[8,8,16,128]{3,2,1,0:T(8,128)(2,1)S(1)}, u32[]{:S(2)}, u32[]{:S(2)}) collective-permute-start(bf16[8,8,16,128]{3,2,1,0:T(8,128)(2,1)S(1)} %get-tuple-element.60), channel_id=1, source_target_pairs={{0,8},{8,0},{1,9},{9,1},{2,10},{10,2},{3,11},{11,3},{4,12},{12,4},... | collective-permute-start | bytes 786440 | tf_op jit(solution)/shard_map/ppermute | solution.py:469
  112.3 12.3 %all-to-all-start.2 = ((bf16[8,144,128]{2,1,0:T(8,128)(2,1)}), bf16[8,144,128]{2,1,0:T(8,128)(2,1)S(1)}, u32[]{:S(2)}, u32[]{:S(2)}) async-start(bf16[8,144,128]{2,1,0:T(8,128)(2,1)} %pad_maximum_fusion.1), calls=%async_computation.2 | async-start | bytes 589824 | tf_op jit(solution)/shard_map/all_to_all | solution.py:456
  133.9 6.0 %collective-permute-start.11 = (bf16[8,192,128]{2,1,0:T(8,128)(2,1)S(1)}, bf16[8,192,128]{2,1,0:T(8,128)(2,1)S(1)}, u32[]{:S(2)}, u32[]{:S(2)}) collective-permute-start(bf16[8,192,128]{2,1,0:T(8,128)(2,1)S(1)} %all_to_all.21), channel_id=1, source_target_pairs={{0,8},{8,0},{1,9},{9,1},{2,10},{10,2},{3,11},{11,3},{4,12},{12,4},... | collective-permute-start | bytes 1179656 | tf_op jit(solution)/shard_map/ppermute | solution.py:518

commit v4 on v3

--- a/solution.py
+++ b/solution.py
@@ -185,8 +185,8 @@
             pltpu.SemaphoreType.DMA((8,)),
             pltpu.SemaphoreType.DMA((8,)),
         ],
-        compiler_params=params(56),
-        cost_estimate=cost(6, 20),
+        compiler_params=params(54),
+        cost_estimate=cost(60, 200),
         name="first_layer",
     )(x, xd, xr, xc, sel, kernel)
 
@@ -290,7 +290,7 @@
             jax.ShapeDtypeStruct((2, 2, 32, 256), BF),
         ),
         scratch_shapes=[WEIGHT, pltpu.VMEM((5, 9, 32, 256), BF)],
-        compiler_params=params(40),
+        compiler_params=params(16),
         cost_estimate=cost(1, 4),
         name="second_layer",
     )(core, h, hd, hr, hc, mine, other)
@@ -324,7 +324,7 @@
         out_specs=vmem(2),
         out_shape=(jax.ShapeDtypeStruct((8, 8, 64, 128), BF),) * 2,
         scratch_shapes=[pltpu.VMEM((5, 9, 32, 256), BF)],
-        compiler_params=params(40),
+        compiler_params=params(16),
         cost_estimate=cost(1, 4),
         name="second_kernel_grad",
     )(core, h, hd, hr, hc, turned)
@@ -404,7 +404,7 @@
         out_specs=vmem(1)[0],
         out_shape=jax.ShapeDtypeStruct((14, 128, 128), F32),
         scratch_shapes=[WEIGHT, pltpu.VMEM((2, 2, 4, 32, 256), BF), pltpu.VMEM((len(INNER), 64, 256), BF)],
-        compiler_params=params(40),
+        compiler_params=params(16),
         cost_estimate=cost(4, 9),
         name="first_kernel_grad_inner",
     )(core, d, mine, other, h, q, qd, qr)
@@ -440,7 +440,7 @@
         out_specs=vmem(2),
         out_shape=(jax.ShapeDtypeStruct((8, 8, 16, 128), BF),) * 2,
         scratch_shapes=[WEIGHT, pltpu.VMEM((2, 3, 5, 32, 256), BF), pltpu.VMEM((len(OUTER), 64, 256), BF)],
-        compiler_params=params(40),
+        compiler_params=params(16),
         cost_estimate=cost(2, 9),
         name="first_kernel_grad",
     )(core, d, dd, dr, mine, other, h, q, qd, qr, partial)
@@ -492,7 +492,7 @@
     xr = shifted(side, 0, 1)
     xd = shifted(last, 1, 0)
     xc = shifted(last[7], 1, 1)
-    mixed, xr, xd, xc = lax.optimization_barrier((mixed, xr, xd, xc))
+    mixed, _ = lax.optimization_barrier((mixed, last))
     mixed = exchange(mixed, FILT)
     h, q, qd, qr, last, side, end = first(inputs, xd, xr, xc, sel, kernel_one.reshape(27, 64, 128))
     mixed, end = lax.optimization_barrier((mixed, end))

time: 143 us -> 138 us (0.965)
  starting transfers between devices: 42 us -> 39.1 us
  waiting for transfers between devices: 22.5 us -> 20.2 us
    all_to_all x2, starting transfers between devices: 12.5 us -> 9.75 us  [exchange(): return lax.all_to_all(value, axes, 0, 0, tiled=True)]
  transfers between devices with their start and end apart: 14 -> 14, of which waited for: 8 -> 7; matrix products, arithmetic and copies ran while one was open for 1% -> 1% of each run, Pallas kernels for 15% -> 15%
where the time goes in v4:
time: 138 us
  blocking collectives  41.5 us (30%)
  starting transfers between devices  39.1 us (28%)
  Pallas kernels  24.3 us (18%)
  waiting for transfers between devices  20.2 us (15%)
  local copies, waits for them, and re-layouts  8.18 us (6%)
  other arithmetic  3.48 us (3%)
    all_to_all x2, blocking collectives, exchange(): return lax.all_to_all(value, axes, 0, 0, tiled=True)  41.5 us
    ppermute x8, starting transfers between devices, shifted(): return lax.ppermute(value, SPACE + FILT, pairs)  23.4 us
    all_to_all x2, waiting for transfers between devices, exchange(): return lax.all_to_all(value, axes, 0, 0, tiled=True)  14.3 us
    pallas_call x1, Pallas kernels, first(): pl.pallas_call(first_kernel, in_specs=[anywhere] + vmem(5), out_specs=vme...  11.1 us
    all_to_all x2, starting transfers between devices, exchange(): return lax.all_to_all(value, axes, 0, 0, tiled=True)  9.75 us
    unnamed x22, local copies, waits for them, and re-layouts  6.8 us
    ppermute x1, starting transfers between devices, body(): other = lax.ppermute(mine, 'core', [(0, 1), (1, 0)])  4.62 us
    ppermute x8, waiting for transfers between devices, shifted(): return lax.ppermute(value, SPACE + FILT, pairs)  4.39 us
  transfers between devices with their start and end apart: 14, of which 7 were waited for; matrix products, arithmetic and copies ran while one was open for 1% of the time, Pallas kernels for 15%

profile of v4, /device:TPU:1, one launch (start us, length us, event | category | flops | bytes accessed | tf_op | source)
XLA Modules:
  0.0 137.8 jit_solution(2888678020646274792)
XLA Ops:
  0.6 0.0 copy-start.2
  0.6 2.2 %copy-done.2 = bf16[2,64,8,16,128]{4,3,2,1,0:T(8,128)(2,1)S(1)} copy-done((bf16[2,64,8,16,128]{4,3,2,1,0:T(8,128)(2,1)S(1)}, bf16[2,64,8,16,128]{4,3,2,1,0:T(8,128)(2,1)}, u32[]{:S(2)}) %copy-start.2) | copy-done | bytes 4194328
  2.8 0.9 input_rims.1
  3.7 4.9 %collective-permute-start = (bf16[16,128,128]{2,1,0:T(8,128)(2,1)S(1)}, bf16[16,128,128]{2,1,0:T(8,128)(2,1)S(1)}, u32[]{:S(2)}, u32[]{:S(2)}) collective-permute-start(bf16[16,128,128]{2,1,0:T(8,128)(2,1)S(1)} %get-tuple-element.29), channel_id=1, source_target_pairs={{0,8},{1,9},{2,10},{3,11},{4,12},{5,13},{6,14},{7,15},{8,16},{9,17... | collective-permute-start | bytes 1572872 | tf_op jit(solution)/shard_map/ppermute | solution.py:481
  8.7 3.1 %collective-permute-start.1 = (bf16[8,128,128]{2,1,0:T(8,128)(2,1)S(1)}, bf16[8,128,128]{2,1,0:T(8,128)(2,1)S(1)}, u32[]{:S(2)}, u32[]{:S(2)}) collective-permute-start(bf16[8,128,128]{2,1,0:T(8,128)(2,1)S(1)} %get-tuple-element.30), channel_id=1, source_target_pairs={{0,1},{1,2},{2,3},{3,4},{4,5},{5,6},{6,7},{8,9},{9,10},{10,11},{11... | collective-permute-start | bytes 786440 | tf_op jit(solution)/shard_map/ppermute | solution.py:481
  11.8 3.1 %collective-permute-start.2 = (bf16[128,128]{1,0:T(8,128)(2,1)S(1)}, bf16[128,128]{1,0:T(8,128)(2,1)S(1)}, u32[]{:S(2)}, u32[]{:S(2)}) collective-permute-start(bf16[128,128]{1,0:T(8,128)(2,1)S(1)} %slice_bitcast_fusion), channel_id=1, source_target_pairs={{0,9},{1,10},{2,11},{3,12},{4,13},{5,14},{6,15},{8,17},{9,18},{10,... | collective-permute-start | bytes 98312 | tf_op jit(solution)/shard_map/ppermute | solution.py:481
  14.9 0.0 copy-done.7
  14.9 0.2 reshape.56
  15.1 0.1 copy.13
  15.2 0.0 copy-done.6
  15.2 1.1 weights_and_cotangent.1
  16.3 5.4 %all-to-all-start = ((bf16[8,560,128]{2,1,0:T(8,128)(2,1)}), bf16[8,560,128]{2,1,0:T(8,128)(2,1)S(1)}, u32[]{:S(2)}, u32[]{:S(2)}) async-start(bf16[8,560,128]{2,1,0:T(8,128)(2,1)} %weights_and_cotangent.1), calls=%async_computation | async-start | bytes 2293760 | tf_op jit(solution)/shard_map/all_to_all | solution.py:456
  21.7 0.0 collective-permute-done.2.xc_ref
  21.7 0.0 copy-start.10
  21.7 0.0 collective-permute-done.1.xr_ref
  21.7 0.0 copy-start.9
  21.7 0.0 collective-permute-done.xd_ref
  21.7 0.0 copy-start.8
  21.8 0.6 copy-done.10
  22.3 0.1 copy-done.9
  22.4 0.2 copy-done.8
  22.6 11.1 %first_layer.1 = (bf16[4,8,64,256]{3,2,1,0:T(8,128)(2,1)}, bf16[8,2,8,160,128]{4,3,2,1,0:T(8,128)(2,1)}, bf16[17,160,128]{2,1,0:T(8,128)(2,1)}, bf16[8,160,128]{...) custom-call(bf16[2,64,8,16,128]{4,3,2,1,0:T(8,128)(2,1)} %x_ref.3, ...), custom_call_target="tpu_custom_call" | custom-call | flops 64424509440 | bytes 209715200 | tf_op jit(solution)/shard_map/first_layer/pallas_call | solution.py:167
  33.8 6.3 %all-to-all-done.m_ref = bf16[8,560,128]{2,1,0:T(8,128)(2,1)S(1)} async-done(((bf16[8,560,128]{2,1,0:T(8,128)(2,1)}), bf16[8,560,128]{2,1,0:T(8,128)(2,1)S(1)}, u32[]{:S(2)}, u32[]{:S(2)}) %all-to-all-start) | async-done | bytes 1146912 | tf_op jit(solution)/shard_map/all_to_all | solution.py:456
  40.1 0.8 collective-permute-start.6
  40.9 3.4 %collective-permute-start.3 = (bf16[8,64,256]{2,1,0:T(8,128)(2,1)}, bf16[8,64,256]{2,1,0:T(8,128)(2,1)S(1)}, u32[]{:S(2)}, u32[]{:S(2)}) collective-permute-start(bf16[8,64,256]{2,1,0:T(8,128)(2,1)} %get-tuple-element.32), channel_id=1, source_target_pairs={{0,8},{1,9},{2,10},{3,11},{4,12},{5,13},{6,14},{7,15},{8,16},{9,17... | collective-permute-start | bytes 786440 | tf_op jit(solution)/shard_map/ppermute | solution.py:481
  44.3 2.5 %collective-permute-start.4 = (bf16[4,64,256]{2,1,0:T(8,128)(2,1)}, bf16[4,64,256]{2,1,0:T(8,128)(2,1)S(1)}, u32[]{:S(2)}, u32[]{:S(2)}) collective-permute-start(bf16[4,64,256]{2,1,0:T(8,128)(2,1)} %get-tuple-element.33), channel_id=1, source_target_pairs={{0,1},{1,2},{2,3},{3,4},{4,5},{5,6},{6,7},{8,9},{9,10},{10,11},{11... | collective-permute-start | bytes 393224 | tf_op jit(solution)/shard_map/ppermute | solution.py:481
  46.8 2.1 %collective-permute-start.5 = (bf16[64,256]{1,0:T(8,128)(2,1)}, bf16[64,256]{1,0:T(8,128)(2,1)S(1)}, u32[]{:S(2)}, u32[]{:S(2)}) collective-permute-start(bf16[64,256]{1,0:T(8,128)(2,1)} %get-tuple-element.36), channel_id=1, source_target_pairs={{0,9},{1,10},{2,11},{3,12},{4,13},{5,14},{6,15},{8,17},{9,18},{10,... | collective-permute-start | bytes 98312 | tf_op jit(solution)/shard_map/ppermute | solution.py:481
  49.0 0.9 collective-permute-done.4.hr_ref
  49.9 0.0 collective-permute-done.3.hd_ref
  49.9 0.4 collective-permute-done.5.hc_ref
  50.3 0.0 collective-permute-done.6.o_ref
  50.3 1.2 copy-done.3
  51.5 2.8 %second_layer.1 = (bf16[8,128,128]{2,1,0:T(8,128)(2,1)S(1)}, bf16[2,2,4,32,256]{4,3,2,1,0:T(8,128)(2,1)S(1)}, bf16[256,512]{1,0:T(8,128)(2,1)S(1)}, bf16[2,4,32,...) custom-call(s32[1]{0:T(128)} %bitcast.core_ref, bf16[4,8,64,256]{3,2,1,0:T(8,128)(2,1)S(1)} %copy-done.3, ...), custom_call_target="tpu_custom_call" | custom-call | flops 1073741824 | bytes 4194304 | tf_op jit(solution)/shard_map/second_layer/pallas_call | solution.py:281
  54.4 1.3 collective-permute-start.7
  55.7 0.0 copy-done.4
  55.7 2.5 %copy-done = bf16[8,2,8,160,128]{4,3,2,1,0:T(8,128)(2,1)S(1)} copy-done((bf16[8,2,8,160,128]{4,3,2,1,0:T(8,128)(2,1)S(1)}, bf16[8,2,8,160,128]{4,3,2,1,0:T(8,128)(2,1)}, u32[]{:S(2)}) %copy-start) | copy-done | bytes 5242904
  58.2 4.0 %first_kernel_grad_inner.1.sum_ref = f32[14,128,128]{2,1,0:T(8,128)S(1)} custom-call(s32[1]{0:T(128)} %bitcast.core_ref, bf16[2,2,4,32,256]{4,3,2,1,0:T(8,128)(2,1)S(1)} %get-tuple-element.44.d_ref, bf16[8,560,128]{2,1,0:T(8,128)(2,1)S(1)} %all-to-all-done.m_ref, bf16[8,560,128]{2,1,0:T(8,128)(2,1)S(1)} %collective-permute-done.6.o_ref, ...), custom_call_target="tpu_custom_call" | custom-call | flops 4294967296 | bytes 9437184 | tf_op jit(solution)/shard_map/first_kernel_grad_inner/pallas_call | solution.py:401
  62.2 0.0 collective-permute-done.7.dr_ref
  62.2 2.8 %collective-permute-start.8 = (bf16[2,5,32,256]{3,2,1,0:T(8,128)(2,1)S(1)}, bf16[2,5,32,256]{3,2,1,0:T(8,128)(2,1)S(1)}, u32[]{:S(2)}, u32[]{:S(2)}) collective-permute-start(bf16[2,5,32,256]{3,2,1,0:T(8,128)(2,1)S(1)} %pad_maximum_fusion.3), channel_id=1, source_target_pairs={{8,0},{9,1},{10,2},{11,3},{12,4},{13,5},{14,6},{15,7},{16,8},{17,9... | collective-permute-start | bytes 491528 | tf_op jit(solution)/shard_map/ppermute | solution.py:481
  65.1 1.2 second_kernel_grad.1
  66.3 3.1 %collective-permute-done.8.dd_ref = bf16[2,5,32,256]{3,2,1,0:T(8,128)(2,1)S(1)} collective-permute-done((bf16[2,5,32,256]{3,2,1,0:T(8,128)(2,1)S(1)}, bf16[2,5,32,256]{3,2,1,0:T(8,128)(2,1)S(1)}, u32[]{:S(2)}, u32[]{:S(2)}) %collective-permute-start.8) | collective-permute-done | bytes 163872 | tf_op jit(solution)/shard_map/ppermute | solution.py:481
  69.3 0.0 collective-permute-start.9
  69.3 3.2 %first_kernel_grad.1 = (bf16[8,8,16,128]{3,2,1,0:T(8,128)(2,1)S(1)}, bf16[8,8,16,128]{3,2,1,0:T(8,128)(2,1)S(1)}) custom-call(s32[1]{0:T(128)} %bitcast.core_ref, bf16[2,2,4,32,256]{4,3,2,1,0:T(8,128)(2,1)S(1)} %get-tuple-element.44.d_ref, bf16[2,5,32,256]{3,2,1,0:T(8,128)(2,1)S(1)} %collective-permute-done.8.dd_ref, ...), custom_call_target="tpu_custom_call" | custom-call | flops 2147483648 | bytes 9437184 | tf_op jit(solution)/shard_map/first_kernel_grad/pallas_call | solution.py:437
  72.5 0.6 collective-permute-start.10
  73.1 1.2 collective-permute-done.10
  74.3 0.1 add_convert_fusion.1
  74.4 0.0 collective-permute-done.9
  74.4 0.4 add_convert_fusion
  74.8 0.1 pad_maximum_fusion
  74.9 32.2 %all_to_all.20 = bf16[64,80,128]{2,1,0:T(8,128)(2,1)S(1)} all-to-all(bf16[64,80,128]{2,1,0:T(8,128)(2,1)S(1)} %bitcast.39), channel_id=1, replica_groups=mesh['y_lo'=2,'z'=4,'core'=2,'y_hi'=2,'x'=4] {'y_lo','z','y_hi','x'}, dimensions={0} | all-to-all | bytes 2621440 | tf_op jit(solution)/shard_map/all_to_all | solution.py:456
  107.1 0.2 reduce_sum.12
  107.3 0.7 pad_maximum_fusion.1
  108.1 4.4 %all-to-all-start.2 = ((bf16[8,144,128]{2,1,0:T(8,128)(2,1)}), bf16[8,144,128]{2,1,0:T(8,128)(2,1)S(1)}, u32[]{:S(2)}, u32[]{:S(2)}) async-start(bf16[8,144,128]{2,1,0:T(8,128)(2,1)} %pad_maximum_fusion.1), calls=%async_computation.2 | async-start | bytes 589824 | tf_op jit(solution)/shard_map/all_to_all | solution.py:456
  112.4 8.0 %all-to-all-done.2 = bf16[8,144,128]{2,1,0:T(8,128)(2,1)S(1)} async-done(((bf16[8,144,128]{2,1,0:T(8,128)(2,1)}), bf16[8,144,128]{2,1,0:T(8,128)(2,1)S(1)}, u32[]{:S(2)}, u32[]{:S(2)}) %all-to-all-start.2) | async-done | bytes 294944 | tf_op jit(solution)/shard_map/all_to_all | solution.py:456
  120.4 0.1 broadcast_in_dim.5
  120.5 9.2 %all_to_all.21 = bf16[8,192,128]{2,1,0:T(8,128)(2,1)S(1)} all-to-all(bf16[8,192,128]{2,1,0:T(8,128)(2,1)S(1)} %broadcast_in_dim.5), channel_id=1, replica_groups=mesh['y_lo'=2,'z'=4,'core'=2,'y_hi'=2,'x'=4] {'y_lo','z'}, dimensions={0} | all-to-all | bytes 786432 | tf_op jit(solution)/shard_map/all_to_all | solution.py:456
  129.7 4.6 %collective-permute-start.11 = (bf16[8,192,128]{2,1,0:T(8,128)(2,1)S(1)}, bf16[8,192,128]{2,1,0:T(8,128)(2,1)S(1)}, u32[]{:S(2)}, u32[]{:S(2)}) collective-permute-start(bf16[8,192,128]{2,1,0:T(8,128)(2,1)S(1)} %all_to_all.21), channel_id=1, source_target_pairs={{0,8},{8,0},{1,9},{9,1},{2,10},{10,2},{3,11},{11,3},{4,12},{12,4},... | collective-permute-start | bytes 1179656 | tf_op jit(solution)/shard_map/ppermute | solution.py:518
  134.4 0.2 copy.14
  134.5 0.8 reshape.60
  135.3 0.4 collective-permute-done.11
  135.7 0.1 select_bitcast_fusion
  135.7 0.1 fusion
  135.9 1.0 convert.4
  137.0 0.8 convert_bitcast_fusion
  (23 shorter events, 0.2 us)
Async XLA Ops:
  0.6 2.2 %copy-start.2 = (bf16[2,64,8,16,128]{4,3,2,1,0:T(8,128)(2,1)S(1)}, bf16[2,64,8,16,128]{4,3,2,1,0:T(8,128)(2,1)}, u32[]{:S(2)}) copy-start(bf16[2,64,8,16,128]{4,3,2,1,0:T(8,128)(2,1)} %x_ref.3) | copy-start | bytes 12582916
  2.8 12.1 %copy-start.7 = (bf16[2,32,2,1024]{3,2,1,0:T(2,128)(2,1)S(1)}, bf16[2,32,2,1024]{3,2,1,0:T(2,128)(2,1)}, u32[]{:S(2)}) copy-start(bf16[2,32,2,1024]{3,2,1,0:T(2,128)(2,1)} %param.8) | copy-start | bytes 786436
  2.8 12.4 %copy-start.6 = (bf16[3,3,3,128,32]{3,4,2,1,0:T(8,128)(2,1)S(1)}, bf16[3,3,3,128,32]{3,4,2,1,0:T(8,128)(2,1)}, u32[]{:S(2)}) copy-start(bf16[3,3,3,128,32]{3,4,2,1,0:T(8,128)(2,1)} %param.7) | copy-start | bytes 663556
  3.7 18.0 %collective-permute-start = (bf16[16,128,128]{2,1,0:T(8,128)(2,1)S(1)}, bf16[16,128,128]{2,1,0:T(8,128)(2,1)S(1)}, u32[]{:S(2)}, u32[]{:S(2)}) collective-permute-start(bf16[16,128,128]{2,1,0:T(8,128)(2,1)S(1)} %get-tuple-element.29), channel_id=1, source_target_pairs={{0,8},{1,9},{2,10},{3,11},{4,12},{5,13},{6,14},{7,15},{8,16},{9,17... | collective-permute-start | bytes 1572872 | tf_op jit(solution)/shard_map/ppermute | solution.py:481
  8.7 13.1 %collective-permute-start.1 = (bf16[8,128,128]{2,1,0:T(8,128)(2,1)S(1)}, bf16[8,128,128]{2,1,0:T(8,128)(2,1)S(1)}, u32[]{:S(2)}, u32[]{:S(2)}) collective-permute-start(bf16[8,128,128]{2,1,0:T(8,128)(2,1)S(1)} %get-tuple-element.30), channel_id=1, source_target_pairs={{0,1},{1,2},{2,3},{3,4},{4,5},{5,6},{6,7},{8,9},{9,10},{10,11},{11... | collective-permute-start | bytes 786440 | tf_op jit(solution)/shard_map/ppermute | solution.py:481
  11.8 9.9 %collective-permute-start.2 = (bf16[128,128]{1,0:T(8,128)(2,1)S(1)}, bf16[128,128]{1,0:T(8,128)(2,1)S(1)}, u32[]{:S(2)}, u32[]{:S(2)}) collective-permute-start(bf16[128,128]{1,0:T(8,128)(2,1)S(1)} %slice_bitcast_fusion), channel_id=1, source_target_pairs={{0,9},{1,10},{2,11},{3,12},{4,13},{5,14},{6,15},{8,17},{9,18},{10,... | collective-permute-start | bytes 98312 | tf_op jit(solution)/shard_map/ppermute | solution.py:481
  16.3 23.8 %all-to-all-start = ((bf16[8,560,128]{2,1,0:T(8,128)(2,1)}), bf16[8,560,128]{2,1,0:T(8,128)(2,1)S(1)}, u32[]{:S(2)}, u32[]{:S(2)}) async-start(bf16[8,560,128]{2,1,0:T(8,128)(2,1)} %weights_and_cotangent.1), calls=%async_computation | async-start | bytes 2293760 | tf_op jit(solution)/shard_map/all_to_all | solution.py:456
  21.7 0.6 copy-start.10
  21.7 0.7 copy-start.9
  21.7 0.9 copy-start.8
  40.1 10.2 %collective-permute-start.6 = (bf16[8,560,128]{2,1,0:T(8,128)(2,1)S(1)}, bf16[8,560,128]{2,1,0:T(8,128)(2,1)S(1)}, u32[]{:S(2)}, u32[]{:S(2)}) collective-permute-start(bf16[8,560,128]{2,1,0:T(8,128)(2,1)S(1)} %all-to-all-done.m_ref), channel_id=1, source_target_pairs={{0,8},{8,0},{1,9},{9,1},{2,10},{10,2},{3,11},{11,3},{4,12},{12,4},... | collective-permute-start | bytes 3440648 | tf_op jit(solution)/shard_map/ppermute | solution.py:499
  40.9 9.0 %collective-permute-start.3 = (bf16[8,64,256]{2,1,0:T(8,128)(2,1)}, bf16[8,64,256]{2,1,0:T(8,128)(2,1)S(1)}, u32[]{:S(2)}, u32[]{:S(2)}) collective-permute-start(bf16[8,64,256]{2,1,0:T(8,128)(2,1)} %get-tuple-element.32), channel_id=1, source_target_pairs={{0,8},{1,9},{2,10},{3,11},{4,12},{5,13},{6,14},{7,15},{8,16},{9,17... | collective-permute-start | bytes 786440 | tf_op jit(solution)/shard_map/ppermute | solution.py:481
  44.3 5.6 %collective-permute-start.4 = (bf16[4,64,256]{2,1,0:T(8,128)(2,1)}, bf16[4,64,256]{2,1,0:T(8,128)(2,1)S(1)}, u32[]{:S(2)}, u32[]{:S(2)}) collective-permute-start(bf16[4,64,256]{2,1,0:T(8,128)(2,1)} %get-tuple-element.33), channel_id=1, source_target_pairs={{0,1},{1,2},{2,3},{3,4},{4,5},{5,6},{6,7},{8,9},{9,10},{10,11},{11... | collective-permute-start | bytes 393224 | tf_op jit(solution)/shard_map/ppermute | solution.py:481
  46.8 3.5 %collective-permute-start.5 = (bf16[64,256]{1,0:T(8,128)(2,1)}, bf16[64,256]{1,0:T(8,128)(2,1)S(1)}, u32[]{:S(2)}, u32[]{:S(2)}) collective-permute-start(bf16[64,256]{1,0:T(8,128)(2,1)} %get-tuple-element.36), channel_id=1, source_target_pairs={{0,9},{1,10},{2,11},{3,12},{4,13},{5,14},{6,15},{8,17},{9,18},{10,... | collective-permute-start | bytes 98312 | tf_op jit(solution)/shard_map/ppermute | solution.py:481
  50.3 1.2 copy-start.3
  51.5 4.2 %copy-start.4 = (bf16[17,160,128]{2,1,0:T(8,128)(2,1)S(1)}, bf16[17,160,128]{2,1,0:T(8,128)(2,1)}, u32[]{:S(2)}) copy-start(bf16[17,160,128]{2,1,0:T(8,128)(2,1)} %get-tuple-element.46.qd_ref) | copy-start | bytes 2088964
  51.5 4.2 %copy-start.5 = (bf16[8,160,128]{2,1,0:T(8,128)(2,1)S(1)}, bf16[8,160,128]{2,1,0:T(8,128)(2,1)}, u32[]{:S(2)}) copy-start(bf16[8,160,128]{2,1,0:T(8,128)(2,1)} %get-tuple-element.47.qr_ref) | copy-start | bytes 983044
  54.4 7.8 %collective-permute-start.7 = (bf16[2,2,32,256]{3,2,1,0:T(8,128)(2,1)S(1)}, bf16[2,2,32,256]{3,2,1,0:T(8,128)(2,1)S(1)}, u32[]{:S(2)}, u32[]{:S(2)}) collective-permute-start(bf16[2,2,32,256]{3,2,1,0:T(8,128)(2,1)S(1)} %get-tuple-element.43), channel_id=1, source_target_pairs={{1,0},{2,1},{3,2},{4,3},{5,4},{6,5},{7,6},{9,8},{10,9},{11,10},{12... | collective-permute-start | bytes 196616 | tf_op jit(solution)/shard_map/ppermute | solution.py:481
  55.7 2.5 %copy-start = (bf16[8,2,8,160,128]{4,3,2,1,0:T(8,128)(2,1)S(1)}, bf16[8,2,8,160,128]{4,3,2,1,0:T(8,128)(2,1)}, u32[]{:S(2)}) copy-start(bf16[8,2,8,160,128]{4,3,2,1,0:T(8,128)(2,1)} %get-tuple-element.45.q_ref) | copy-start | bytes 15728644
  58.2 11.1 %copy-start.1 = (bf16[8,2,8,160,128]{4,3,2,1,0:T(8,128)(2,1)S(1)}, bf16[8,2,8,160,128]{4,3,2,1,0:T(8,128)(2,1)}, u32[]{:S(2)}) copy-start(bf16[8,2,8,160,128]{4,3,2,1,0:T(8,128)(2,1)} %get-tuple-element.45.q_ref) | copy-start | bytes 15728644
  62.2 7.1 %collective-permute-start.8 = (bf16[2,5,32,256]{3,2,1,0:T(8,128)(2,1)S(1)}, bf16[2,5,32,256]{3,2,1,0:T(8,128)(2,1)S(1)}, u32[]{:S(2)}, u32[]{:S(2)}) collective-permute-start(bf16[2,5,32,256]{3,2,1,0:T(8,128)(2,1)S(1)} %pad_maximum_fusion.3), channel_id=1, source_target_pairs={{8,0},{9,1},{10,2},{11,3},{12,4},{13,5},{14,6},{15,7},{16,8},{17,9... | collective-permute-start | bytes 491528 | tf_op jit(solution)/shard_map/ppermute | solution.py:481
  69.3 5.0 %collective-permute-start.9 = (bf16[8,8,64,128]{3,2,1,0:T(8,128)(2,1)S(1)}, bf16[8,8,64,128]{3,2,1,0:T(8,128)(2,1)S(1)}, u32[]{:S(2)}, u32[]{:S(2)}) collective-permute-start(bf16[8,8,64,128]{3,2,1,0:T(8,128)(2,1)S(1)} %get-tuple-element.50), channel_id=1, source_target_pairs={{0,8},{8,0},{1,9},{9,1},{2,10},{10,2},{3,11},{11,3},{4,12},{12,4},... | collective-permute-start | bytes 3145736 | tf_op jit(solution)/shard_map/ppermute | solution.py:469
  72.5 1.7 %collective-permute-start.10 = (bf16[8,8,16,128]{3,2,1,0:T(8,128)(2,1)S(1)}, bf16[8,8,16,128]{3,2,1,0:T(8,128)(2,1)S(1)}, u32[]{:S(2)}, u32[]{:S(2)}) collective-permute-start(bf16[8,8,16,128]{3,2,1,0:T(8,128)(2,1)S(1)} %get-tuple-element.54), channel_id=1, source_target_pairs={{0,8},{8,0},{1,9},{9,1},{2,10},{10,2},{3,11},{11,3},{4,12},{12,4},... | collective-permute-start | bytes 786440 | tf_op jit(solution)/shard_map/ppermute | solution.py:469
  108.1 12.3 %all-to-all-start.2 = ((bf16[8,144,128]{2,1,0:T(8,128)(2,1)}), bf16[8,144,128]{2,1,0:T(8,128)(2,1)S(1)}, u32[]{:S(2)}, u32[]{:S(2)}) async-start(bf16[8,144,128]{2,1,0:T(8,128)(2,1)} %pad_maximum_fusion.1), calls=%async_computation.2 | async-start | bytes 589824 | tf_op jit(solution)/shard_map/all_to_all | solution.py:456
  129.7 6.0 %collective-permute-start.11 = (bf16[8,192,128]{2,1,0:T(8,128)(2,1)S(1)}, bf16[8,192,128]{2,1,0:T(8,128)(2,1)S(1)}, u32[]{:S(2)}, u32[]{:S(2)}) collective-permute-start(bf16[8,192,128]{2,1,0:T(8,128)(2,1)S(1)} %all_to_all.21), channel_id=1, source_target_pairs={{0,8},{8,0},{1,9},{9,1},{2,10},{10,2},{3,11},{11,3},{4,12},{12,4},... | collective-permute-start | bytes 1179656 | tf_op jit(solution)/shard_map/ppermute | solution.py:518

commit v5 on v4

--- a/solution.py
+++ b/solution.py
@@ -98,10 +98,11 @@
     )(core, own, parts)
 
 
-def field_tile(q_ref, qd_ref, qr_ref, a, b, t, u, v):
+def field_tile(q_ref, qd_ref, qr_ref, corner_ref, a, b, t, u, v):
     d = 2 * a + t - 1
     if d < 0:
-        ref = qd_ref.at[(b, 9 + b, b + 1)[u]]
+        at = (b, 9 + b, b + 1)[u]
+        ref = corner_ref if at == 0 and corner_ref is not None else qd_ref.at[at]
     elif u == 0:
         ref = q_ref.at[d, 1, b - 1] if b else qr_ref.at[d]
     else:
@@ -112,12 +113,12 @@
 
 
 def field_rows(q_ref, qd_ref, qr_ref, a, t, u, v):
-    return jnp.concatenate([field_tile(q_ref, qd_ref, qr_ref, a, b, t, u, v) for b in range(8)], 0)
+    return jnp.concatenate([field_tile(q_ref, qd_ref, qr_ref, None, a, b, t, u, v) for b in range(8)], 0)
 
 
 def first_kernel(
-    x_ref, xd_ref, xr_ref, xc_ref, sel_ref, k_ref,
-    h_ref, q_out, qd_ref, qr_ref, last_ref, side_ref, end_ref,
+    x_ref, xd_ref, xr_ref, sel_ref, k_ref,
+    h_ref, q_out, qd_ref, qr_ref, last_ref, side_ref, end_ref, open_ref,
     x_slabs, q_ref, w_ref, wide, came, went,
 ):
     def load(d):
@@ -129,7 +130,8 @@
     for d in range(8):
         load(d).start()
     sel = sel_ref[...]
-    qd_ref[0] = spread(sel, xc_ref[...])
+    qd_ref[0] = jnp.zeros((160, 128), BF)
+    last_ref[8] = jnp.concatenate([xr_ref[7, 0:64], xr_ref[7, 64:128]], 1)
     for k in range(16):
         qd_ref[k + 1] = spread(sel, xd_ref[k])
     for k in range(8):
@@ -156,26 +158,29 @@
         h_ref[a] = out
         side_ref[a] = out[7]
         if a == 3:
-            last_ref[...] = out
+            last_ref[0:8] = out
             end_ref[...] = out[7]
+        if a == 0:
+            open_ref[...] = pre[0:64]
     for d in range(8):
         store(d).wait()
 
 
-def first(x, xd, xr, xc, sel, kernel):
+def first(x, xd, xr, sel, kernel):
     anywhere = pl.BlockSpec(memory_space=pl.ANY)
     return pl.pallas_call(
         first_kernel,
-        in_specs=[anywhere] + vmem(5),
-        out_specs=vmem(1) + [anywhere] + vmem(5),
+        in_specs=[anywhere] + vmem(4),
+        out_specs=vmem(1) + [anywhere] + vmem(6),
         out_shape=(
             jax.ShapeDtypeStruct((4, 8, 64, 256), BF),
             jax.ShapeDtypeStruct((8, 2, 8, 160, 128), BF),
             jax.ShapeDtypeStruct((17, 160, 128), BF),
             jax.ShapeDtypeStruct((8, 160, 128), BF),
-            jax.ShapeDtypeStruct((8, 64, 256), BF),
+            jax.ShapeDtypeStruct((9, 64, 256), BF),
             jax.ShapeDtypeStruct((4, 64, 256), BF),
             jax.ShapeDtypeStruct((64, 256), BF),
+            jax.ShapeDtypeStruct((64, 256), F32),
         ),
         scratch_shapes=[
             pltpu.VMEM((8, 2, 64, 16, 128), BF),
@@ -188,7 +193,7 @@
         compiler_params=params(54),
         cost_estimate=cost(60, 200),
         name="first_layer",
-    )(x, xd, xr, xc, sel, kernel)
+    )(x, xd, xr, sel, kernel)
 
 
 def hidden_part(h_ref, hd_ref, hr_ref, hc_ref, a, b):
@@ -249,8 +254,20 @@
 
 
 def second_kernel(
-    core_ref, h_ref, hd_ref, hr_ref, hc_ref, m_ref, o_ref, act_ref, delta_ref, turned_ref, last_ref, side_ref, w_ref, hs_ref
+    core_ref, h_in, hd_ref, hr_ref, hc_ref, m_ref, o_ref, sel_ref, k_ref, open_ref,
+    act_ref, delta_ref, turned_ref, last_ref, side_ref, h_ref, corner_ref, w_ref, hs_ref,
 ):
+    corner = spread(sel_ref[...], jnp.concatenate([hd_ref[8, :, 0:128], hd_ref[8, :, 128:256]], 0))
+    corner_ref[...] = corner
+    taps = jnp.concatenate([jnp.concatenate([corner[0:32], corner[96:128]], 0), corner[32:96], corner[96:160]], 1)
+    nothing = jnp.zeros((64, 128), BF)
+    spaced = []
+    for k in range(3):
+        spaced.append(jnp.concatenate([k_ref[k], nothing], 1))
+        spaced.append(jnp.concatenate([nothing, k_ref[k]], 1))
+    pre = open_ref[...] + dot(taps, jnp.concatenate(spaced, 0))
+    h_ref[...] = h_in[...]
+    h_ref[0, 0] = jnp.where(pre > 0, pre, 0.3 * pre).astype(BF)
     parts = (h_ref, hd_ref, hr_ref, hc_ref)
     hidden_shifts(parts, hs_ref)
     whole_weight(core_ref, m_ref, o_ref, w_ref)
@@ -277,23 +294,25 @@
             turned_ref[:, rows] = dot(large, delta, LANES).astype(BF)
 
 
-def second(core, h, hd, hr, hc, mine, other):
+def second(core, h, hd, hr, hc, mine, other, sel, kernel, partial):
     return pl.pallas_call(
         second_kernel,
-        in_specs=[SCALAR] + vmem(6),
-        out_specs=vmem(5),
+        in_specs=[SCALAR] + vmem(9),
+        out_specs=vmem(7),
         out_shape=(
             jax.ShapeDtypeStruct((8, 128, 128), BF),
             jax.ShapeDtypeStruct((2, 2, 4, 32, 256), BF),
             jax.ShapeDtypeStruct((256, 512), BF),
             jax.ShapeDtypeStruct((2, 4, 32, 256), BF),
             jax.ShapeDtypeStruct((2, 2, 32, 256), BF),
+            jax.ShapeDtypeStruct((4, 8, 64, 256), BF),
+            jax.ShapeDtypeStruct((160, 128), BF),
         ),
         scratch_shapes=[WEIGHT, pltpu.VMEM((5, 9, 32, 256), BF)],
         compiler_params=params(16),
         cost_estimate=cost(1, 4),
         name="second_layer",
-    )(core, h, hd, hr, hc, mine, other)
+    )(core, h, hd, hr, hc, mine, other, sel, kernel, partial)
 
 
 def second_grad_kernel(core_ref, h_ref, hd_ref, hr_ref, hc_ref, turned_ref, keep_ref, send_ref, hs_ref):
@@ -385,7 +404,9 @@
         yield k, jnp.where(lane < 64, one, two).T
 
 
-def inner_kernel(core_ref, d_ref, m_ref, o_ref, h_ref, q_ref, qd_ref, qr_ref, out_ref, w_ref, ds_ref, one_ref):
+def inner_kernel(
+    core_ref, d_ref, m_ref, o_ref, h_ref, q_ref, qd_ref, qr_ref, corner_ref, out_ref, w_ref, ds_ref, one_ref
+):
     whole_weight(core_ref, m_ref, o_ref, w_ref)
     for n in range(2):
         for a in range(2):
@@ -393,21 +414,21 @@
                 ds_ref[n, a, b] = shift_rows(d_ref[n, a, b], -1)
     parts = (d_ref, None, None)
     back_rows(parts, ds_ref, w_ref, h_ref, one_ref, INNER)
-    for k, rows in grad_rows(one_ref, (q_ref, qd_ref, qr_ref), INNER):
+    for k, rows in grad_rows(one_ref, (q_ref, qd_ref, qr_ref, corner_ref), INNER):
         out_ref[k // 2] = rows
 
 
-def inner(core, d, mine, other, h, q, qd, qr):
+def inner(core, d, mine, other, h, q, qd, qr, corner):
     return pl.pallas_call(
         inner_kernel,
-        in_specs=[SCALAR] + vmem(7),
+        in_specs=[SCALAR] + vmem(8),
         out_specs=vmem(1)[0],
         out_shape=jax.ShapeDtypeStruct((14, 128, 128), F32),
         scratch_shapes=[WEIGHT, pltpu.VMEM((2, 2, 4, 32, 256), BF), pltpu.VMEM((len(INNER), 64, 256), BF)],
         compiler_params=params(16),
         cost_estimate=cost(4, 9),
         name="first_kernel_grad_inner",
-    )(core, d, mine, other, h, q, qd, qr)
+    )(core, d, mine, other, h, q, qd, qr, corner)
 
 
 def outer_kernel(
@@ -422,7 +443,7 @@
                 ds_ref[n, a, b] = shift_rows(delta_part(*parts, n, a, b)[...], -1)
     back_rows(parts, ds_ref, w_ref, h_ref, one_ref, OUTER)
     even = core_ref[0] == 0
-    for k, rows in grad_rows(one_ref, (q_ref, qd_ref, qr_ref), OUTER):
+    for k, rows in grad_rows(one_ref, (q_ref, qd_ref, qr_ref, None), OUTER):
         rows = rows + sum_ref[k // 2]
         for j in range(4):
             low, high = rows[32 * j : 32 * j + 16], rows[32 * j + 16 : 32 * j + 32]
@@ -491,18 +512,20 @@
     side, last = rims_of(inputs)
     xr = shifted(side, 0, 1)
     xd = shifted(last, 1, 0)
-    xc = shifted(last[7], 1, 1)
     mixed, _ = lax.optimization_barrier((mixed, last))
     mixed = exchange(mixed, FILT)
-    h, q, qd, qr, last, side, end = first(inputs, xd, xr, xc, sel, kernel_one.reshape(27, 64, 128))
+    taps = kernel_one.reshape(27, 64, 128)
+    h, q, qd, qr, last, side, end, partial = first(inputs, xd, xr, sel, taps)
     mixed, end = lax.optimization_barrier((mixed, end))
     other = lax.ppermute(mixed, "core", [(0, 1), (1, 0)])
     hr = shifted(side, 0, 1)
     hd = shifted(last, 1, 0)
     hc = shifted(end, 1, 1)
-    act, delta, turned, last, side = second(core, h, hd, hr, hc, mixed, other)
+    act, delta, turned, last, side, h, corner = second(
+        core, h, hd, hr, hc, mixed, other, sel, taps[:3], partial
+    )
     dr = shifted(side, 0, -1)
-    partial = inner(core, delta, mixed, other, h, q, qd, qr)
+    partial = inner(core, delta, mixed, other, h, q, qd, qr, corner)
     dr, partial = lax.optimization_barrier((dr, partial))
     dd = shifted(jnp.concatenate([last, dr[:, :1]], 1), -1, 0)
     two = second_grad(core, h, hd, hr, hc, turned)

time: 138 us -> 137 us (level)
  starting transfers between devices: 39.1 us -> 36.8 us
  local copies, waits for them, and re-layouts: 8.18 us -> 9.83 us
    ppermute x8 -> x7, starting transfers between devices: 23.4 us -> 20.5 us  [shifted(): return lax.ppermute(value, SPACE + FILT, pairs)]
    unnamed x22 -> x24, local copies, waits for them, and re-layouts: 6.8 us -> 7.65 us
    ppermute x8 -> x7, waiting for transfers between devices: 4.39 us -> 3.7 us  [shifted(): return lax.ppermute(value, SPACE + FILT, pairs)]
  transfers between devices with their start and end apart: 14 -> 13, of which waited for: 7 -> 6; matrix products, arithmetic and copies ran while one was open for 1% -> 2% of each run, Pallas kernels for 15% -> 15%
where the time goes in v5:
time: 137 us; the launch traced here: 136 us
  blocking collectives  41.7 us (30%)
  starting transfers between devices  36.8 us (27%)
  Pallas kernels  24.5 us (18%)
  waiting for transfers between devices  19 us (14%)
  local copies, waits for them, and re-layouts  9.83 us (7%)
  other arithmetic  3.48 us (3%)
    all_to_all x2, blocking collectives, exchange(): return lax.all_to_all(value, axes, 0, 0, tiled=True)  41.7 us
    ppermute x7, starting transfers between devices, shifted(): return lax.ppermute(value, SPACE + FILT, pairs)  20.5 us
    all_to_all x2, waiting for transfers between devices, exchange(): return lax.all_to_all(value, axes, 0, 0, tiled=True)  13.7 us
    pallas_call x1, Pallas kernels, first(): pl.pallas_call(first_kernel, in_specs=[anywhere] + vmem(4), out_specs=vme...  11.1 us
    all_to_all x2, starting transfers between devices, exchange(): return lax.all_to_all(value, axes, 0, 0, tiled=True)  10.7 us
    unnamed x24, local copies, waits for them, and re-layouts  7.65 us
    ppermute x1, starting transfers between devices, body(): other = lax.ppermute(mine, 'core', [(0, 1), (1, 0)])  4.62 us
    pallas_call x1, Pallas kernels, inner(): pl.pallas_call(inner_kernel, in_specs=[SCALAR] + vmem(8), out_specs=vmem(...  3.98 us
  transfers between devices with their start and end apart: 13, of which 6 were waited for; matrix products, arithmetic and copies ran while one was open for 2% of the time, Pallas kernels for 15%

profile of v5, /device:TPU:1, one launch (start us, length us, event | category | flops | bytes accessed | tf_op | source)
XLA Modules:
  0.0 136.3 jit_solution(16381352071384220868)
XLA Ops:
  0.6 0.0 copy-start.2
  0.6 2.2 %copy-done.2 = bf16[2,64,8,16,128]{4,3,2,1,0:T(8,128)(2,1)S(1)} copy-done((bf16[2,64,8,16,128]{4,3,2,1,0:T(8,128)(2,1)S(1)}, bf16[2,64,8,16,128]{4,3,2,1,0:T(8,128)(2,1)}, u32[]{:S(2)}) %copy-start.2) | copy-done | bytes 4194328
  2.8 0.9 input_rims.1
  3.7 4.9 %collective-permute-start = (bf16[16,128,128]{2,1,0:T(8,128)(2,1)S(1)}, bf16[16,128,128]{2,1,0:T(8,128)(2,1)S(1)}, u32[]{:S(2)}, u32[]{:S(2)}) collective-permute-start(bf16[16,128,128]{2,1,0:T(8,128)(2,1)S(1)} %get-tuple-element.32), channel_id=1, source_target_pairs={{0,8},{1,9},{2,10},{3,11},{4,12},{5,13},{6,14},{7,15},{8,16},{9,17... | collective-permute-start | bytes 1572872 | tf_op jit(solution)/shard_map/ppermute | solution.py:502
  8.7 3.1 %collective-permute-start.1 = (bf16[8,128,128]{2,1,0:T(8,128)(2,1)S(1)}, bf16[8,128,128]{2,1,0:T(8,128)(2,1)S(1)}, u32[]{:S(2)}, u32[]{:S(2)}) collective-permute-start(bf16[8,128,128]{2,1,0:T(8,128)(2,1)S(1)} %get-tuple-element.33), channel_id=1, source_target_pairs={{0,1},{1,2},{2,3},{3,4},{4,5},{5,6},{6,7},{8,9},{9,10},{10,11},{11... | collective-permute-start | bytes 786440 | tf_op jit(solution)/shard_map/ppermute | solution.py:502
  11.8 0.0 copy-done.9
  11.8 0.2 reshape.56
  12.0 0.1 copy.13
  12.1 1.1 weights_and_cotangent.1
  13.2 6.3 %all-to-all-start = ((bf16[8,560,128]{2,1,0:T(8,128)(2,1)}), bf16[8,560,128]{2,1,0:T(8,128)(2,1)S(1)}, u32[]{:S(2)}, u32[]{:S(2)}) async-start(bf16[8,560,128]{2,1,0:T(8,128)(2,1)} %weights_and_cotangent.1), calls=%async_computation | async-start | bytes 2293760 | tf_op jit(solution)/shard_map/all_to_all | solution.py:477
  19.5 0.0 collective-permute-done.1.xr_ref
  19.5 0.0 copy-start.11
  19.6 0.0 collective-permute-done.xd_ref
  19.6 0.7 copy-done.11
  20.2 0.2 copy-done.10
  20.5 11.1 %first_layer.1 = (bf16[4,8,64,256]{3,2,1,0:T(8,128)(2,1)}, bf16[8,2,8,160,128]{4,3,2,1,0:T(8,128)(2,1)}, bf16[17,160,128]{2,1,0:T(8,128)(2,1)}, bf16[8,160,128]{...) custom-call(bf16[2,64,8,16,128]{4,3,2,1,0:T(8,128)(2,1)} %x_ref.3, ...), custom_call_target="tpu_custom_call" | custom-call | flops 64424509440 | bytes 209715200 | tf_op jit(solution)/shard_map/first_layer/pallas_call | solution.py:171
  31.6 0.0 copy-start.3
  31.6 0.0 copy-start.4
  31.6 5.8 %all-to-all-done.m_ref = bf16[8,560,128]{2,1,0:T(8,128)(2,1)S(1)} async-done(((bf16[8,560,128]{2,1,0:T(8,128)(2,1)}), bf16[8,560,128]{2,1,0:T(8,128)(2,1)S(1)}, u32[]{:S(2)}, u32[]{:S(2)}) %all-to-all-start) | async-done | bytes 1146912 | tf_op jit(solution)/shard_map/all_to_all | solution.py:477
  37.4 0.3 collective-permute-start.5
  37.8 3.7 %collective-permute-start.2 = (bf16[9,64,256]{2,1,0:T(8,128)(2,1)}, bf16[9,64,256]{2,1,0:T(8,128)(2,1)S(1)}, u32[]{:S(2)}, u32[]{:S(2)}) collective-permute-start(bf16[9,64,256]{2,1,0:T(8,128)(2,1)} %get-tuple-element.35), channel_id=1, source_target_pairs={{0,8},{1,9},{2,10},{3,11},{4,12},{5,13},{6,14},{7,15},{8,16},{9,17... | collective-permute-start | bytes 884744 | tf_op jit(solution)/shard_map/ppermute | solution.py:502
  41.5 2.5 %collective-permute-start.3 = (bf16[4,64,256]{2,1,0:T(8,128)(2,1)}, bf16[4,64,256]{2,1,0:T(8,128)(2,1)S(1)}, u32[]{:S(2)}, u32[]{:S(2)}) collective-permute-start(bf16[4,64,256]{2,1,0:T(8,128)(2,1)} %get-tuple-element.36), channel_id=1, source_target_pairs={{0,1},{1,2},{2,3},{3,4},{4,5},{5,6},{6,7},{8,9},{9,10},{10,11},{11... | collective-permute-start | bytes 393224 | tf_op jit(solution)/shard_map/ppermute | solution.py:502
  44.0 2.2 %collective-permute-start.4 = (bf16[64,256]{1,0:T(8,128)(2,1)}, bf16[64,256]{1,0:T(8,128)(2,1)S(1)}, u32[]{:S(2)}, u32[]{:S(2)}) collective-permute-start(bf16[64,256]{1,0:T(8,128)(2,1)} %get-tuple-element.39), channel_id=1, source_target_pairs={{0,9},{1,10},{2,11},{3,12},{4,13},{5,14},{6,15},{8,17},{9,18},{10,... | collective-permute-start | bytes 98312 | tf_op jit(solution)/shard_map/ppermute | solution.py:502
  46.2 0.8 slice.40.k_ref
  47.0 0.0 collective-permute-done.3.hr_ref
  47.0 0.0 collective-permute-done.2.hd_ref
  47.0 0.5 collective-permute-done.4.hc_ref
  47.6 0.0 collective-permute-done.5.o_ref
  47.6 1.2 copy-done.7
  48.8 0.8 copy-done.8
  49.6 2.9 %second_layer.1 = (bf16[8,128,128]{2,1,0:T(8,128)(2,1)S(1)}, bf16[2,2,4,32,256]{4,3,2,1,0:T(8,128)(2,1)S(1)}, bf16[256,512]{1,0:T(8,128)(2,1)S(1)}, bf16[2,4,32,...) custom-call(s32[1]{0:T(128)} %bitcast.core_ref, ...), custom_call_target="tpu_custom_call" | custom-call | flops 1073741824 | bytes 4194304 | tf_op jit(solution)/shard_map/second_layer/pallas_call | solution.py:298
  52.5 1.3 collective-permute-start.6
  53.8 0.0 copy-done.3
  53.9 0.0 copy-done.4
  53.9 0.0 copy-start
  53.9 2.5 %copy-done = bf16[8,2,8,160,128]{4,3,2,1,0:T(8,128)(2,1)S(1)} copy-done((bf16[8,2,8,160,128]{4,3,2,1,0:T(8,128)(2,1)S(1)}, bf16[8,2,8,160,128]{4,3,2,1,0:T(8,128)(2,1)}, u32[]{:S(2)}) %copy-start) | copy-done | bytes 5242904
  56.4 4.0 %first_kernel_grad_inner.1.sum_ref = f32[14,128,128]{2,1,0:T(8,128)S(1)} custom-call(s32[1]{0:T(128)} %bitcast.core_ref, bf16[2,2,4,32,256]{4,3,2,1,0:T(8,128)(2,1)S(1)} %get-tuple-element.49.d_ref, bf16[8,560,128]{2,1,0:T(8,128)(2,1)S(1)} %all-to-all-done.m_ref, bf16[8,560,128]{2,1,0:T(8,128)(2,1)S(1)} %collective-permute-done.5.o_ref, ...), custom_call_target="tpu_custom_call" | custom-call | flops 4294967296 | bytes 9437184 | tf_op jit(solution)/shard_map/first_kernel_grad_inner/pallas_call | solution.py:422
  60.3 0.0 collective-permute-done.6.dr_ref
  60.4 2.7 %collective-permute-start.7 = (bf16[2,5,32,256]{3,2,1,0:T(8,128)(2,1)S(1)}, bf16[2,5,32,256]{3,2,1,0:T(8,128)(2,1)S(1)}, u32[]{:S(2)}, u32[]{:S(2)}) collective-permute-start(bf16[2,5,32,256]{3,2,1,0:T(8,128)(2,1)S(1)} %pad_maximum_fusion.3), channel_id=1, source_target_pairs={{8,0},{9,1},{10,2},{11,3},{12,4},{13,5},{14,6},{15,7},{16,8},{17,9... | collective-permute-start | bytes 491528 | tf_op jit(solution)/shard_map/ppermute | solution.py:502
  63.1 1.2 second_kernel_grad.1
  64.4 3.2 %collective-permute-done.7.dd_ref = bf16[2,5,32,256]{3,2,1,0:T(8,128)(2,1)S(1)} collective-permute-done((bf16[2,5,32,256]{3,2,1,0:T(8,128)(2,1)S(1)}, bf16[2,5,32,256]{3,2,1,0:T(8,128)(2,1)S(1)}, u32[]{:S(2)}, u32[]{:S(2)}) %collective-permute-start.7) | collective-permute-done | bytes 163872 | tf_op jit(solution)/shard_map/ppermute | solution.py:502
  67.6 0.0 collective-permute-start.8
  67.6 3.2 %first_kernel_grad.1 = (bf16[8,8,16,128]{3,2,1,0:T(8,128)(2,1)S(1)}, bf16[8,8,16,128]{3,2,1,0:T(8,128)(2,1)S(1)}) custom-call(s32[1]{0:T(128)} %bitcast.core_ref, bf16[2,2,4,32,256]{4,3,2,1,0:T(8,128)(2,1)S(1)} %get-tuple-element.49.d_ref, bf16[2,5,32,256]{3,2,1,0:T(8,128)(2,1)S(1)} %collective-permute-done.7.dd_ref, ...), custom_call_target="tpu_custom_call" | custom-call | flops 2147483648 | bytes 9437184 | tf_op jit(solution)/shard_map/first_kernel_grad/pallas_call | solution.py:458
  70.8 0.6 collective-permute-start.9
  71.4 1.2 collective-permute-done.9
  72.5 0.1 add_convert_fusion.1
  72.6 0.0 collective-permute-done.8
  72.6 0.4 add_convert_fusion
  73.0 0.1 pad_maximum_fusion
  73.1 32.5 %all_to_all.20 = bf16[64,80,128]{2,1,0:T(8,128)(2,1)S(1)} all-to-all(bf16[64,80,128]{2,1,0:T(8,128)(2,1)S(1)} %bitcast.37), channel_id=1, replica_groups=mesh['y_lo'=2,'z'=4,'core'=2,'y_hi'=2,'x'=4] {'y_lo','z','y_hi','x'}, dimensions={0} | all-to-all | bytes 2621440 | tf_op jit(solution)/shard_map/all_to_all | solution.py:477
  105.6 0.2 reduce_sum.12
  105.8 0.7 pad_maximum_fusion.1
  106.6 4.4 %all-to-all-start.2 = ((bf16[8,144,128]{2,1,0:T(8,128)(2,1)}), bf16[8,144,128]{2,1,0:T(8,128)(2,1)S(1)}, u32[]{:S(2)}, u32[]{:S(2)}) async-start(bf16[8,144,128]{2,1,0:T(8,128)(2,1)} %pad_maximum_fusion.1), calls=%async_computation.2 | async-start | bytes 589824 | tf_op jit(solution)/shard_map/all_to_all | solution.py:477
  110.9 8.0 %all-to-all-done.2 = bf16[8,144,128]{2,1,0:T(8,128)(2,1)S(1)} async-done(((bf16[8,144,128]{2,1,0:T(8,128)(2,1)}), bf16[8,144,128]{2,1,0:T(8,128)(2,1)S(1)}, u32[]{:S(2)}, u32[]{:S(2)}) %all-to-all-start.2) | async-done | bytes 294944 | tf_op jit(solution)/shard_map/all_to_all | solution.py:477
  118.9 0.1 broadcast_in_dim.5
  119.0 9.2 %all_to_all.21 = bf16[8,192,128]{2,1,0:T(8,128)(2,1)S(1)} all-to-all(bf16[8,192,128]{2,1,0:T(8,128)(2,1)S(1)} %broadcast_in_dim.5), channel_id=1, replica_groups=mesh['y_lo'=2,'z'=4,'core'=2,'y_hi'=2,'x'=4] {'y_lo','z'}, dimensions={0} | all-to-all | bytes 786432 | tf_op jit(solution)/shard_map/all_to_all | solution.py:477
  128.2 4.6 %collective-permute-start.10 = (bf16[8,192,128]{2,1,0:T(8,128)(2,1)S(1)}, bf16[8,192,128]{2,1,0:T(8,128)(2,1)S(1)}, u32[]{:S(2)}, u32[]{:S(2)}) collective-permute-start(bf16[8,192,128]{2,1,0:T(8,128)(2,1)S(1)} %all_to_all.21), channel_id=1, source_target_pairs={{0,8},{8,0},{1,9},{9,1},{2,10},{10,2},{3,11},{11,3},{4,12},{12,4},... | collective-permute-start | bytes 1179656 | tf_op jit(solution)/shard_map/ppermute | solution.py:541
  132.9 0.2 copy.14
  133.0 0.8 reshape.60
  133.8 0.4 collective-permute-done.10
  134.2 0.1 select_bitcast_fusion
  134.2 0.1 fusion
  134.4 1.0 convert.4
  135.5 0.8 convert_bitcast_fusion
  (23 shorter events, 0.2 us)
Async XLA Ops:
  0.6 2.2 %copy-start.2 = (bf16[2,64,8,16,128]{4,3,2,1,0:T(8,128)(2,1)S(1)}, bf16[2,64,8,16,128]{4,3,2,1,0:T(8,128)(2,1)}, u32[]{:S(2)}) copy-start(bf16[2,64,8,16,128]{4,3,2,1,0:T(8,128)(2,1)} %x_ref.3) | copy-start | bytes 12582916
  2.8 9.0 %copy-start.9 = (bf16[2,32,2,1024]{3,2,1,0:T(2,128)(2,1)S(1)}, bf16[2,32,2,1024]{3,2,1,0:T(2,128)(2,1)}, u32[]{:S(2)}) copy-start(bf16[2,32,2,1024]{3,2,1,0:T(2,128)(2,1)} %param.8) | copy-start | bytes 786436
  2.8 9.2 %copy-start.5 = (bf16[3,3,3,128,32]{3,4,2,1,0:T(8,128)(2,1)S(1)}, bf16[3,3,3,128,32]{3,4,2,1,0:T(8,128)(2,1)}, u32[]{:S(2)}) copy-start(bf16[3,3,3,128,32]{3,4,2,1,0:T(8,128)(2,1)} %param.7) | copy-start | bytes 663556
  3.7 15.8 %collective-permute-start = (bf16[16,128,128]{2,1,0:T(8,128)(2,1)S(1)}, bf16[16,128,128]{2,1,0:T(8,128)(2,1)S(1)}, u32[]{:S(2)}, u32[]{:S(2)}) collective-permute-start(bf16[16,128,128]{2,1,0:T(8,128)(2,1)S(1)} %get-tuple-element.32), channel_id=1, source_target_pairs={{0,8},{1,9},{2,10},{3,11},{4,12},{5,13},{6,14},{7,15},{8,16},{9,17... | collective-permute-start | bytes 1572872 | tf_op jit(solution)/shard_map/ppermute | solution.py:502
  8.7 10.9 %collective-permute-start.1 = (bf16[8,128,128]{2,1,0:T(8,128)(2,1)S(1)}, bf16[8,128,128]{2,1,0:T(8,128)(2,1)S(1)}, u32[]{:S(2)}, u32[]{:S(2)}) collective-permute-start(bf16[8,128,128]{2,1,0:T(8,128)(2,1)S(1)} %get-tuple-element.33), channel_id=1, source_target_pairs={{0,1},{1,2},{2,3},{3,4},{4,5},{5,6},{6,7},{8,9},{9,10},{10,11},{11... | collective-permute-start | bytes 786440 | tf_op jit(solution)/shard_map/ppermute | solution.py:502
  13.2 24.2 %all-to-all-start = ((bf16[8,560,128]{2,1,0:T(8,128)(2,1)}), bf16[8,560,128]{2,1,0:T(8,128)(2,1)S(1)}, u32[]{:S(2)}, u32[]{:S(2)}) async-start(bf16[8,560,128]{2,1,0:T(8,128)(2,1)} %weights_and_cotangent.1), calls=%async_computation | async-start | bytes 2293760 | tf_op jit(solution)/shard_map/all_to_all | solution.py:477
  19.5 0.7 copy-start.11
  19.6 0.9 copy-start.10
  20.5 27.1 %copy-start.6 = (bf16[160,128]{1,0:T(8,128)(2,1)S(1)}, bf16[160,128]{1,0:T(8,128)(2,1)}, u32[]{:S(2)}) copy-start(bf16[160,128]{1,0:T(8,128)(2,1)} %constant.13.clone.sel_ref) | copy-start | bytes 122884
  31.6 22.2 %copy-start.3 = (bf16[17,160,128]{2,1,0:T(8,128)(2,1)S(1)}, bf16[17,160,128]{2,1,0:T(8,128)(2,1)}, u32[]{:S(2)}) copy-start(bf16[17,160,128]{2,1,0:T(8,128)(2,1)} %get-tuple-element.51.qd_ref) | copy-start | bytes 2088964
  31.6 22.2 %copy-start.4 = (bf16[8,160,128]{2,1,0:T(8,128)(2,1)S(1)}, bf16[8,160,128]{2,1,0:T(8,128)(2,1)}, u32[]{:S(2)}) copy-start(bf16[8,160,128]{2,1,0:T(8,128)(2,1)} %get-tuple-element.52.qr_ref) | copy-start | bytes 983044
  37.4 10.1 %collective-permute-start.5 = (bf16[8,560,128]{2,1,0:T(8,128)(2,1)S(1)}, bf16[8,560,128]{2,1,0:T(8,128)(2,1)S(1)}, u32[]{:S(2)}, u32[]{:S(2)}) collective-permute-start(bf16[8,560,128]{2,1,0:T(8,128)(2,1)S(1)} %all-to-all-done.m_ref), channel_id=1, source_target_pairs={{0,8},{8,0},{1,9},{9,1},{2,10},{10,2},{3,11},{11,3},{4,12},{12,4},... | collective-permute-start | bytes 3440648 | tf_op jit(solution)/shard_map/ppermute | solution.py:520
  37.8 9.3 %collective-permute-start.2 = (bf16[9,64,256]{2,1,0:T(8,128)(2,1)}, bf16[9,64,256]{2,1,0:T(8,128)(2,1)S(1)}, u32[]{:S(2)}, u32[]{:S(2)}) collective-permute-start(bf16[9,64,256]{2,1,0:T(8,128)(2,1)} %get-tuple-element.35), channel_id=1, source_target_pairs={{0,8},{1,9},{2,10},{3,11},{4,12},{5,13},{6,14},{7,15},{8,16},{9,17... | collective-permute-start | bytes 884744 | tf_op jit(solution)/shard_map/ppermute | solution.py:502
  41.5 5.5 %collective-permute-start.3 = (bf16[4,64,256]{2,1,0:T(8,128)(2,1)}, bf16[4,64,256]{2,1,0:T(8,128)(2,1)S(1)}, u32[]{:S(2)}, u32[]{:S(2)}) collective-permute-start(bf16[4,64,256]{2,1,0:T(8,128)(2,1)} %get-tuple-element.36), channel_id=1, source_target_pairs={{0,1},{1,2},{2,3},{3,4},{4,5},{5,6},{6,7},{8,9},{9,10},{10,11},{11... | collective-permute-start | bytes 393224 | tf_op jit(solution)/shard_map/ppermute | solution.py:502
  44.0 3.6 %collective-permute-start.4 = (bf16[64,256]{1,0:T(8,128)(2,1)}, bf16[64,256]{1,0:T(8,128)(2,1)S(1)}, u32[]{:S(2)}, u32[]{:S(2)}) collective-permute-start(bf16[64,256]{1,0:T(8,128)(2,1)} %get-tuple-element.39), channel_id=1, source_target_pairs={{0,9},{1,10},{2,11},{3,12},{4,13},{5,14},{6,15},{8,17},{9,18},{10,... | collective-permute-start | bytes 98312 | tf_op jit(solution)/shard_map/ppermute | solution.py:502
  47.6 1.2 copy-start.7
  48.8 0.8 copy-start.8
  52.5 7.8 %collective-permute-start.6 = (bf16[2,2,32,256]{3,2,1,0:T(8,128)(2,1)S(1)}, bf16[2,2,32,256]{3,2,1,0:T(8,128)(2,1)S(1)}, u32[]{:S(2)}, u32[]{:S(2)}) collective-permute-start(bf16[2,2,32,256]{3,2,1,0:T(8,128)(2,1)S(1)} %get-tuple-element.48), channel_id=1, source_target_pairs={{1,0},{2,1},{3,2},{4,3},{5,4},{6,5},{7,6},{9,8},{10,9},{11,10},{12... | collective-permute-start | bytes 196616 | tf_op jit(solution)/shard_map/ppermute | solution.py:502
  53.9 2.5 %copy-start = (bf16[8,2,8,160,128]{4,3,2,1,0:T(8,128)(2,1)S(1)}, bf16[8,2,8,160,128]{4,3,2,1,0:T(8,128)(2,1)}, u32[]{:S(2)}) copy-start(bf16[8,2,8,160,128]{4,3,2,1,0:T(8,128)(2,1)} %get-tuple-element.50.q_ref) | copy-start | bytes 15728644
  56.3 11.2 %copy-start.1 = (bf16[8,2,8,160,128]{4,3,2,1,0:T(8,128)(2,1)S(1)}, bf16[8,2,8,160,128]{4,3,2,1,0:T(8,128)(2,1)}, u32[]{:S(2)}) copy-start(bf16[8,2,8,160,128]{4,3,2,1,0:T(8,128)(2,1)} %get-tuple-element.50.q_ref) | copy-start | bytes 15728644
  60.4 7.2 %collective-permute-start.7 = (bf16[2,5,32,256]{3,2,1,0:T(8,128)(2,1)S(1)}, bf16[2,5,32,256]{3,2,1,0:T(8,128)(2,1)S(1)}, u32[]{:S(2)}, u32[]{:S(2)}) collective-permute-start(bf16[2,5,32,256]{3,2,1,0:T(8,128)(2,1)S(1)} %pad_maximum_fusion.3), channel_id=1, source_target_pairs={{8,0},{9,1},{10,2},{11,3},{12,4},{13,5},{14,6},{15,7},{16,8},{17,9... | collective-permute-start | bytes 491528 | tf_op jit(solution)/shard_map/ppermute | solution.py:502
  67.6 5.0 %collective-permute-start.8 = (bf16[8,8,64,128]{3,2,1,0:T(8,128)(2,1)S(1)}, bf16[8,8,64,128]{3,2,1,0:T(8,128)(2,1)S(1)}, u32[]{:S(2)}, u32[]{:S(2)}) collective-permute-start(bf16[8,8,64,128]{3,2,1,0:T(8,128)(2,1)S(1)} %get-tuple-element.56), channel_id=1, source_target_pairs={{0,8},{8,0},{1,9},{9,1},{2,10},{10,2},{3,11},{11,3},{4,12},{12,4},... | collective-permute-start | bytes 3145736 | tf_op jit(solution)/shard_map/ppermute | solution.py:490
  70.8 1.7 %collective-permute-start.9 = (bf16[8,8,16,128]{3,2,1,0:T(8,128)(2,1)S(1)}, bf16[8,8,16,128]{3,2,1,0:T(8,128)(2,1)S(1)}, u32[]{:S(2)}, u32[]{:S(2)}) collective-permute-start(bf16[8,8,16,128]{3,2,1,0:T(8,128)(2,1)S(1)} %get-tuple-element.60), channel_id=1, source_target_pairs={{0,8},{8,0},{1,9},{9,1},{2,10},{10,2},{3,11},{11,3},{4,12},{12,4},... | collective-permute-start | bytes 786440 | tf_op jit(solution)/shard_map/ppermute | solution.py:490
  106.6 12.3 %all-to-all-start.2 = ((bf16[8,144,128]{2,1,0:T(8,128)(2,1)}), bf16[8,144,128]{2,1,0:T(8,128)(2,1)S(1)}, u32[]{:S(2)}, u32[]{:S(2)}) async-start(bf16[8,144,128]{2,1,0:T(8,128)(2,1)} %pad_maximum_fusion.1), calls=%async_computation.2 | async-start | bytes 589824 | tf_op jit(solution)/shard_map/all_to_all | solution.py:477
  128.2 6.0 %collective-permute-start.10 = (bf16[8,192,128]{2,1,0:T(8,128)(2,1)S(1)}, bf16[8,192,128]{2,1,0:T(8,128)(2,1)S(1)}, u32[]{:S(2)}, u32[]{:S(2)}) collective-permute-start(bf16[8,192,128]{2,1,0:T(8,128)(2,1)S(1)} %all_to_all.21), channel_id=1, source_target_pairs={{0,8},{8,0},{1,9},{9,1},{2,10},{10,2},{3,11},{11,3},{4,12},{12,4},... | collective-permute-start | bytes 1179656 | tf_op jit(solution)/shard_map/ppermute | solution.py:541

commit v6 on v5

--- a/solution.py
+++ b/solution.py
@@ -310,7 +310,7 @@
         ),
         scratch_shapes=[WEIGHT, pltpu.VMEM((5, 9, 32, 256), BF)],
         compiler_params=params(16),
-        cost_estimate=cost(1, 4),
+        cost_estimate=cost(10, 40),
         name="second_layer",
     )(core, h, hd, hr, hc, mine, other, sel, kernel, partial)
 

time: 137 us -> 135 us (0.985)
  local copies, waits for them, and re-layouts: 9.83 us -> 7.35 us
    unnamed x24 -> x22, local copies, waits for them, and re-layouts: 7.65 us -> 5.17 us
  transfers between devices with their start and end apart: 13 -> 13, of which waited for: 6 -> 7; matrix products, arithmetic and copies ran while one was open for 2% -> 2% of each run, Pallas kernels for 15% -> 15%
where the time goes in v6:
time: 135 us; the launch traced here: 134 us
  blocking collectives  40.9 us (30%)
  starting transfers between devices  37.1 us (27%)
  Pallas kernels  24.5 us (18%)
  waiting for transfers between devices  19.6 us (15%)
  local copies, waits for them, and re-layouts  7.35 us (5%)
  other arithmetic  3.48 us (3%)
    all_to_all x2, blocking collectives, exchange(): return lax.all_to_all(value, axes, 0, 0, tiled=True)  40.9 us
    ppermute x7, starting transfers between devices, shifted(): return lax.ppermute(value, SPACE + FILT, pairs)  20.8 us
    all_to_all x2, waiting for transfers between devices, exchange(): return lax.all_to_all(value, axes, 0, 0, tiled=True)  13.8 us
    pallas_call x1, Pallas kernels, first(): pl.pallas_call(first_kernel, in_specs=[anywhere] + vmem(4), out_specs=vme...  11.1 us
    all_to_all x2, starting transfers between devices, exchange(): return lax.all_to_all(value, axes, 0, 0, tiled=True)  10.7 us
    unnamed x22, local copies, waits for them, and re-layouts  5.17 us
    ppermute x1, starting transfers between devices, body(): other = lax.ppermute(mine, 'core', [(0, 1), (1, 0)])  4.62 us
    ppermute x7, waiting for transfers between devices, shifted(): return lax.ppermute(value, SPACE + FILT, pairs)  4.27 us
  transfers between devices with their start and end apart: 13, of which 7 were waited for; matrix products, arithmetic and copies ran while one was open for 2% of the time, Pallas kernels for 15%

profile of v6, /device:TPU:1, one launch (start us, length us, event | category | flops | bytes accessed | tf_op | source)
XLA Modules:
  0.0 133.9 jit_solution(2572518052574548864)
XLA Ops:
  0.6 0.0 copy-start.1
  0.6 2.2 %copy-done.1 = bf16[2,64,8,16,128]{4,3,2,1,0:T(8,128)(2,1)S(1)} copy-done((bf16[2,64,8,16,128]{4,3,2,1,0:T(8,128)(2,1)S(1)}, bf16[2,64,8,16,128]{4,3,2,1,0:T(8,128)(2,1)}, u32[]{:S(2)}) %copy-start.1) | copy-done | bytes 4194328
  2.8 0.9 input_rims.1
  3.7 4.9 %collective-permute-start = (bf16[16,128,128]{2,1,0:T(8,128)(2,1)S(1)}, bf16[16,128,128]{2,1,0:T(8,128)(2,1)S(1)}, u32[]{:S(2)}, u32[]{:S(2)}) collective-permute-start(bf16[16,128,128]{2,1,0:T(8,128)(2,1)S(1)} %get-tuple-element.32), channel_id=1, source_target_pairs={{0,8},{1,9},{2,10},{3,11},{4,12},{5,13},{6,14},{7,15},{8,16},{9,17... | collective-permute-start | bytes 1572872 | tf_op jit(solution)/shard_map/ppermute | solution.py:502
  8.7 3.1 %collective-permute-start.1 = (bf16[8,128,128]{2,1,0:T(8,128)(2,1)S(1)}, bf16[8,128,128]{2,1,0:T(8,128)(2,1)S(1)}, u32[]{:S(2)}, u32[]{:S(2)}) collective-permute-start(bf16[8,128,128]{2,1,0:T(8,128)(2,1)S(1)} %get-tuple-element.33), channel_id=1, source_target_pairs={{0,1},{1,2},{2,3},{3,4},{4,5},{5,6},{6,7},{8,9},{9,10},{10,11},{11... | collective-permute-start | bytes 786440 | tf_op jit(solution)/shard_map/ppermute | solution.py:502
  11.8 0.0 copy-done.8
  11.8 0.2 reshape.56
  12.0 0.1 copy.13
  12.1 0.0 copy-done.4
  12.1 1.1 weights_and_cotangent.1
  13.2 6.3 %all-to-all-start = ((bf16[8,560,128]{2,1,0:T(8,128)(2,1)}), bf16[8,560,128]{2,1,0:T(8,128)(2,1)S(1)}, u32[]{:S(2)}, u32[]{:S(2)}) async-start(bf16[8,560,128]{2,1,0:T(8,128)(2,1)} %weights_and_cotangent.1), calls=%async_computation | async-start | bytes 2293760 | tf_op jit(solution)/shard_map/all_to_all | solution.py:477
  19.5 0.0 collective-permute-done.1.xr_ref
  19.5 0.0 copy-start.10
  19.5 0.0 collective-permute-done.xd_ref
  19.6 0.0 copy-start.9
  19.6 0.7 copy-done.10
  20.2 0.2 copy-done.9
  20.5 11.1 %first_layer.1 = (bf16[4,8,64,256]{3,2,1,0:T(8,128)(2,1)}, bf16[8,2,8,160,128]{4,3,2,1,0:T(8,128)(2,1)}, bf16[17,160,128]{2,1,0:T(8,128)(2,1)}, bf16[8,160,128]{...) custom-call(bf16[2,64,8,16,128]{4,3,2,1,0:T(8,128)(2,1)} %x_ref.3, ...), custom_call_target="tpu_custom_call" | custom-call | flops 64424509440 | bytes 209715200 | tf_op jit(solution)/shard_map/first_layer/pallas_call | solution.py:171
  31.6 5.8 %all-to-all-done.m_ref = bf16[8,560,128]{2,1,0:T(8,128)(2,1)S(1)} async-done(((bf16[8,560,128]{2,1,0:T(8,128)(2,1)}), bf16[8,560,128]{2,1,0:T(8,128)(2,1)S(1)}, u32[]{:S(2)}, u32[]{:S(2)}) %all-to-all-start) | async-done | bytes 1146912 | tf_op jit(solution)/shard_map/all_to_all | solution.py:477
  37.4 0.3 collective-permute-start.5
  37.8 3.7 %collective-permute-start.2 = (bf16[9,64,256]{2,1,0:T(8,128)(2,1)}, bf16[9,64,256]{2,1,0:T(8,128)(2,1)S(1)}, u32[]{:S(2)}, u32[]{:S(2)}) collective-permute-start(bf16[9,64,256]{2,1,0:T(8,128)(2,1)} %get-tuple-element.35), channel_id=1, source_target_pairs={{0,8},{1,9},{2,10},{3,11},{4,12},{5,13},{6,14},{7,15},{8,16},{9,17... | collective-permute-start | bytes 884744 | tf_op jit(solution)/shard_map/ppermute | solution.py:502
  41.5 2.5 %collective-permute-start.3 = (bf16[4,64,256]{2,1,0:T(8,128)(2,1)}, bf16[4,64,256]{2,1,0:T(8,128)(2,1)S(1)}, u32[]{:S(2)}, u32[]{:S(2)}) collective-permute-start(bf16[4,64,256]{2,1,0:T(8,128)(2,1)} %get-tuple-element.36), channel_id=1, source_target_pairs={{0,1},{1,2},{2,3},{3,4},{4,5},{5,6},{6,7},{8,9},{9,10},{10,11},{11... | collective-permute-start | bytes 393224 | tf_op jit(solution)/shard_map/ppermute | solution.py:502
  44.0 2.2 %collective-permute-start.4 = (bf16[64,256]{1,0:T(8,128)(2,1)}, bf16[64,256]{1,0:T(8,128)(2,1)S(1)}, u32[]{:S(2)}, u32[]{:S(2)}) collective-permute-start(bf16[64,256]{1,0:T(8,128)(2,1)} %get-tuple-element.39), channel_id=1, source_target_pairs={{0,9},{1,10},{2,11},{3,12},{4,13},{5,14},{6,15},{8,17},{9,18},{10,... | collective-permute-start | bytes 98312 | tf_op jit(solution)/shard_map/ppermute | solution.py:502
  46.2 0.8 slice.40.k_ref
  47.0 0.0 collective-permute-done.3.hr_ref
  47.0 0.0 collective-permute-done.2.hd_ref
  47.0 0.5 collective-permute-done.4.hc_ref
  47.5 0.0 collective-permute-done.5.o_ref
  47.5 0.0 copy-done.5
  47.5 1.2 copy-done.6
  48.8 0.8 copy-done.7
  49.6 2.9 %second_layer.1 = (bf16[8,128,128]{2,1,0:T(8,128)(2,1)S(1)}, bf16[2,2,4,32,256]{4,3,2,1,0:T(8,128)(2,1)S(1)}, bf16[256,512]{1,0:T(8,128)(2,1)S(1)}, bf16[2,4,32,...) custom-call(s32[1]{0:T(128)} %bitcast.core_ref, ...), custom_call_target="tpu_custom_call" | custom-call | flops 10737418240 | bytes 41943040 | tf_op jit(solution)/shard_map/second_layer/pallas_call | solution.py:298
  52.5 1.3 collective-permute-start.6
  53.8 0.0 copy-done
  53.9 0.0 copy-done.2
  53.9 0.0 copy-done.3
  53.9 4.0 %first_kernel_grad_inner.1.sum_ref = f32[14,128,128]{2,1,0:T(8,128)S(1)} custom-call(s32[1]{0:T(128)} %bitcast.core_ref, bf16[2,2,4,32,256]{4,3,2,1,0:T(8,128)(2,1)S(1)} %get-tuple-element.49.d_ref, bf16[8,560,128]{2,1,0:T(8,128)(2,1)S(1)} %all-to-all-done.m_ref, bf16[8,560,128]{2,1,0:T(8,128)(2,1)S(1)} %collective-permute-done.5.o_ref, ...), custom_call_target="tpu_custom_call" | custom-call | flops 4294967296 | bytes 9437184 | tf_op jit(solution)/shard_map/first_kernel_grad_inner/pallas_call | solution.py:422
  57.9 0.6 collective-permute-done.6.dr_ref
  58.6 3.0 %collective-permute-start.7 = (bf16[2,5,32,256]{3,2,1,0:T(8,128)(2,1)S(1)}, bf16[2,5,32,256]{3,2,1,0:T(8,128)(2,1)S(1)}, u32[]{:S(2)}, u32[]{:S(2)}) collective-permute-start(bf16[2,5,32,256]{3,2,1,0:T(8,128)(2,1)S(1)} %pad_maximum_fusion.3), channel_id=1, source_target_pairs={{8,0},{9,1},{10,2},{11,3},{12,4},{13,5},{14,6},{15,7},{16,8},{17,9... | collective-permute-start | bytes 491528 | tf_op jit(solution)/shard_map/ppermute | solution.py:502
  61.6 1.2 second_kernel_grad.1
  62.8 3.1 %collective-permute-done.7.dd_ref = bf16[2,5,32,256]{3,2,1,0:T(8,128)(2,1)S(1)} collective-permute-done((bf16[2,5,32,256]{3,2,1,0:T(8,128)(2,1)S(1)}, bf16[2,5,32,256]{3,2,1,0:T(8,128)(2,1)S(1)}, u32[]{:S(2)}, u32[]{:S(2)}) %collective-permute-start.7) | collective-permute-done | bytes 163872 | tf_op jit(solution)/shard_map/ppermute | solution.py:502
  66.0 0.0 collective-permute-start.8
  66.0 3.2 %first_kernel_grad.1 = (bf16[8,8,16,128]{3,2,1,0:T(8,128)(2,1)S(1)}, bf16[8,8,16,128]{3,2,1,0:T(8,128)(2,1)S(1)}) custom-call(s32[1]{0:T(128)} %bitcast.core_ref, bf16[2,2,4,32,256]{4,3,2,1,0:T(8,128)(2,1)S(1)} %get-tuple-element.49.d_ref, bf16[2,5,32,256]{3,2,1,0:T(8,128)(2,1)S(1)} %collective-permute-done.7.dd_ref, ...), custom_call_target="tpu_custom_call" | custom-call | flops 2147483648 | bytes 9437184 | tf_op jit(solution)/shard_map/first_kernel_grad/pallas_call | solution.py:458
  69.2 0.6 collective-permute-start.9
  69.8 1.2 collective-permute-done.9
  70.9 0.1 add_convert_fusion.1
  71.0 0.0 collective-permute-done.8
  71.0 0.4 add_convert_fusion
  71.4 0.1 pad_maximum_fusion
  71.5 31.7 %all_to_all.20 = bf16[64,80,128]{2,1,0:T(8,128)(2,1)S(1)} all-to-all(bf16[64,80,128]{2,1,0:T(8,128)(2,1)S(1)} %bitcast.37), channel_id=1, replica_groups=mesh['y_lo'=2,'z'=4,'core'=2,'y_hi'=2,'x'=4] {'y_lo','z','y_hi','x'}, dimensions={0} | all-to-all | bytes 2621440 | tf_op jit(solution)/shard_map/all_to_all | solution.py:477
  103.2 0.2 reduce_sum.12
  103.4 0.7 pad_maximum_fusion.1
  104.2 4.4 %all-to-all-start.2 = ((bf16[8,144,128]{2,1,0:T(8,128)(2,1)}), bf16[8,144,128]{2,1,0:T(8,128)(2,1)S(1)}, u32[]{:S(2)}, u32[]{:S(2)}) async-start(bf16[8,144,128]{2,1,0:T(8,128)(2,1)} %pad_maximum_fusion.1), calls=%async_computation.2 | async-start | bytes 589824 | tf_op jit(solution)/shard_map/all_to_all | solution.py:477
  108.5 8.0 %all-to-all-done.2 = bf16[8,144,128]{2,1,0:T(8,128)(2,1)S(1)} async-done(((bf16[8,144,128]{2,1,0:T(8,128)(2,1)}), bf16[8,144,128]{2,1,0:T(8,128)(2,1)S(1)}, u32[]{:S(2)}, u32[]{:S(2)}) %all-to-all-start.2) | async-done | bytes 294944 | tf_op jit(solution)/shard_map/all_to_all | solution.py:477
  116.5 0.1 broadcast_in_dim.5
  116.6 9.2 %all_to_all.21 = bf16[8,192,128]{2,1,0:T(8,128)(2,1)S(1)} all-to-all(bf16[8,192,128]{2,1,0:T(8,128)(2,1)S(1)} %broadcast_in_dim.5), channel_id=1, replica_groups=mesh['y_lo'=2,'z'=4,'core'=2,'y_hi'=2,'x'=4] {'y_lo','z'}, dimensions={0} | all-to-all | bytes 786432 | tf_op jit(solution)/shard_map/all_to_all | solution.py:477
  125.8 4.6 %collective-permute-start.10 = (bf16[8,192,128]{2,1,0:T(8,128)(2,1)S(1)}, bf16[8,192,128]{2,1,0:T(8,128)(2,1)S(1)}, u32[]{:S(2)}, u32[]{:S(2)}) collective-permute-start(bf16[8,192,128]{2,1,0:T(8,128)(2,1)S(1)} %all_to_all.21), channel_id=1, source_target_pairs={{0,8},{8,0},{1,9},{9,1},{2,10},{10,2},{3,11},{11,3},{4,12},{12,4},... | collective-permute-start | bytes 1179656 | tf_op jit(solution)/shard_map/ppermute | solution.py:541
  130.4 0.2 copy.14
  130.6 0.8 reshape.60
  131.4 0.4 collective-permute-done.10
  131.8 0.1 select_bitcast_fusion
  131.8 0.1 fusion
  132.0 1.0 convert.4
  133.1 0.8 convert_bitcast_fusion
  (21 shorter events, 0.2 us)
Async XLA Ops:
  0.6 2.2 %copy-start.1 = (bf16[2,64,8,16,128]{4,3,2,1,0:T(8,128)(2,1)S(1)}, bf16[2,64,8,16,128]{4,3,2,1,0:T(8,128)(2,1)}, u32[]{:S(2)}) copy-start(bf16[2,64,8,16,128]{4,3,2,1,0:T(8,128)(2,1)} %x_ref.3) | copy-start | bytes 12582916
  2.8 9.0 %copy-start.8 = (bf16[2,32,2,1024]{3,2,1,0:T(2,128)(2,1)S(1)}, bf16[2,32,2,1024]{3,2,1,0:T(2,128)(2,1)}, u32[]{:S(2)}) copy-start(bf16[2,32,2,1024]{3,2,1,0:T(2,128)(2,1)} %param.8) | copy-start | bytes 786436
  2.8 9.2 %copy-start.4 = (bf16[3,3,3,128,32]{3,4,2,1,0:T(8,128)(2,1)S(1)}, bf16[3,3,3,128,32]{3,4,2,1,0:T(8,128)(2,1)}, u32[]{:S(2)}) copy-start(bf16[3,3,3,128,32]{3,4,2,1,0:T(8,128)(2,1)} %param.7) | copy-start | bytes 663556
  3.7 15.8 %collective-permute-start = (bf16[16,128,128]{2,1,0:T(8,128)(2,1)S(1)}, bf16[16,128,128]{2,1,0:T(8,128)(2,1)S(1)}, u32[]{:S(2)}, u32[]{:S(2)}) collective-permute-start(bf16[16,128,128]{2,1,0:T(8,128)(2,1)S(1)} %get-tuple-element.32), channel_id=1, source_target_pairs={{0,8},{1,9},{2,10},{3,11},{4,12},{5,13},{6,14},{7,15},{8,16},{9,17... | collective-permute-start | bytes 1572872 | tf_op jit(solution)/shard_map/ppermute | solution.py:502
  8.7 10.9 %collective-permute-start.1 = (bf16[8,128,128]{2,1,0:T(8,128)(2,1)S(1)}, bf16[8,128,128]{2,1,0:T(8,128)(2,1)S(1)}, u32[]{:S(2)}, u32[]{:S(2)}) collective-permute-start(bf16[8,128,128]{2,1,0:T(8,128)(2,1)S(1)} %get-tuple-element.33), channel_id=1, source_target_pairs={{0,1},{1,2},{2,3},{3,4},{4,5},{5,6},{6,7},{8,9},{9,10},{10,11},{11... | collective-permute-start | bytes 786440 | tf_op jit(solution)/shard_map/ppermute | solution.py:502
  13.2 24.2 %all-to-all-start = ((bf16[8,560,128]{2,1,0:T(8,128)(2,1)}), bf16[8,560,128]{2,1,0:T(8,128)(2,1)S(1)}, u32[]{:S(2)}, u32[]{:S(2)}) async-start(bf16[8,560,128]{2,1,0:T(8,128)(2,1)} %weights_and_cotangent.1), calls=%async_computation | async-start | bytes 2293760 | tf_op jit(solution)/shard_map/all_to_all | solution.py:477
  19.5 0.7 copy-start.10
  19.6 0.9 copy-start.9
  20.5 27.1 %copy-start.5 = (bf16[160,128]{1,0:T(8,128)(2,1)S(1)}, bf16[160,128]{1,0:T(8,128)(2,1)}, u32[]{:S(2)}) copy-start(bf16[160,128]{1,0:T(8,128)(2,1)} %constant.13.clone.sel_ref) | copy-start | bytes 122884
  37.4 10.1 %collective-permute-start.5 = (bf16[8,560,128]{2,1,0:T(8,128)(2,1)S(1)}, bf16[8,560,128]{2,1,0:T(8,128)(2,1)S(1)}, u32[]{:S(2)}, u32[]{:S(2)}) collective-permute-start(bf16[8,560,128]{2,1,0:T(8,128)(2,1)S(1)} %all-to-all-done.m_ref), channel_id=1, source_target_pairs={{0,8},{8,0},{1,9},{9,1},{2,10},{10,2},{3,11},{11,3},{4,12},{12,4},... | collective-permute-start | bytes 3440648 | tf_op jit(solution)/shard_map/ppermute | solution.py:520
  37.8 9.3 %collective-permute-start.2 = (bf16[9,64,256]{2,1,0:T(8,128)(2,1)}, bf16[9,64,256]{2,1,0:T(8,128)(2,1)S(1)}, u32[]{:S(2)}, u32[]{:S(2)}) collective-permute-start(bf16[9,64,256]{2,1,0:T(8,128)(2,1)} %get-tuple-element.35), channel_id=1, source_target_pairs={{0,8},{1,9},{2,10},{3,11},{4,12},{5,13},{6,14},{7,15},{8,16},{9,17... | collective-permute-start | bytes 884744 | tf_op jit(solution)/shard_map/ppermute | solution.py:502
  41.5 5.5 %collective-permute-start.3 = (bf16[4,64,256]{2,1,0:T(8,128)(2,1)}, bf16[4,64,256]{2,1,0:T(8,128)(2,1)S(1)}, u32[]{:S(2)}, u32[]{:S(2)}) collective-permute-start(bf16[4,64,256]{2,1,0:T(8,128)(2,1)} %get-tuple-element.36), channel_id=1, source_target_pairs={{0,1},{1,2},{2,3},{3,4},{4,5},{5,6},{6,7},{8,9},{9,10},{10,11},{11... | collective-permute-start | bytes 393224 | tf_op jit(solution)/shard_map/ppermute | solution.py:502
  44.0 3.6 %collective-permute-start.4 = (bf16[64,256]{1,0:T(8,128)(2,1)}, bf16[64,256]{1,0:T(8,128)(2,1)S(1)}, u32[]{:S(2)}, u32[]{:S(2)}) collective-permute-start(bf16[64,256]{1,0:T(8,128)(2,1)} %get-tuple-element.39), channel_id=1, source_target_pairs={{0,9},{1,10},{2,11},{3,12},{4,13},{5,14},{6,15},{8,17},{9,18},{10,... | collective-permute-start | bytes 98312 | tf_op jit(solution)/shard_map/ppermute | solution.py:502
  47.5 1.2 copy-start.6
  48.8 0.8 copy-start.7
  49.6 4.2 %copy-start = (bf16[8,2,8,160,128]{4,3,2,1,0:T(8,128)(2,1)S(1)}, bf16[8,2,8,160,128]{4,3,2,1,0:T(8,128)(2,1)}, u32[]{:S(2)}) copy-start(bf16[8,2,8,160,128]{4,3,2,1,0:T(8,128)(2,1)} %get-tuple-element.50.q_ref) | copy-start | bytes 15728644
  49.6 4.2 %copy-start.2 = (bf16[17,160,128]{2,1,0:T(8,128)(2,1)S(1)}, bf16[17,160,128]{2,1,0:T(8,128)(2,1)}, u32[]{:S(2)}) copy-start(bf16[17,160,128]{2,1,0:T(8,128)(2,1)} %get-tuple-element.51.qd_ref) | copy-start | bytes 2088964
  49.6 4.3 %copy-start.3 = (bf16[8,160,128]{2,1,0:T(8,128)(2,1)S(1)}, bf16[8,160,128]{2,1,0:T(8,128)(2,1)}, u32[]{:S(2)}) copy-start(bf16[8,160,128]{2,1,0:T(8,128)(2,1)} %get-tuple-element.52.qr_ref) | copy-start | bytes 983044
  52.5 6.0 %collective-permute-start.6 = (bf16[2,2,32,256]{3,2,1,0:T(8,128)(2,1)S(1)}, bf16[2,2,32,256]{3,2,1,0:T(8,128)(2,1)S(1)}, u32[]{:S(2)}, u32[]{:S(2)}) collective-permute-start(bf16[2,2,32,256]{3,2,1,0:T(8,128)(2,1)S(1)} %get-tuple-element.48), channel_id=1, source_target_pairs={{1,0},{2,1},{3,2},{4,3},{5,4},{6,5},{7,6},{9,8},{10,9},{11,10},{12... | collective-permute-start | bytes 196616 | tf_op jit(solution)/shard_map/ppermute | solution.py:502
  58.6 7.4 %collective-permute-start.7 = (bf16[2,5,32,256]{3,2,1,0:T(8,128)(2,1)S(1)}, bf16[2,5,32,256]{3,2,1,0:T(8,128)(2,1)S(1)}, u32[]{:S(2)}, u32[]{:S(2)}) collective-permute-start(bf16[2,5,32,256]{3,2,1,0:T(8,128)(2,1)S(1)} %pad_maximum_fusion.3), channel_id=1, source_target_pairs={{8,0},{9,1},{10,2},{11,3},{12,4},{13,5},{14,6},{15,7},{16,8},{17,9... | collective-permute-start | bytes 491528 | tf_op jit(solution)/shard_map/ppermute | solution.py:502
  66.0 5.0 %collective-permute-start.8 = (bf16[8,8,64,128]{3,2,1,0:T(8,128)(2,1)S(1)}, bf16[8,8,64,128]{3,2,1,0:T(8,128)(2,1)S(1)}, u32[]{:S(2)}, u32[]{:S(2)}) collective-permute-start(bf16[8,8,64,128]{3,2,1,0:T(8,128)(2,1)S(1)} %get-tuple-element.56), channel_id=1, source_target_pairs={{0,8},{8,0},{1,9},{9,1},{2,10},{10,2},{3,11},{11,3},{4,12},{12,4},... | collective-permute-start | bytes 3145736 | tf_op jit(solution)/shard_map/ppermute | solution.py:490
  69.2 1.7 %collective-permute-start.9 = (bf16[8,8,16,128]{3,2,1,0:T(8,128)(2,1)S(1)}, bf16[8,8,16,128]{3,2,1,0:T(8,128)(2,1)S(1)}, u32[]{:S(2)}, u32[]{:S(2)}) collective-permute-start(bf16[8,8,16,128]{3,2,1,0:T(8,128)(2,1)S(1)} %get-tuple-element.60), channel_id=1, source_target_pairs={{0,8},{8,0},{1,9},{9,1},{2,10},{10,2},{3,11},{11,3},{4,12},{12,4},... | collective-permute-start | bytes 786440 | tf_op jit(solution)/shard_map/ppermute | solution.py:490
  104.2 12.3 %all-to-all-start.2 = ((bf16[8,144,128]{2,1,0:T(8,128)(2,1)}), bf16[8,144,128]{2,1,0:T(8,128)(2,1)S(1)}, u32[]{:S(2)}, u32[]{:S(2)}) async-start(bf16[8,144,128]{2,1,0:T(8,128)(2,1)} %pad_maximum_fusion.1), calls=%async_computation.2 | async-start | bytes 589824 | tf_op jit(solution)/shard_map/all_to_all | solution.py:477
  125.8 6.0 %collective-permute-start.10 = (bf16[8,192,128]{2,1,0:T(8,128)(2,1)S(1)}, bf16[8,192,128]{2,1,0:T(8,128)(2,1)S(1)}, u32[]{:S(2)}, u32[]{:S(2)}) collective-permute-start(bf16[8,192,128]{2,1,0:T(8,128)(2,1)S(1)} %all_to_all.21), channel_id=1, source_target_pairs={{0,8},{8,0},{1,9},{9,1},{2,10},{10,2},{3,11},{11,3},{4,12},{12,4},... | collective-permute-start | bytes 1179656 | tf_op jit(solution)/shard_map/ppermute | solution.py:541
